TPU v7x, 128 devices: a whole 4x4x4 slice. The times are simulated.
128 devices in a mesh: cols: 16 (over x_hi, y, core), rows: 8 (over z, x_lo).
Axes of the slice: x: 4 (x_hi: 2, x_lo: 2; x = x_hi * 2 + x_lo), y: 4, z: 4, core: 2. Of those that a mesh axis runs over, the one named last changes fastest.
Arguments:
- weight: float32 [8192, 28672], P('rows', 'cols'), may hold values from -6 to 6
- scales: float32 [8192], P('rows'), may hold values from 0.2 to 0.5
- panels: float32 [2048, 28672], P('cols', 'rows')
- block_inverse: float32 [2, 128, 128], replicated
- grid_codes: int32 [16], replicated, may hold values from -12 to 12, as said below
- block_starts: int32 [2], replicated, may hold values from 0 to 26880, as said below
Outputs:
- result: float32 [8192, 28672], P('rows', 'cols')
Inputs may be any that keep to these rules, and one draw needn't show every extreme that they name: `grid_codes`: strictly increasing. `block_starts`: strictly increasing multiples of 1792; the last block starts at the last device's columns.
All inputs are finite; a program needn't handle non-finite values.
Results may differ from a plain program's by a relative error of at most 0.00012.
Values sent between devices are 32-bit elements; how exact they have to be, the bound alone decides.
No kernel may reach another device: no remote copies, remote signals or barrier semaphores. Data moves between devices by JAX's collectives and lax.ppermute only.
A program may use at most 128 MiB of HBM per device.

v0:
```python
import jax
import jax.numpy as jnp
from jax import lax
from jax.sharding import Mesh
from jax.sharding import PartitionSpec as P

BLK = 128
SUB = 32
LEVELS = 16
BLOCKS = 2
ROWS = ("rows_0", "rows_1")


softness = 0.2


def from_root(value, axis, source):
    kept = jnp.where(lax.axis_index(axis) == source, value, 0).astype(value.dtype)
    return lax.psum(kept, axis)


def spread(shard, axes, root):
    shard = jnp.where(lax.axis_index(axes) == root, shard, jnp.zeros_like(shard))
    for axis in axes:
        shard = lax.psum(shard, axis)
    return shard


def broadcast(shard, axis, root):
    return lax.dynamic_index_in_dim(lax.all_gather(shard, axis), root, 0, keepdims=False)


def quantize(values, scales, grid_codes):
    levels = grid_codes.astype(jnp.float32)
    ratio = values / scales[:, None]
    output = jnp.zeros_like(values) + levels[0]
    for level_id in range(LEVELS - 1):
        level_gap = levels[level_id + 1] - levels[level_id]
        midpoint = 0.5 * (levels[level_id] + levels[level_id + 1])
        output = output + level_gap * jax.nn.sigmoid((ratio - midpoint) / softness)
    return output * scales[:, None]


def inner_block(block_cols, diag_block, inverse, scales, grid_codes):
    local_ids = jnp.arange(BLK, dtype=jnp.int32)
    pieces = []
    for piece_id in range(BLK // SUB):
        low_col = piece_id * SUB
        current = block_cols[:, low_col : low_col + SUB]
        quantized = quantize(current, scales, grid_codes)
        error_part = jnp.dot(
            current - quantized,
            inverse[low_col : low_col + SUB, low_col : low_col + SUB],
            precision=lax.Precision.HIGHEST,
            preferred_element_type=jnp.float32,
        )
        later_rows = jnp.where(
            local_ids[None, :] >= low_col + SUB, diag_block[low_col : low_col + SUB, :], 0.0
        )
        block_cols = block_cols - jnp.dot(
            error_part,
            later_rows,
            precision=lax.Precision.HIGHEST,
            preferred_element_type=jnp.float32,
        )
        block_cols = block_cols.at[:, low_col : low_col + SUB].set(quantized)
        pieces.append(error_part)
    return (block_cols, jnp.concatenate(pieces, axis=1))


def local(weight, scales, panels, block_inverse, grid_codes, block_starts):
    cols_per = weight.shape[1]
    slab_width = panels.shape[1]
    own_index = lax.axis_index("cols")
    first_col = own_index * cols_per
    column_ids = first_col + jnp.arange(cols_per, dtype=jnp.int32)
    holder = first_col // slab_width
    offset = first_col - holder * slab_width
    for block_id in range(BLOCKS):
        start_col = block_starts[block_id]
        owner_id = start_col // cols_per
        panel_slab = from_root(panels, "cols", owner_id)
        needed = lax.dynamic_slice_in_dim(panel_slab, offset, cols_per, 1)
        panel_local = spread(needed, ROWS, holder)
        trail_rows = jnp.where(column_ids[None, :] >= start_col + BLK, panel_local, 0.0)
        diag_block, trail_rows = (panel_local[:, :BLK], trail_rows)
        block_cols, errors = inner_block(
            weight[:, :BLK], diag_block, block_inverse[block_id], scales, grid_codes
        )
        errors = broadcast(errors, "cols", owner_id)
        block_cols, errors = (block_cols, errors)
        weight = jnp.where(own_index == owner_id, weight.at[:, :BLK].set(block_cols), weight)
        weight = weight - jnp.dot(
            errors, trail_rows, precision=lax.Precision.HIGHEST, preferred_element_type=jnp.float32
        )
    return weight


def solution(mesh):
    torus = Mesh(mesh.devices.reshape(mesh.shape["cols"], 4, 2), ("cols", "rows_0", "rows_1"))
    return jax.shard_map(
        local,
        mesh=torus,
        in_specs=(P(ROWS, "cols"), P(ROWS), P("cols", ROWS), P(), P(), P()),
        out_specs=P(ROWS, "cols"),
        check_vma=False,
    )
```

profile of v0, /device:TPU:1, one launch (start us, length us, event | category | flops | bytes accessed | tf_op | source)
XLA Modules:
  0.0 519.6 jit_solution(15605433078648100774)
XLA Ops:
  6.5 1.4 fusion.78
  11.9 3.8 broadcast_select_fusion
  15.8 151.7 %all-reduce.7.cloned.1.call-done = (f32[128,3584]{1,0:T(8,128)}, f32[128,3584]{1,0:T(8,128)}) async-done(((f32[128,3584]{1,0:T(8,128)}, f32[128,3584]{1,0:T(8,128)}), (f32[128,3584]{1,0:T(8,128)}, f32[128,3584]{1,0:T(8,128)})) %all-reduce.7.cloned.1.call-update) | async-done | bytes 3670032 | tf_op jit(solution)/shard_map/psum | solution.py:19
  167.5 2.8 dynamic-slice_select_fusion
  170.4 56.4 %all-reduce.9.cloned.1.call-done = (f32[128,1792]{1,0:T(8,128)}, f32[128,1792]{1,0:T(8,128)}) async-done(((f32[128,1792]{1,0:T(8,128)}, f32[128,1792]{1,0:T(8,128)}), (f32[128,1792]{1,0:T(8,128)}, f32[128,1792]{1,0:T(8,128)})) %all-reduce.9.cloned.1.call-update) | async-done | bytes 1835024 | tf_op jit(solution)/shard_map/psum | solution.py:25
  226.9 0.7 fusion.79
  265.0 8.6 %copy.9 = f32[1024,1792]{0,1:T(8,128)} copy(f32[1024,1792]{1,0:T(8,128)} %param.26) | data formatting | bytes 14680064 | tf_op args[0]
  273.6 0.7 compare_reduce_fusion.2
  274.3 0.7 compare_reduce_fusion
  275.0 2.5 fusion.32
  277.5 15.5 %all-reduce.11.cloned.1.call-done = (f32[128,1792]{1,0:T(8,128)}, f32[128,1792]{1,0:T(8,128)}) async-done(((f32[128,1792]{1,0:T(8,128)}, f32[128,1792]{1,0:T(8,128)}), (f32[128,1792]{1,0:T(8,128)}, f32[128,1792]{1,0:T(8,128)})) %all-reduce.11.cloned.1.call-update) | async-done | bytes 1835024 | tf_op jit(solution)/shard_map/psum | solution.py:25
  292.9 1.8 convolution_subtract_fusion.9
  294.7 2.8 fusion.17
  297.5 1.5 fusion.30
  299.0 0.6 convolution_subtract_fusion.8
  299.7 1.9 fusion.16
  301.5 1.5 fusion.28
  303.1 0.6 convolution_subtract_fusion.7
  303.7 1.9 fusion.15
  305.6 1.5 fusion.26
  307.1 0.8 pad_maximum_fusion
  308.7 0.9 compare_reduce_fusion.3
  309.5 0.6 convolution_subtract_fusion.6
  310.2 1.3 constant_dynamic-update-slice_fusion.1
  311.4 2.5 fusion.2
  314.0 68.4 %all-gather.5.cloned.1.call-done = f32[16384,128]{0,1:T(8,128)} async-done(((f32[1024,128]{0,1:T(8,128)}), f32[16384,128]{0,1:T(8,128)}) %all-gather.5.cloned.1.call-update) | async-done | bytes 8388624 | tf_op jit(solution)/shard_map/all_gather | solution.py:30
  382.4 10.1 %copy.19 = f32[16,8,16,1024]{3,2,1,0:T(8,128)S(1)} copy(f32[16,8,16,1024]{3,1,2,0:T(8,128)} %bitcast.55) | data formatting | bytes 16777216
  392.4 0.5 constant_dynamic-slice_fusion.1
  393.0 6.4 %convolution_subtract_fusion.1 = f32[1024,1792]{0,1:T(8,128)S(1)} fusion(f32[1024,1792]{0,1:T(8,128)S(1)} %bitcast.51, f32[128,1792]{1,0:T(8,128)S(1)} %copy-done.2, f32[1,1024,128]{1,0,2:T(1,128)S(1)} %constant_dynamic-slice_fusion.1, pred[1792]{0:T(1024)(128)(4,1)S(1)} %fusion.51), kind=kOutput, calls=%fused_computation.1 | convolution fusion | flops 2820636672 | bytes 16123648 | tf_op jit(solution)/shard_map/dot_general | solution.py:93
  399.4 1.6 fusion.24
  401.3 0.6 convolution_subtract_fusion.5
  401.9 1.9 fusion.14
  403.8 1.5 fusion.22
  405.3 0.6 convolution_subtract_fusion.4
  406.0 1.9 fusion.13
  407.9 1.5 fusion.20
  409.4 0.6 convolution_subtract_fusion.3
  410.0 1.9 fusion.12
  411.9 1.5 fusion.18
  413.4 0.9 pad_maximum_fusion.1
  415.0 0.6 convolution_subtract_fusion.2
  415.6 1.3 constant_dynamic-update-slice_fusion
  416.9 2.5 fusion.3
  419.4 65.7 %all-gather.7.cloned.1.call-done = f32[16384,128]{0,1:T(8,128)} async-done(((f32[1024,128]{0,1:T(8,128)}), f32[16384,128]{0,1:T(8,128)}) %all-gather.7.cloned.1.call-update) | async-done | bytes 8388624 | tf_op jit(solution)/shard_map/all_gather | solution.py:30
  485.2 10.3 %copy.20 = f32[16,8,16,1024]{3,2,1,0:T(8,128)S(1)} copy(f32[16,8,16,1024]{3,1,2,0:T(8,128)} %bitcast.54) | data formatting | bytes 16777216
  495.5 0.5 constant_dynamic-slice_fusion
  496.1 8.2 %convolution_subtract_fusion = f32[1024,1792]{0,1:T(8,128)} fusion(f32[1024,1792]{0,1:T(8,128)S(1)} %bitcast.49, f32[128,1792]{1,0:T(8,128)S(1)} %copy-done.1, f32[1,1024,128]{1,0,2:T(1,128)S(1)} %constant_dynamic-slice_fusion, pred[1792]{0:T(1024)(128)(4,1)S(1)} %fusion.50), kind=kOutput, calls=%fused_computation | convolution fusion | flops 2820636672 | bytes 16123648 | tf_op jit(solution)/shard_map/dot_general | solution.py:93
  504.3 8.4 %copy.13 = f32[1024,1792]{1,0:T(8,128)} copy(f32[1024,1792]{0,1:T(8,128)} %convolution_subtract_fusion) | data formatting | bytes 14680064 | tf_op jit(solution)/shard_map/sub | solution.py:93
  (40 shorter events, 0.6 us)
Async XLA Ops:
  6.5 161.0 %all-reduce.7.cloned.1.call-start = ((), (), s32[]{:S(2)}) async-start(), calls=%async_computation.2 | async-start | bytes 7340032 | tf_op jit(solution)/shard_map/psum | solution.py:19
  11.9 215.0 %copy-start.5 = (s32[16]{0:T(128)S(1)}, s32[16]{0:T(128)}, u32[]{:S(2)}) copy-start(s32[16]{0:T(128)} %param.30) | copy-start | bytes 196
  15.7 211.1 %all-reduce.9.cloned.1.call-start = ((), (), s32[]{:S(2)}) async-start(), calls=%async_computation.3 | async-start | bytes 3670016 | tf_op jit(solution)/shard_map/psum | solution.py:25
  170.3 122.6 %all-reduce.11.cloned.1.call-start = ((), (), s32[]{:S(2)}) async-start(), calls=%async_computation.4 | async-start | bytes 3670016 | tf_op jit(solution)/shard_map/psum | solution.py:25
  226.9 155.5 %all-gather.5.cloned.1.call-start = ((), (), s32[]{:S(2)}) async-start(), calls=%async_computation | async-start | bytes 8912896 | tf_op jit(solution)/shard_map/all_gather | solution.py:30
  265.0 10.0 %copy-start.3 = (f32[2,128,128]{2,1,0:T(8,128)S(1)}, f32[2,128,128]{2,1,0:T(8,128)}, u32[]{:S(2)}) copy-start(f32[2,128,128]{2,1,0:T(8,128)} %param.29) | copy-start | bytes 393220
  265.0 10.0 %copy-start.4 = (f32[1024]{0:T(1024)S(1)}, f32[1024]{0:T(1024)}, u32[]{:S(2)}) copy-start(f32[1024]{0:T(1024)} %param.27) | copy-start | bytes 12292
  292.9 6.1 %copy-start.2 = (f32[128,1792]{1,0:T(8,128)S(1)}, f32[128,1792]{1,0:T(8,128)}, u32[]{:S(2)}) copy-start(f32[128,1792]{1,0:T(8,128)} %get-tuple-element.129) | copy-start | bytes 2752516
  308.0 177.2 %all-gather.7.cloned.1.call-start = ((), (), s32[]{:S(2)}) async-start(), calls=%async_computation.1 | async-start | bytes 8912896 | tf_op jit(solution)/shard_map/all_gather | solution.py:30
  382.4 10.6 %slice-start.2 = ((s8[7340032]{0:T(1024)(128)(4,1)}), s8[4194304]{0:T(1024)(128)(4,1)S(1)}, s32[]{:S(2)}) async-start(s8[7340032]{0:T(1024)(128)(4,1)} %bitcast.50), calls=%async_computation.7 | async-start | bytes 8388608
  382.4 10.6 %slice-start.3 = ((s8[7340032]{0:T(1024)(128)(4,1)}), s8[3145728]{0:T(1024)(128)(4,1)S(1)}, s32[]{:S(2)}) async-start(s8[7340032]{0:T(1024)(128)(4,1)} %bitcast.50), calls=%async_computation.8 | async-start | bytes 6291456
  399.4 5.9 %copy-start = (f32[1024,1792]{0,1:T(8,128)}, f32[1024,1792]{0,1:T(8,128)S(1)}, u32[]{:S(2)}) copy-start(f32[1024,1792]{0,1:T(8,128)S(1)} %convolution_subtract_fusion.1) | copy-start | bytes 22020100
  399.4 1.9 copy-start.1
  485.2 10.9 %slice-start = ((s8[7340032]{0:T(1024)(128)(4,1)}), s8[4194304]{0:T(1024)(128)(4,1)S(1)}, s32[]{:S(2)}) async-start(s8[7340032]{0:T(1024)(128)(4,1)} %bitcast.48), calls=%async_computation.5 | async-start | bytes 8388608
  485.2 10.9 %slice-start.1 = ((s8[7340032]{0:T(1024)(128)(4,1)}), s8[3145728]{0:T(1024)(128)(4,1)S(1)}, s32[]{:S(2)}) async-start(s8[7340032]{0:T(1024)(128)(4,1)} %bitcast.48), calls=%async_computation.6 | async-start | bytes 6291456
Sparse Core Ops, SparseCore 0:
  15.8 151.6 all-reduce.6
  170.5 56.3 all-reduce.8
  229.3 63.5 all-reduce.10
  308.1 74.2 all-gather.4
  414.4 70.6 all-gather.6
where the time goes:
time: 527 us; the launch traced here: 520 us
  waiting for transfers between devices  358 us (68%)
  between operations  56.6 us (11%)
  local copies, waits for them, and re-layouts  40.7 us (8%)
  matrix products  33.8 us (6%)
  other arithmetic  30.5 us (6%)
    psum x1, waiting for transfers between devices, from_root(): return lax.psum(kept, axis)  152 us
    all_gather x2, waiting for transfers between devices, broadcast(): lax.all_gather(shard, axis)  134 us
    psum x2, waiting for transfers between devices, spread(): shard = lax.psum(shard, axis)  71.9 us
    unnamed x23, local copies, waits for them, and re-layouts  29.2 us
    scatter x8, other arithmetic, inner_block(): block_cols = block_cols.at[:, low_col:low_col + SUB].set(quantized)  14.8 us
    dot_general x2, matrix products, local(): jnp.dot(errors, trail_rows, precision=lax.Precision.HIGHEST, preferred_el...  14.6 us
    dot_general x8, matrix products, inner_block(): jnp.dot(current - quantized, inverse[low_col:low_col + SUB, low_col:low_c...  13.1 us
  transfers between devices with their start and end apart: 5, of which 5 were waited for; matrix products, arithmetic and copies ran while one was open for 4% of the time, Pallas kernels for 0%

commit v1 on v0

v1 whole, which is shorter than its diff:
```python
import jax
import jax.numpy as jnp
from jax import lax
from jax.experimental import pallas as pl
from jax.experimental.pallas import tpu as pltpu
from jax.sharding import Mesh
from jax.sharding import PartitionSpec as P

BLK = 128
SUB = 32
LEVELS = 16
softness = 0.2

SIZES = (2, 4, 2, 4, 2)
AXES = ("xh", "y", "k", "z", "xl")
COLS = ("xh", "y", "k")
ROWS = ("z", "xl")
CHIPS = ("xh", "y")
N_CHIPS = 8
N_ROWS = 8
LANES = 256
VMEM = 48 * 1024 * 1024


def dot(a, b):
    return jnp.dot(a, b, precision=lax.Precision.HIGHEST, preferred_element_type=jnp.float32)


def fast_dot(a, b):
    return jnp.dot(a, b, preferred_element_type=jnp.float32)


def split(value):
    high = value.astype(jnp.bfloat16)
    low = (value - high.astype(jnp.float32)).astype(jnp.bfloat16)
    return high, low


def quantize(values, steps, inverse_steps, codes):
    levels = [codes[i].astype(jnp.float32) for i in range(LEVELS)]
    scaled = values * (inverse_steps * (0.5 / softness))
    output = jnp.full(values.shape, 0.5 * (levels[0] + levels[-1]), jnp.float32)
    for i in range(LEVELS - 1):
        half_gap = 0.5 * (levels[i + 1] - levels[i])
        shift = (levels[i] + levels[i + 1]) * (0.25 / softness)
        output = output + half_gap * jnp.tanh(scaled - shift)
    return output * steps


def inner_block(parts, steps, diag, inverse, codes):
    diag_t, inverse_t = diag.T, inverse.T
    rounded = [[] for _ in parts]
    errors = [[] for _ in parts]
    parts = list(parts)
    recip = [1.0 / s for s in steps]
    for g in range(BLK // SUB):
        low = g * SUB
        inv_g = inverse_t[low : low + SUB, low : low + SUB]
        later = diag_t[low + SUB :, low : low + SUB]
        for i, part in enumerate(parts):
            current = part[:SUB]
            quantized = quantize(current, steps[i], recip[i], codes)
            error = dot(inv_g, current - quantized)
            rounded[i].append(quantized)
            errors[i].append(error)
            if low + SUB < BLK:
                parts[i] = part[SUB:] - dot(later, error)
    return [jnp.concatenate(r, 0) for r in rounded], [jnp.concatenate(e, 0) for e in errors]


def transposed_parts(tiles):
    per = LANES // BLK
    turned = [t.T for t in tiles]
    return [jnp.concatenate(turned[i : i + per], 1) for i in range(0, len(turned), per)]


def first_kernel(flags, codes, halves_ref, scales_ref, inverse_ref, error_ref, rounded_ref):
    own = flags[0]
    tiles = []
    for half in range(2):
        for q in range(4):
            tiles.append(halves_ref[half, :, q * BLK : (q + 1) * BLK])
    diag = halves_ref[own, :, 4 * BLK : 5 * BLK]
    parts = transposed_parts(tiles)
    steps = [scales_ref[:, i * LANES : (i + 1) * LANES] for i in range(len(parts))]
    rounded, errors = inner_block(parts, steps, diag, inverse_ref[...], codes)
    for i in range(len(parts)):
        rows = slice(i * LANES, (i + 1) * LANES)
        rounded_ref[rows, :] = rounded[i].T
        high, low = split(errors[i].T)
        error_ref[rows, :BLK] = high
        error_ref[rows, BLK:] = low


def last_kernel(
    flags, codes, weight_ref, block_ref, rounded_ref, error_ref, panel_ref, panel1_ref, scales_ref, inverse_ref,
    out_ref, m0_ref, m0_low_ref, m1_ref, m1_low_ref, error1_ref, rounded1_ref,
):
    step = pl.program_id(0)
    after, owner, last = flags[1], flags[2], flags[3]
    rows = out_ref.shape[0]

    def stage(source, masked, pair_ref, low_ref):
        value = source[...]
        ids = lax.broadcasted_iota(jnp.int32, value.shape, 1)
        value = jnp.where(jnp.logical_and(masked == 1, ids < BLK), 0.0, value)
        high, low = split(value)
        pair_ref[:BLK, :] = high
        pair_ref[BLK:, :] = high
        low_ref[...] = low

    def product(error, pair, low):
        return fast_dot(error, pair) + fast_dot(error[:, :BLK], low)

    @pl.when(jnp.logical_and(step == 0, after == 1))
    def _():
        stage(panel_ref, owner, m0_ref, m0_low_ref)

    @pl.when(jnp.logical_and(step == 0, last == 1))
    def _():
        block = block_ref[...] - product(error_ref[...], m0_ref[:, :BLK], m0_low_ref[:, :BLK])
        tiles = [block[i * BLK : (i + 1) * BLK] for i in range(block.shape[0] // BLK)]
        parts = transposed_parts(tiles)
        steps = [scales_ref[:, i * LANES : (i + 1) * LANES] for i in range(len(parts))]
        rounded, errors = inner_block(parts, steps, panel1_ref[:, :BLK], inverse_ref[...], codes)
        for i in range(len(parts)):
            span = slice(i * LANES, (i + 1) * LANES)
            rounded1_ref[span, :] = rounded[i].T
            high, low = split(errors[i].T)
            error1_ref[span, :BLK] = high
            error1_ref[span, BLK:] = low
        stage(panel1_ref, last, m1_ref, m1_low_ref)

    here = pl.ds(pl.multiple_of(step * rows, rows), rows)

    @pl.when(after == 0)
    def _():
        out_ref[...] = weight_ref[...]

    @pl.when(jnp.logical_and(after == 1, last == 0))
    def _():
        out_ref[...] = weight_ref[...] - product(error_ref[here, :], m0_ref[...], m0_low_ref[...])

    @pl.when(last == 1)
    def _():
        out_ref[...] = (
            weight_ref[...]
            - product(error_ref[here, :], m0_ref[...], m0_low_ref[...])
            - product(error1_ref[here, :], m1_ref[...], m1_low_ref[...])
        )
        out_ref[:, :BLK] = rounded1_ref[here, :]

    @pl.when(owner == 1)
    def _():
        out_ref[:, :BLK] = rounded_ref[here, :]


def first_call(flags, codes, halves, scales, inverse):
    n = scales.shape[1]
    smem, vmem = pl.BlockSpec(memory_space=pltpu.SMEM), pl.BlockSpec(memory_space=pltpu.VMEM)
    return pl.pallas_call(
        first_kernel,
        out_shape=(jax.ShapeDtypeStruct((n, 2 * BLK), jnp.bfloat16), jax.ShapeDtypeStruct((n, BLK), jnp.float32)),
        in_specs=[smem, smem, vmem, vmem, vmem],
        out_specs=(vmem, vmem),
        compiler_params=pltpu.CompilerParams(vmem_limit_bytes=VMEM),
        cost_estimate=pl.CostEstimate(flops=10**9, bytes_accessed=2 * 10**6, transcendentals=2 * 10**6),
        name="round_first",
    )(flags, codes, halves, scales, inverse)


def last_call(flags, codes, weight, block, rounded, error, panel, panel1, scales, inverse):
    n, width = weight.shape
    rows = 128
    smem, vmem = pl.BlockSpec(memory_space=pltpu.SMEM), pl.BlockSpec(memory_space=pltpu.VMEM)
    tall = pl.BlockSpec((rows, width), lambda i: (i, 0))
    return pl.pallas_call(
        last_kernel,
        grid=(n // rows,),
        out_shape=jax.ShapeDtypeStruct((n, width), jnp.float32),
        in_specs=[smem, smem, tall, vmem, vmem, vmem, vmem, vmem, vmem, vmem],
        out_specs=tall,
        scratch_shapes=[
            pltpu.VMEM((2 * BLK, width), jnp.bfloat16),
            pltpu.VMEM((BLK, width), jnp.bfloat16),
            pltpu.VMEM((2 * BLK, width), jnp.bfloat16),
            pltpu.VMEM((BLK, width), jnp.bfloat16),
            pltpu.VMEM((n, 2 * BLK), jnp.bfloat16),
            pltpu.VMEM((n, BLK), jnp.float32),
        ],
        compiler_params=pltpu.CompilerParams(vmem_limit_bytes=VMEM),
        cost_estimate=pl.CostEstimate(flops=2 * 10**9, bytes_accessed=16 * 10**6, transcendentals=2 * 10**6),
        name="update_all",
    )(flags, codes, weight, block, rounded, error, panel, panel1, scales, inverse)


def device_at(chip, core, row):
    return (chip * 2 + core) * N_ROWS + row


def local(weight, scales, panels, block_inverse, grid_codes, block_starts):
    width = weight.shape[1]
    xh, y, core, z, xl = (lax.axis_index(a) for a in AXES)
    chip = xh * 4 + y
    row = z * 2 + xl
    col = chip * 2 + core
    owner = block_starts[0] // width
    owner_chip, owner_core = owner // 2, owner % 2
    piece = BLK // N_CHIPS
    swap = [(0, 1), (1, 0)]

    last_chip, last_core, last_row = N_CHIPS - 1, 1, N_ROWS - 1
    panel1 = panels[:, width:]
    for bit in (1, 2, 4):
        pairs = []
        for r in range(N_ROWS):
            if (r ^ last_row) & ~(2 * bit - 1) == 0:
                pairs.append((device_at(last_chip, last_core, r), device_at(last_chip, last_core, r ^ bit)))
        got = lax.ppermute(panel1, AXES, pairs)
        panel1 = jnp.where((row & bit) != 0, panel1, got)

    diag = jnp.where(core == 0, panels[:, :BLK], panels[:, width : width + BLK])
    got = lax.ppermute(diag, "xl", swap)
    diag = jnp.where(xl == (chip & 1), diag, got)
    got = lax.ppermute(diag, "z", [(i, i ^ 1) for i in range(4)])
    diag = jnp.where((z & 1) == ((chip >> 1) & 1), diag, got)
    got = lax.ppermute(diag, "z", [(i, i ^ 2) for i in range(4)])
    diag = jnp.where((z >> 1) == (chip >> 2), diag, got)

    block = weight[:, :BLK]
    half = block.shape[0] // 2
    left, right = panels[:, :width], panels[:, width:]
    top, bottom = block[:half], block[half:]
    got_panel = lax.ppermute(jnp.where(core == 0, right, left), "k", swap)
    got_block = lax.ppermute(jnp.where(core == 0, bottom, top), "k", swap)
    mine = core == owner_core
    panel = jnp.where(mine, jnp.where(core == 0, left, right), got_panel)
    rows_b = jnp.where(mine, jnp.where(core == 0, top, bottom), got_block)
    quarters = [rows_b[q * BLK : (q + 1) * BLK] for q in range(4)]

    sent = jnp.concatenate([panel] + quarters + [diag], axis=1)
    came = lax.all_to_all(sent, CHIPS, 0, 0, tiled=True)
    came = lax.dynamic_slice_in_dim(came, owner_chip * piece, piece, 0)

    pairs = [
        (device_at(d, k, r), device_at(r, k, d)) for d in range(N_CHIPS) for k in range(2) for r in range(N_ROWS)
    ]
    turned = lax.ppermute(came[:, :width], AXES, pairs)

    small = jnp.tile(came[:, width:], (N_CHIPS, 1))
    small = lax.all_to_all(small, CHIPS, 0, 0, tiled=True)
    other = lax.ppermute(small, "k", swap)
    halves = jnp.stack([jnp.where(core == 0, small, other), jnp.where(core == 0, other, small)])

    flags = jnp.stack(
        [
            owner_core,
            (col >= owner).astype(jnp.int32),
            (col == owner).astype(jnp.int32),
            (col == 2 * N_CHIPS - 1).astype(jnp.int32),
        ]
    )
    wide_scales = scales[None, :]
    error, rounded = first_call(flags, grid_codes, halves, wide_scales, block_inverse[0])

    panel0 = lax.all_to_all(jnp.tile(turned, (N_ROWS, 1)), ROWS, 0, 0, tiled=True)
    return last_call(
        flags, grid_codes, weight, block, rounded, error, panel0, panel1, wide_scales, block_inverse[1]
    )


def solution(mesh):
    torus = Mesh(mesh.devices.reshape(SIZES), AXES)
    return jax.shard_map(
        local,
        mesh=torus,
        in_specs=(P(ROWS, COLS), P(ROWS), P(COLS, ROWS), P(), P(), P()),
        out_specs=P(ROWS, COLS),
        check_vma=False,
    )
```

time: 527 us -> 99.8 us (0.19)
  the two profiles are of different devices: /device:TPU:1 before, /device:TPU:29 now
where the time goes in v1:
time: 99.8 us; the launch traced here: 99.2 us
  starting transfers between devices  31.8 us (32%)
  waiting for transfers between devices  31.6 us (32%)
  Pallas kernels  16.9 us (17%)
  other arithmetic  12.5 us (13%)
  local copies, waits for them, and re-layouts  5.95 us (6%)
    all_to_all x1, waiting for transfers between devices, local(): came = lax.all_to_all(sent, CHIPS, 0, 0, tiled=True)  14.2 us
    pallas_call x1, Pallas kernels, last_call(): pl.pallas_call(last_kernel, grid=(n // rows,), out_shape=jax.ShapeDtypeSt...  13.7 us
    ppermute x1, waiting for transfers between devices, local(): turned = lax.ppermute(came[:, :width], AXES, pairs)  9.64 us
    all_to_all x1, waiting for transfers between devices, local(): lax.all_to_all(jnp.tile(turned, (N_ROWS, 1)), ROWS, 0, 0, tiled=True)  6.94 us
    all_to_all x1, starting transfers between devices, local(): came = lax.all_to_all(sent, CHIPS, 0, 0, tiled=True)  6.62 us
    all_to_all x1, starting transfers between devices, local(): small = lax.all_to_all(small, CHIPS, 0, 0, tiled=True)  6.35 us
    select_n x3, other arithmetic, local(): panel1 = jnp.where(row & bit != 0, panel1, got)  6.15 us
    ppermute x3, starting transfers between devices, local(): got = lax.ppermute(panel1, AXES, pairs)  5.58 us
  transfers between devices with their start and end apart: 13, of which 4 were waited for; matrix products, arithmetic and copies ran while one was open for 17% of the time, Pallas kernels for 3%

profile of v1, /device:TPU:29, one launch (start us, length us, event | category | flops | bytes accessed | tf_op | source)
XLA Modules:
  0.0 99.2 jit_solution(15229000991023288604)
XLA Ops:
  0.0 0.9 slice_select_fusion.2
  0.9 0.0 copy-start.2
  0.9 0.0 copy-start.4
  0.9 1.0 %collective-permute-start.2 = (f32[128,128]{1,0:T(8,128)S(1)}, f32[128,128]{1,0:T(8,128)S(1)}, u32[]{:S(2)}, u32[]{:S(2)}) collective-permute-start(f32[128,128]{1,0:T(8,128)S(1)} %slice_select_fusion.2), channel_id=1, source_target_pairs={{0,1},{1,0},{2,3},{3,2},{4,5},{5,4},{6,7},{7,6},{8,9},{9,8},{10,11... | collective-permute-start | bytes 196616 | tf_op jit(solution)/shard_map/ppermute | solution.py:223
  1.9 2.5 %fusion = (f32[128,1792]{1,0:T(8,128)}, f32[128,1792]{1,0:T(8,128)S(1)}) fusion(f32[128,3584]{1,0:T(8,128)} %param.8, pred[]{:T(512)S(6)} %eq.31), kind=kLoop, calls=%fused_computation.22 | loop fusion | flops 229376 | bytes 3670017 | tf_op jit(solution)/shard_map/slice | solution.py:232
  4.4 1.6 %collective-permute-start.7 = (f32[128,1792]{1,0:T(8,128)}, f32[128,1792]{1,0:T(8,128)}, u32[]{:S(2)}, u32[]{:S(2)}) collective-permute-start(f32[128,1792]{1,0:T(8,128)} %get-tuple-element.11), channel_id=1, source_target_pairs={{126,127},{127,126}} | collective-permute-start | bytes 2752520 | tf_op jit(solution)/shard_map/ppermute | solution.py:219
  6.0 1.0 collective-permute-start
  7.0 0.0 collective-permute-done.2
  7.0 1.7 %collective-permute-start.3 = (f32[128,128]{1,0:T(8,128)S(1)}, f32[128,128]{1,0:T(8,128)S(1)}, u32[]{:S(2)}, u32[]{:S(2)}) collective-permute-start(f32[128,128]{1,0:T(8,128)S(1)} %broadcast_select_fusion.3), channel_id=1, source_target_pairs={{0,2},{2,0},{4,6},{6,4},{1,3},{3,1},{5,7},{7,5},{8,10},{10,8},{12,... | collective-permute-start | bytes 196616 | tf_op jit(solution)/shard_map/ppermute | solution.py:225
  8.7 1.1 %slice_select_fusion.1 = f32[512,128]{1,0:T(8,128)S(1)} fusion(f32[1024,1792]{1,0:T(8,128)} %weight_ref.1, pred[]{:T(512)S(6)} %eq.31), kind=kLoop, calls=%fused_computation.9 | loop fusion | flops 65536 | bytes 786433 | tf_op jit(solution)/shard_map/jit(_where)/select_n | solution.py:235
  9.8 0.4 collective-permute-start.1
  10.3 0.8 collective-permute-done.3
  11.1 3.3 %collective-permute-start.4 = (f32[128,128]{1,0:T(8,128)S(1)}, f32[128,128]{1,0:T(8,128)S(1)}, u32[]{:S(2)}, u32[]{:S(2)}) collective-permute-start(f32[128,128]{1,0:T(8,128)S(1)} %broadcast_select_fusion.4), channel_id=1, source_target_pairs={{0,4},{2,6},{4,0},{6,2},{1,5},{3,7},{5,1},{7,3},{8,12},{10,14},{12... | collective-permute-start | bytes 196616 | tf_op jit(solution)/shard_map/ppermute | solution.py:227
  14.4 0.0 collective-permute-done.1
  14.4 1.1 %select_select_fusion = f32[512,128]{1,0:T(8,128)S(1)} fusion(f32[512,128]{1,0:T(8,128)S(1)} %collective-permute-done.1, f32[1024,1792]{1,0:T(8,128)} %weight_ref.1, pred[]{:T(512)S(6)} %eq.31, pred[]{:T(512)S(6)} %eq.32), kind=kLoop, calls=%fused_computation.8 | loop fusion | flops 131072 | bytes 1048578 | tf_op jit(solution)/shard_map/jit(_where)/select_n | solution.py:238
  15.5 0.0 collective-permute-done.7
  15.5 0.0 collective-permute-done
  15.5 2.6 %broadcast_select_fusion = (f32[128,1792]{1,0:T(8,128)S(1)}, f32[128,2432]{1,0:T(8,128)}) fusion(f32[128,1792]{1,0:T(8,128)} %collective-permute-done.7, pred[]{:T(512)S(6)} %ne.35, f32[128,3584]{1,0:T(8,128)S(1)} %copy-done.2, f32[128,1792]{1,0:T(8,128)} %collective-permute-done, pred[]{:T(512)S(6)} %eq.31, pred[]{:T(512)S(6)} %eq.32), kind=kLoop, calls=%fused_computation.3 | loop fusion | flops 688127 | bytes 5505027 | tf_op jit(solution)/shard_map/jit(_where)/select_n | solution.py:220
  18.1 0.6 slice_dynamic-update-slice_fusion.3
  18.7 0.6 slice_dynamic-update-slice_fusion.2
  19.4 0.6 slice_dynamic-update-slice_fusion.1
  20.0 0.6 slice_dynamic-update-slice_fusion
  20.7 0.0 collective-permute-done.4
  20.7 0.6 select_dynamic-update-slice_fusion.1
  21.3 6.6 %all-to-all-start = ((f32[8,16,2432]{2,1,0:T(8,128)}), f32[8,16,2432]{2,1,0:T(8,128)S(1)}, u32[]{:S(2)}, u32[]{:S(2)}) async-start(f32[8,16,2432]{2,1,0:T(8,128)} %bitcast.6), calls=%async_computation | async-start | bytes 2490368 | tf_op jit(solution)/shard_map/all_to_all | solution.py:242
  27.9 1.6 %collective-permute-start.8 = (f32[128,1792]{1,0:T(8,128)S(1)}, f32[128,1792]{1,0:T(8,128)}, u32[]{:S(2)}, u32[]{:S(2)}) collective-permute-start(f32[128,1792]{1,0:T(8,128)S(1)} %get-tuple-element.9), channel_id=1, source_target_pairs={{124,126},{125,127},{126,124},{127,125}} | collective-permute-start | bytes 2752520 | tf_op jit(solution)/shard_map/ppermute | solution.py:219
  29.5 14.2 %all-to-all-done = f32[8,16,2432]{2,1,0:T(8,128)S(1)} async-done(((f32[8,16,2432]{2,1,0:T(8,128)}), f32[8,16,2432]{2,1,0:T(8,128)S(1)}, u32[]{:S(2)}, u32[]{:S(2)}) %all-to-all-start) | async-done | bytes 1245216 | tf_op jit(solution)/shard_map/all_to_all | solution.py:242
  43.8 0.7 tile.4
  44.5 6.4 %all-to-all-start.1 = ((f32[8,16,640]{2,1,0:T(8,128)}), f32[8,16,640]{2,1,0:T(8,128)S(1)}, u32[]{:S(2)}, u32[]{:S(2)}) async-start(f32[8,16,640]{2,1,0:T(8,128)} %tile.4), calls=%async_computation.1 | async-start | bytes 655360 | tf_op jit(solution)/shard_map/all_to_all | solution.py:251
  50.9 0.0 collective-permute-done.8
  50.9 2.3 %broadcast_select_fusion.1 = f32[128,1792]{1,0:T(8,128)} fusion(f32[128,1792]{1,0:T(8,128)S(1)} %get-tuple-element.9, f32[128,1792]{1,0:T(8,128)} %collective-permute-done.8, pred[]{:T(512)S(6)} %ne.34), kind=kLoop, calls=%fused_computation.4 | loop fusion | flops 229376 | bytes 2752513 | tf_op jit(solution)/shard_map/jit(_where)/select_n | solution.py:220
  53.2 2.4 %collective-permute-start.9 = (f32[128,1792]{1,0:T(8,128)}, f32[128,1792]{1,0:T(8,128)}, u32[]{:S(2)}, u32[]{:S(2)}) collective-permute-start(f32[128,1792]{1,0:T(8,128)} %broadcast_select_fusion.1), channel_id=1, source_target_pairs={{120,124},{121,125},{122,126},{123,127},{124,120},{125,121},{126,1... | collective-permute-start | bytes 2752520 | tf_op jit(solution)/shard_map/ppermute | solution.py:219
  55.6 1.9 %collective-permute-start.6 = (f32[16,1792]{1,0:T(8,128)S(1)}, f32[16,1792]{1,0:T(8,128)S(1)}, u32[]{:S(2)}, u32[]{:S(2)}) collective-permute-start(f32[16,1792]{1,0:T(8,128)S(1)} %constant_dynamic-slice_fusion), channel_id=1, source_target_pairs={{0,0},{1,16},{2,32},{3,48},{4,64},{5,80},{6,96},{7,112},{8,8},{9,2... | collective-permute-start | bytes 344072 | tf_op jit(solution)/shard_map/ppermute | solution.py:248
  57.5 0.4 collective-permute-start.5
  57.9 1.1 %slice.52.block_ref = f32[1024,128]{1,0:T(8,128)S(1)} slice(f32[1024,1792]{1,0:T(8,128)} %weight_ref.1), slice={[0:1024], [0:128]} | slice | bytes 1048576 | tf_op jit(solution)/shard_map/slice | solution.py:230
  59.0 0.1 pad_add_fusion.flags
  59.1 9.6 %collective-permute-done.6 = f32[16,1792]{1,0:T(8,128)S(1)} collective-permute-done((f32[16,1792]{1,0:T(8,128)S(1)}, f32[16,1792]{1,0:T(8,128)S(1)}, u32[]{:S(2)}, u32[]{:S(2)}) %collective-permute-start.6) | collective-permute-done | bytes 114720 | tf_op jit(solution)/shard_map/ppermute | solution.py:248
  68.7 1.0 tile.5
  69.7 3.6 %all-to-all-start.2 = ((f32[8,16,1792]{2,1,0:T(8,128)}), f32[8,16,1792]{2,1,0:T(8,128)S(1)}, u32[]{:S(2)}, u32[]{:S(2)}) async-start(f32[8,16,1792]{2,1,0:T(8,128)} %tile.5), calls=%async_computation.2 | async-start | bytes 1835008 | tf_op jit(solution)/shard_map/all_to_all | solution.py:266
  73.3 0.0 copy-start
  73.3 0.0 copy-start.1
  73.3 0.0 collective-permute-done.5
  73.3 0.1 select_bitcast_fusion.1
  73.4 0.5 copy-done
  74.0 3.3 %round_first.1 = (bf16[1024,256]{1,0:T(8,128)(2,1)S(1)}, f32[1024,128]{1,0:T(8,128)S(1)}) custom-call(s32[4]{0:T(128)S(1)} %pad_add_fusion.flags, s32[16]{0:T(128)S(1)} %copy-done.1, f32[2,128,640]{2,1,0:T(8,128)S(1)} %pad_maximum_fusion.halves_ref, f32[1,1024]{1,0:T(1,128)S(1)} %bitcast.23, f32[128,128]{1,0:T(8,128)S(1)} %get-tuple-element.16.inverse_ref), custom_call_target="tpu_custom_call" | custom-call | flops 1000000000 | bytes 2000000 | tf_op jit(solution)/shard_map/round_first/pallas_call | solution.py:161
  77.2 1.3 %broadcast_select_fusion.2.panel1_ref = f32[128,1792]{1,0:T(8,128)S(1)} fusion(f32[128,1792]{1,0:T(8,128)} %broadcast_select_fusion.1, f32[128,1792]{1,0:T(8,128)} %collective-permute-done.9, pred[]{:T(512)S(6)} %ne.33), kind=kLoop, calls=%fused_computation.5 | loop fusion | flops 229376 | bytes 2752513 | tf_op jit(solution)/shard_map/jit(_where)/select_n | solution.py:220
  78.5 6.9 %all-to-all-done.2 = f32[8,16,1792]{2,1,0:T(8,128)S(1)} async-done(((f32[8,16,1792]{2,1,0:T(8,128)}), f32[8,16,1792]{2,1,0:T(8,128)S(1)}, u32[]{:S(2)}, u32[]{:S(2)}) %all-to-all-start.2) | async-done | bytes 917536 | tf_op jit(solution)/shard_map/all_to_all | solution.py:266
  85.5 13.7 %update_all.1 = f32[1024,1792]{1,0:T(8,128)} custom-call(s32[4]{0:T(128)S(1)} %pad_add_fusion.flags, s32[16]{0:T(128)S(1)} %copy-done.1, f32[1024,1792]{1,0:T(8,128)} %weight_ref.1, f32[1024,128]{1,0:T(8,128)S(1)} %slice.52.block_ref, f32[1024,128]{1,0:T(8,128)S(1)} %get-tuple-element.7.rounded_ref, bf16[1024,256]{1,0:T(8,128)(2,1)S(1)} %get-tuple-element.8.error_ref, ...), custom_call_target="tpu_custom_call" | custom-call | flops 2000000000 | bytes 16000000 | tf_op jit(solution)/shard_map/update_all/pallas_call | solution.py:177
  (13 shorter events, 0.1 us)
Async XLA Ops:
  0.9 6.1 %copy-start.2 = (f32[128,3584]{1,0:T(8,128)S(1)}, f32[128,3584]{1,0:T(8,128)}, u32[]{:S(2)}) copy-start(f32[128,3584]{1,0:T(8,128)} %param.8) | copy-start | bytes 5505028
  0.9 9.3 %copy-start.4 = (s32[2]{0:T(128)S(1)}, s32[2]{0:T(128)}, u32[]{:S(2)}) copy-start(s32[2]{0:T(128)} %param.11) | copy-start | bytes 28
  0.9 6.1 %collective-permute-start.2 = (f32[128,128]{1,0:T(8,128)S(1)}, f32[128,128]{1,0:T(8,128)S(1)}, u32[]{:S(2)}, u32[]{:S(2)}) collective-permute-start(f32[128,128]{1,0:T(8,128)S(1)} %slice_select_fusion.2), channel_id=1, source_target_pairs={{0,1},{1,0},{2,3},{3,2},{4,5},{5,4},{6,7},{7,6},{8,9},{9,8},{10,11... | collective-permute-start | bytes 196616 | tf_op jit(solution)/shard_map/ppermute | solution.py:223
  4.4 11.1 %collective-permute-start.7 = (f32[128,1792]{1,0:T(8,128)}, f32[128,1792]{1,0:T(8,128)}, u32[]{:S(2)}, u32[]{:S(2)}) collective-permute-start(f32[128,1792]{1,0:T(8,128)} %get-tuple-element.11), channel_id=1, source_target_pairs={{126,127},{127,126}} | collective-permute-start | bytes 2752520 | tf_op jit(solution)/shard_map/ppermute | solution.py:219
  6.0 9.5 %collective-permute-start = (f32[128,1792]{1,0:T(8,128)S(1)}, f32[128,1792]{1,0:T(8,128)}, u32[]{:S(2)}, u32[]{:S(2)}) collective-permute-start(f32[128,1792]{1,0:T(8,128)S(1)} %get-tuple-element.12), channel_id=1, source_target_pairs={{0,8},{8,0},{1,9},{9,1},{2,10},{10,2},{3,11},{11,3},{4,12},{12,4},... | collective-permute-start | bytes 2752520 | tf_op jit(solution)/shard_map/ppermute | solution.py:234
  7.0 4.1 %collective-permute-start.3 = (f32[128,128]{1,0:T(8,128)S(1)}, f32[128,128]{1,0:T(8,128)S(1)}, u32[]{:S(2)}, u32[]{:S(2)}) collective-permute-start(f32[128,128]{1,0:T(8,128)S(1)} %broadcast_select_fusion.3), channel_id=1, source_target_pairs={{0,2},{2,0},{4,6},{6,4},{1,3},{3,1},{5,7},{7,5},{8,10},{10,8},{12,... | collective-permute-start | bytes 196616 | tf_op jit(solution)/shard_map/ppermute | solution.py:225
  9.8 4.6 %collective-permute-start.1 = (f32[512,128]{1,0:T(8,128)S(1)}, f32[512,128]{1,0:T(8,128)S(1)}, u32[]{:S(2)}, u32[]{:S(2)}) collective-permute-start(f32[512,128]{1,0:T(8,128)S(1)} %slice_select_fusion.1), channel_id=1, source_target_pairs={{0,8},{8,0},{1,9},{9,1},{2,10},{10,2},{3,11},{11,3},{4,12},{12,4},... | collective-permute-start | bytes 786440 | tf_op jit(solution)/shard_map/ppermute | solution.py:235
  11.1 9.5 %collective-permute-start.4 = (f32[128,128]{1,0:T(8,128)S(1)}, f32[128,128]{1,0:T(8,128)S(1)}, u32[]{:S(2)}, u32[]{:S(2)}) collective-permute-start(f32[128,128]{1,0:T(8,128)S(1)} %broadcast_select_fusion.4), channel_id=1, source_target_pairs={{0,4},{2,6},{4,0},{6,2},{1,5},{3,7},{5,1},{7,3},{8,12},{10,14},{12... | collective-permute-start | bytes 196616 | tf_op jit(solution)/shard_map/ppermute | solution.py:227
  21.3 22.5 %all-to-all-start = ((f32[8,16,2432]{2,1,0:T(8,128)}), f32[8,16,2432]{2,1,0:T(8,128)S(1)}, u32[]{:S(2)}, u32[]{:S(2)}) async-start(f32[8,16,2432]{2,1,0:T(8,128)} %bitcast.6), calls=%async_computation | async-start | bytes 2490368 | tf_op jit(solution)/shard_map/all_to_all | solution.py:242
  27.9 23.0 %collective-permute-start.8 = (f32[128,1792]{1,0:T(8,128)S(1)}, f32[128,1792]{1,0:T(8,128)}, u32[]{:S(2)}, u32[]{:S(2)}) collective-permute-start(f32[128,1792]{1,0:T(8,128)S(1)} %get-tuple-element.9), channel_id=1, source_target_pairs={{124,126},{125,127},{126,124},{127,125}} | collective-permute-start | bytes 2752520 | tf_op jit(solution)/shard_map/ppermute | solution.py:219
  44.5 12.9 %all-to-all-start.1 = ((f32[8,16,640]{2,1,0:T(8,128)}), f32[8,16,640]{2,1,0:T(8,128)S(1)}, u32[]{:S(2)}, u32[]{:S(2)}) async-start(f32[8,16,640]{2,1,0:T(8,128)} %tile.4), calls=%async_computation.1 | async-start | bytes 655360 | tf_op jit(solution)/shard_map/all_to_all | solution.py:251
  50.9 7.0 %copy-start.3 = (f32[2,128,128]{2,1,0:T(8,128)S(1)}, f32[2,128,128]{2,1,0:T(8,128)}, u32[]{:S(2)}) copy-start(f32[2,128,128]{2,1,0:T(8,128)} %param.9) | copy-start | bytes 393220
  53.2 24.1 %collective-permute-start.9 = (f32[128,1792]{1,0:T(8,128)}, f32[128,1792]{1,0:T(8,128)}, u32[]{:S(2)}, u32[]{:S(2)}) collective-permute-start(f32[128,1792]{1,0:T(8,128)} %broadcast_select_fusion.1), channel_id=1, source_target_pairs={{120,124},{121,125},{122,126},{123,127},{124,120},{125,121},{126,1... | collective-permute-start | bytes 2752520 | tf_op jit(solution)/shard_map/ppermute | solution.py:219
  55.6 13.2 %collective-permute-start.6 = (f32[16,1792]{1,0:T(8,128)S(1)}, f32[16,1792]{1,0:T(8,128)S(1)}, u32[]{:S(2)}, u32[]{:S(2)}) collective-permute-start(f32[16,1792]{1,0:T(8,128)S(1)} %constant_dynamic-slice_fusion), channel_id=1, source_target_pairs={{0,0},{1,16},{2,32},{3,48},{4,64},{5,80},{6,96},{7,112},{8,8},{9,2... | collective-permute-start | bytes 344072 | tf_op jit(solution)/shard_map/ppermute | solution.py:248
  57.5 15.8 %collective-permute-start.5 = (f32[128,640]{1,0:T(8,128)S(1)}, f32[128,640]{1,0:T(8,128)S(1)}, u32[]{:S(2)}, u32[]{:S(2)}) collective-permute-start(f32[128,640]{1,0:T(8,128)S(1)} %bitcast.27), channel_id=1, source_target_pairs={{0,8},{8,0},{1,9},{9,1},{2,10},{10,2},{3,11},{11,3},{4,12},{12,4},... | collective-permute-start | bytes 983048 | tf_op jit(solution)/shard_map/ppermute | solution.py:252
  69.7 15.8 %all-to-all-start.2 = ((f32[8,16,1792]{2,1,0:T(8,128)}), f32[8,16,1792]{2,1,0:T(8,128)S(1)}, u32[]{:S(2)}, u32[]{:S(2)}) async-start(f32[8,16,1792]{2,1,0:T(8,128)} %tile.5), calls=%async_computation.2 | async-start | bytes 1835008 | tf_op jit(solution)/shard_map/all_to_all | solution.py:266
  73.3 0.7 copy-start
  73.3 0.7 copy-start.1

commit v2 on v1

v2 whole, which is shorter than its diff:
```python
import functools

import jax
import jax.numpy as jnp
from jax import lax
from jax.experimental import pallas as pl
from jax.experimental.pallas import tpu as pltpu
from jax.sharding import Mesh
from jax.sharding import PartitionSpec as P

BLK = 128
SUB = 32
LEVELS = 16
softness = 0.2

SIZES = (2, 4, 2, 4, 2)
AXES = ("xh", "y", "k", "z", "xl")
COLS = ("xh", "y", "k")
ROWS = ("z", "xl")
CHIPS = ("xh", "y")
N_CHIPS = 8
N_ROWS = 8
LANES = 256
VMEM = 16 * 1024 * 1024
WIDE_VMEM = 51 * 1024 * 1024
BIG_VMEM = 54 * 1024 * 1024


def dot(a, b):
    return jnp.dot(a, b, precision=lax.Precision.HIGHEST, preferred_element_type=jnp.float32)


def fast_dot(a, b):
    return jnp.dot(a, b, preferred_element_type=jnp.float32)


def split(value):
    high = value.astype(jnp.bfloat16)
    low = (value - high.astype(jnp.float32)).astype(jnp.bfloat16)
    return high, low


def quantize(values, steps, inverse_steps, codes):
    levels = [codes[i].astype(jnp.float32) for i in range(LEVELS)]
    scaled = values * (inverse_steps * (0.5 / softness))
    output = jnp.full(values.shape, 0.5 * (levels[0] + levels[-1]), jnp.float32)
    for i in range(LEVELS - 1):
        half_gap = 0.5 * (levels[i + 1] - levels[i])
        shift = (levels[i] + levels[i + 1]) * (0.25 / softness)
        output = output + half_gap * jnp.tanh(scaled - shift)
    return output * steps


def inner_block(parts, steps, diag, inverse, codes):
    diag_t, inverse_t = diag.T, inverse.T
    rounded = [[] for _ in parts]
    errors = [[] for _ in parts]
    parts = list(parts)
    recip = [1.0 / s for s in steps]
    for g in range(BLK // SUB):
        low = g * SUB
        inv_g = inverse_t[low : low + SUB, low : low + SUB]
        later = diag_t[low + SUB :, low : low + SUB]
        for i, part in enumerate(parts):
            current = part[:SUB]
            quantized = quantize(current, steps[i], recip[i], codes)
            error = dot(inv_g, current - quantized)
            rounded[i].append(quantized)
            errors[i].append(error)
            if low + SUB < BLK:
                parts[i] = part[SUB:] - dot(later, error)
    return [jnp.concatenate(r, 0) for r in rounded], [jnp.concatenate(e, 0) for e in errors]


def transposed_parts(tiles):
    per = LANES // BLK
    turned = [t.T for t in tiles]
    return [jnp.concatenate(turned[i : i + per], 1) for i in range(0, len(turned), per)]


def first_kernel(flags, codes, small_ref, other_ref, scales_ref, inverse_ref, error_ref, rounded_ref):
    core, mine = flags[4], flags[0]
    half = scales_ref.shape[1] // 2
    parts, steps, places = [], [], []
    for ref, side in ((small_ref, core), (other_ref, 1 - core)):
        tiles = [ref[i : i + BLK, :] for i in range(0, half, BLK)]
        for i, part in enumerate(transposed_parts(tiles)):
            place = pl.multiple_of(side * half + i * LANES, LANES)
            parts.append(part)
            places.append(place)
            steps.append(scales_ref[:, pl.ds(place, LANES)])
    diag = jnp.where(mine == 1, small_ref[half:, :], other_ref[half:, :])
    rounded, errors = inner_block(parts, steps, diag, inverse_ref[...], codes)
    for i, place in enumerate(places):
        rows = pl.ds(place, LANES)
        rounded_ref[rows, :] = rounded[i].T
        high, low = split(errors[i].T)
        error_ref[rows, :BLK] = high
        error_ref[rows, BLK:] = low


def prepare_kernel(panel_ref, block_ref, own_ref, other_ref, diag_ref, one_ref, two_ref):
    core = lax.axis_index("k")
    last = (lax.axis_index("xh") * 4 + lax.axis_index("y")) * 2 + core == 2 * N_CHIPS - 1
    width, half = panel_ref.shape[1] // 2, block_ref.shape[0] // 2

    @pl.when(last)
    def _():
        one_ref[...] = panel_ref[:, width : width + width // 2]
        two_ref[...] = panel_ref[:, width + width // 2 :]

    piece = BLK // N_CHIPS
    for side in range(2):

        @pl.when(core == side)
        def _():
            diag_ref[...] = panel_ref[:, side * width : side * width + BLK]
            for ref, take in ((own_ref, side), (other_ref, 1 - side)):
                ref[:, :width] = panel_ref[:, take * width : (take + 1) * width]
                for q in range(half // BLK):
                    row = take * half + q * BLK
                    ref[:, width + q * BLK : width + (q + 1) * BLK] = block_ref[row : row + BLK, :]


def join_kernel(flags, rows_ref, diag_ref, got_ref, small_ref):
    z, chip = flags[5], flags[6]
    near = lax.div(z, 2) == lax.div(chip, 4)
    n = rows_ref.shape[0]
    small_ref[:n, :] = rows_ref[...]
    small_ref[n:, :] = jnp.where(near, diag_ref[...], got_ref[...])


def copies_kernel(flags, piece_ref, spread_ref):
    for e in range(N_ROWS):
        spread_ref[e] = piece_ref[...]


def choose_kernel(flags, own_ref, got_ref, panel_ref, rows_ref):
    mine, width = flags[0], panel_ref.shape[1]
    for value, ref in ((1, own_ref), (0, got_ref)):

        @pl.when(mine == value)
        def _():
            panel_ref[...] = ref[:, :width]
            for q in range(rows_ref.shape[0] // BLK):
                rows_ref[q * BLK : (q + 1) * BLK, :] = ref[:, width + q * BLK : width + (q + 1) * BLK]


def small_call(kernel, name, shapes, flags, *arrays, flops=0):
    smem, vmem = pl.BlockSpec(memory_space=pltpu.SMEM), pl.BlockSpec(memory_space=pltpu.VMEM)
    return pl.pallas_call(
        kernel,
        out_shape=tuple(jax.ShapeDtypeStruct(shape, jnp.float32) for shape in shapes),
        in_specs=[smem] + [vmem] * len(arrays),
        out_specs=(vmem,) * len(shapes),
        compiler_params=pltpu.CompilerParams(vmem_limit_bytes=VMEM),
        cost_estimate=pl.CostEstimate(flops=flops, bytes_accessed=10**5, transcendentals=0),
        name=name,
    )(flags, *arrays)


def prepare_call(panels, weight):
    n, wide = panels.shape
    rows = weight.shape[0]
    tall = wide // 2 + rows // 2
    whole = lambda shape: pl.BlockSpec(shape, lambda i: (0, 0))
    return pl.pallas_call(
        prepare_kernel,
        grid=(1,),
        out_shape=tuple(jax.ShapeDtypeStruct(s, jnp.float32) for s in ((n, tall), (n, tall), (n, BLK), (n, wide // 4), (n, wide // 4))),
        in_specs=[whole((n, wide)), whole((rows, BLK))],
        out_specs=(whole((n, tall)), whole((n, tall)), whole((n, BLK)), whole((n, wide // 4)), whole((n, wide // 4))),
        compiler_params=pltpu.CompilerParams(vmem_limit_bytes=BIG_VMEM),
        name="halves",
    )(panels, weight)


def last_kernel(
    flags, codes, weight_hbm, rounded_ref, error_ref, panel_ref, one_hbm, got_one_hbm, two_hbm, got_two_hbm, scales_ref, inverse_ref,
    out_ref, m0_ref, m0_low_ref, m1_ref, m1_low_ref, error1_ref, rounded1_ref, weight_ref, arrived, panel1_ref, block_ref, down_done,
):
    step = pl.program_id(0)
    after, owner, last = flags[1], flags[2], flags[3]
    rows = out_ref.shape[0]

    def read(i):
        span = pl.ds(pl.multiple_of(i * rows, rows), rows)
        return pltpu.make_async_copy(weight_hbm.at[span, :], weight_ref.at[span, :], arrived.at[i])

    block_read = pltpu.make_async_copy(weight_hbm.at[:, :BLK], block_ref, down_done.at[1])

    @pl.when(jnp.logical_and(step == 0, last == 1))
    def _():
        block_read.start()

    half = out_ref.shape[1] // 2
    left, right = panel1_ref.at[:, :half], panel1_ref.at[:, half:]
    for bit, kept, got, place, at in ((4, one_hbm, got_one_hbm, left, 0), (1, two_hbm, got_two_hbm, right, 2)):
        for held, source in ((True, kept), (False, got)):

            @pl.when(jnp.logical_and(jnp.logical_and(step == 0, last == 1), ((flags[8] & bit) != 0) == held))
            def _():
                pltpu.make_async_copy(source, place, down_done.at[at]).start()

    @pl.when(step == 0)
    def _():
        for i in range(weight_hbm.shape[0] // rows):
            read(i).start()

    def stage(source, masked, pair_ref, low_ref):
        value = source[...]
        ids = lax.broadcasted_iota(jnp.int32, value.shape, 1)
        value = jnp.where(jnp.logical_and(masked == 1, ids < BLK), 0.0, value)
        high, low = split(value)
        pair_ref[:BLK, :] = high
        pair_ref[BLK:, :] = high
        low_ref[...] = low

    def product(error, pair, low):
        return fast_dot(error, pair) + fast_dot(error[:, :BLK], low)

    @pl.when(jnp.logical_and(step == 0, after == 1))
    def _():
        stage(panel_ref, owner, m0_ref, m0_low_ref)

    @pl.when(jnp.logical_and(step == 0, last == 1))
    def _():
        pltpu.make_async_copy(one_hbm, left, down_done.at[0]).wait()
        pltpu.make_async_copy(two_hbm, right, down_done.at[2]).wait()
        block_read.wait()
        block = block_ref[...] - product(error_ref[...], m0_ref[:, :BLK], m0_low_ref[:, :BLK])
        tiles = [block[i * BLK : (i + 1) * BLK] for i in range(block.shape[0] // BLK)]
        parts = transposed_parts(tiles)
        steps = [scales_ref[:, i * LANES : (i + 1) * LANES] for i in range(len(parts))]
        rounded, errors = inner_block(parts, steps, panel1_ref[:, :BLK], inverse_ref[...], codes)
        for i in range(len(parts)):
            span = slice(i * LANES, (i + 1) * LANES)
            rounded1_ref[span, :] = rounded[i].T
            high, low = split(errors[i].T)
            error1_ref[span, :BLK] = high
            error1_ref[span, BLK:] = low
        stage(panel1_ref, last, m1_ref, m1_low_ref)

    here = pl.ds(pl.multiple_of(step * rows, rows), rows)
    read(step).wait()

    @pl.when(after == 0)
    def _():
        out_ref[...] = weight_ref[here, :]

    @pl.when(jnp.logical_and(after == 1, last == 0))
    def _():
        out_ref[...] = weight_ref[here, :] - product(error_ref[here, :], m0_ref[...], m0_low_ref[...])

    @pl.when(last == 1)
    def _():
        out_ref[...] = (
            weight_ref[here, :]
            - product(error_ref[here, :], m0_ref[...], m0_low_ref[...])
            - product(error1_ref[here, :], m1_ref[...], m1_low_ref[...])
        )
        out_ref[:, :BLK] = rounded1_ref[here, :]

    @pl.when(owner == 1)
    def _():
        out_ref[:, :BLK] = rounded_ref[here, :]


def first_call(flags, codes, small, other, scales, inverse):
    n = scales.shape[1]
    smem, vmem = pl.BlockSpec(memory_space=pltpu.SMEM), pl.BlockSpec(memory_space=pltpu.VMEM)
    return pl.pallas_call(
        first_kernel,
        out_shape=(jax.ShapeDtypeStruct((n, 2 * BLK), jnp.bfloat16), jax.ShapeDtypeStruct((n, BLK), jnp.float32)),
        in_specs=[smem, smem, vmem, vmem, vmem, vmem],
        out_specs=(vmem, vmem),
        compiler_params=pltpu.CompilerParams(vmem_limit_bytes=VMEM),
        cost_estimate=pl.CostEstimate(flops=0, bytes_accessed=10**5, transcendentals=0),
        name="round_first",
    )(flags, codes, small, other, scales, inverse)


def last_call(flags, codes, weight, rounded, error, panel, panel1, scales, inverse):
    n, width = weight.shape
    rows = 256
    smem, vmem = pl.BlockSpec(memory_space=pltpu.SMEM), pl.BlockSpec(memory_space=pltpu.VMEM)
    tall, hbm = pl.BlockSpec((rows, width), lambda i: (i, 0)), pl.BlockSpec(memory_space=pltpu.HBM)
    return pl.pallas_call(
        last_kernel,
        grid=(n // rows,),
        out_shape=jax.ShapeDtypeStruct((n, width), jnp.float32),
        in_specs=[smem, smem, hbm] + [vmem] * 3 + [hbm] * 4 + [vmem] * 2,
        out_specs=tall,
        scratch_shapes=[
            pltpu.VMEM((2 * BLK, width), jnp.bfloat16),
            pltpu.VMEM((BLK, width), jnp.bfloat16),
            pltpu.VMEM((2 * BLK, width), jnp.bfloat16),
            pltpu.VMEM((BLK, width), jnp.bfloat16),
            pltpu.VMEM((n, 2 * BLK), jnp.bfloat16),
            pltpu.VMEM((n, BLK), jnp.float32),
            pltpu.VMEM((n, width), jnp.float32),
            pltpu.SemaphoreType.DMA((n // rows,)),
            pltpu.VMEM((BLK, width), jnp.float32),
            pltpu.VMEM((n, BLK), jnp.float32),
            pltpu.SemaphoreType.DMA((3,)),
        ],
        compiler_params=pltpu.CompilerParams(vmem_limit_bytes=WIDE_VMEM),
        cost_estimate=pl.CostEstimate(flops=2 * 10**9, bytes_accessed=16 * 10**6, transcendentals=2 * 10**6),
        name="update_all",
    )(flags, codes, weight, rounded, error, panel, *panel1, scales, inverse)


def device_at(chip, core, row):
    return (chip * 2 + core) * N_ROWS + row


def local(weight, scales, panels, block_inverse, grid_codes, block_starts):
    width = weight.shape[1]
    xh, y, core, z, xl = (lax.axis_index(a) for a in AXES)
    chip = xh * 4 + y
    row = z * 2 + xl
    col = chip * 2 + core
    owner = block_starts[0] // width
    owner_chip, owner_core = owner // 2, owner % 2
    mine = core == owner_core
    piece = BLK // N_CHIPS
    swap = [(0, 1), (1, 0)]
    flags = jnp.stack(
        [
            mine.astype(jnp.int32),
            (col >= owner).astype(jnp.int32),
            (col == owner).astype(jnp.int32),
            (col == 2 * N_CHIPS - 1).astype(jnp.int32),
            core,
            z,
            chip,
            owner_chip,
            row,
        ]
    )

    own, other, diag, one, two = prepare_call(panels, weight)
    got = lax.ppermute(diag, "xl", swap)
    sent, rows_b = small_call(
        choose_kernel, "choose", ((BLK, width), (weight.shape[0] // 2, BLK)), flags, own, lax.ppermute(other, "k", swap)
    )
    sent, got, diag, one, two = lax.optimization_barrier((sent, got, diag, one, two))
    came = lax.all_to_all(sent, CHIPS, 0, 0, tiled=True)
    diag = jnp.where(xl == (chip & 1), diag, got)
    got = lax.ppermute(diag, "z", [(i, i ^ 1) for i in range(4)])
    diag = jnp.where((z & 1) == ((chip >> 1) & 1), diag, got)
    got = lax.ppermute(diag, "z", [(i, i ^ 2) for i in range(4)])

    last_chip, last_core, last_row = N_CHIPS - 1, 1, N_ROWS - 1

    def down(value, bit, mask):
        rows = [r for r in range(N_ROWS) if (r ^ last_row) & ~mask == 0]
        at = functools.partial(device_at, last_chip, last_core)
        return lax.ppermute(value, AXES, [(at(r), at(r ^ bit)) for r in rows])

    one = jnp.where((row & 1) != 0, one, down(one, 1, 1))
    two = jnp.where((row & 4) != 0, two, down(two, 4, 4))
    (small,) = small_call(join_kernel, "join", ((weight.shape[0] // 2 + BLK, BLK),), flags, rows_b, diag, got)
    came, one, two, small = lax.optimization_barrier((came, one, two, small))
    got_one, got_two = down(one, 2, 3), down(two, 2, 6)

    pairs = [
        (device_at(d, k, r), device_at(r, k, d)) for d in range(N_CHIPS) for k in range(2) for r in range(N_ROWS)
    ]
    turned = lax.ppermute(lax.dynamic_slice_in_dim(came, owner_chip * piece, piece, 0), AXES, pairs)
    got = lax.ppermute(small, "xh", swap)
    small = jnp.where((chip & 4) == (owner_chip & 4), small, got)
    (copies,) = small_call(copies_kernel, "copies", ((N_ROWS, piece, width),), flags, turned)
    copies, small, got_one, got_two = lax.optimization_barrier((copies, small, got_one, got_two))
    panel0 = lax.all_to_all(copies, ROWS, 0, 0, tiled=True).reshape(BLK, width)
    got = lax.ppermute(small, "y", [(i, i ^ 1) for i in range(4)])
    small = jnp.where((chip & 1) == (owner_chip & 1), small, got)
    one = jnp.where((row & 2) != 0, one, got_one)
    two = jnp.where((row & 2) != 0, two, got_two)
    small, one, two = lax.optimization_barrier((small, one, two))
    got_one, got_two = down(one, 4, 7), down(two, 1, 7)
    got = lax.ppermute(small, "y", [(i, i ^ 2) for i in range(4)])
    small = jnp.where((chip & 2) == (owner_chip & 2), small, got)
    panel0, small = lax.optimization_barrier((panel0, small))
    other = lax.ppermute(small, "k", swap)

    wide_scales = scales[None, :]
    error, rounded = first_call(flags, grid_codes, small, other, wide_scales, block_inverse[0])
    return last_call(flags, grid_codes, weight, rounded, error, panel0, (one, got_one, two, got_two), wide_scales, block_inverse[1])


def solution(mesh):
    torus = Mesh(mesh.devices.reshape(SIZES), AXES)
    return jax.shard_map(
        local,
        mesh=torus,
        in_specs=(P(ROWS, COLS), P(ROWS), P(COLS, ROWS), P(), P(), P()),
        out_specs=P(ROWS, COLS),
        check_vma=False,
    )
```

time: 99.8 us -> 92.6 us (0.928); the launches traced: 99.2 us -> 93 us
  waiting for transfers between devices: 31.6 us -> 21.7 us
  starting transfers between devices: 31.8 us -> 41.5 us
  other arithmetic: 12.5 us -> 5.38 us
  Pallas kernels: 16.9 us -> 22 us
  local copies, waits for them, and re-layouts: 5.95 us -> 2.07 us
    all_to_all x1, waiting for transfers between devices: 14.2 us -> 1.73 us  [local(): came = lax.all_to_all(sent, CHIPS, 0, 0, tiled=True)]
    ppermute x6 -> x11, starting transfers between devices: 8.82 us -> 19.6 us  [the longest x1 8.14 us: local(): lax.ppermute(lax.dynamic_slice_in_dim(came, owner_chip * piece, piece, 0)...]
    pallas_call x0 -> x4, Pallas kernels: none -> 7.17 us  [the longest x3 3.63 us: small_call(): pl.pallas_call(kernel, out_shape=tuple((jax.ShapeDtypeStruct(shape, jnp.f...]
    ppermute x6 -> x11, waiting for transfers between devices: 9.65 us -> 16.6 us  [the longest x1 10.4 us: local(): lax.ppermute(lax.dynamic_slice_in_dim(came, owner_chip * piece, piece, 0)...]
    all_to_all x2 -> x1, waiting for transfers between devices: 6.95 us -> 0.01 us  [local(): panel0 = lax.all_to_all(copies, ROWS, 0, 0, tiled=True).reshape(BLK, width)]
    all_to_all x2 -> x1, starting transfers between devices: 9.91 us -> 5.06 us  [local(): panel0 = lax.all_to_all(copies, ROWS, 0, 0, tiled=True).reshape(BLK, width)]
    select_n x6, other arithmetic: 9.17 us -> 5.36 us  [the longest x1 1.17 us: local(): two = jnp.where(row & 2 != 0, two, got_two)]
    slice x1 -> x0, other arithmetic: 2.53 us -> none  [local(): left, right = (panels[:, :width], panels[:, width:])]
  transfers between devices with their start and end apart: 13 -> 17, of which waited for: 4 -> 7; matrix products, arithmetic and copies ran while one was open for 17% -> 6% of each run, Pallas kernels for 3% -> 7%
where the time goes in v2:
time: 92.6 us; the launch traced here: 93 us
  starting transfers between devices  41.5 us (45%)
  Pallas kernels  22 us (24%)
  waiting for transfers between devices  21.7 us (23%)
  other arithmetic  5.38 us (6%)
  local copies, waits for them, and re-layouts  2.07 us (2%)
    pallas_call x1, Pallas kernels, last_call(): pl.pallas_call(last_kernel, grid=(n // rows,), out_shape=jax.ShapeDtypeSt...  11.5 us
    ppermute x1, waiting for transfers between devices, local(): lax.ppermute(lax.dynamic_slice_in_dim(came, owner_chip * piece, piece, 0)...  10.4 us
    ppermute x1, starting transfers between devices, local(): lax.ppermute(lax.dynamic_slice_in_dim(came, owner_chip * piece, piece, 0)...  8.14 us
    ppermute x6, starting transfers between devices, down(): return lax.ppermute(value, AXES, [(at(r), at(r ^ bit)) for r in rows])  7.94 us
    all_to_all x1, starting transfers between devices, local(): came = lax.all_to_all(sent, CHIPS, 0, 0, tiled=True)  6.53 us
    ppermute x1, starting transfers between devices, local(): got = lax.ppermute(diag, 'z', [(i, i ^ 2) for i in range(4)])  5.34 us
    all_to_all x1, starting transfers between devices, local(): panel0 = lax.all_to_all(copies, ROWS, 0, 0, tiled=True).reshape(BLK, width)  5.06 us
    pallas_call x3, Pallas kernels, small_call(): pl.pallas_call(kernel, out_shape=tuple((jax.ShapeDtypeStruct(shape, jnp.f...  3.63 us
  transfers between devices with their start and end apart: 17, of which 7 were waited for; matrix products, arithmetic and copies ran while one was open for 6% of the time, Pallas kernels for 7%

profile of v2, /device:TPU:29, one launch (start us, length us, event | category | flops | bytes accessed | tf_op | source)
XLA Modules:
  0.0 93.0 jit_solution(16581706079667816687)
XLA Ops:
  0.0 3.5 %halves.1 = (f32[128,2304]{1,0:T(8,128)}, f32[128,2304]{1,0:T(8,128)}, f32[128,128]{1,0:T(8,128)}, f32[128,896]{1,0:T(8,128)}, f32[128,896]{1,0:T(8,128)}) custom-call(f32[128,3584]{1,0:T(8,128)} %panel_ref.1, f32[1024,1792]{1,0:T(8,128)} %weight_hbm.1), custom_call_target="tpu_custom_call" | custom-call | tf_op jit(solution)/shard_map/halves/pallas_call | solution.py:167
  3.5 0.6 collective-permute-start
  4.2 0.9 collective-permute-start.1
  5.3 0.1 stack.55.flags
  5.3 1.5 %collective-permute-done.got_ref = f32[128,2304]{1,0:T(8,128)S(1)} collective-permute-done((f32[128,2304]{1,0:T(8,128)}, f32[128,2304]{1,0:T(8,128)S(1)}, u32[]{:S(2)}, u32[]{:S(2)}) %collective-permute-start) | collective-permute-done | bytes 1179680 | tf_op jit(solution)/shard_map/ppermute | solution.py:345
  6.8 1.3 %copy-done = f32[128,2304]{1,0:T(8,128)S(1)} copy-done((f32[128,2304]{1,0:T(8,128)S(1)}, f32[128,2304]{1,0:T(8,128)}, u32[]{:S(2)}) %copy-start) | copy-done | bytes 1179672
  8.1 1.5 %choose.1 = (f32[128,1792]{1,0:T(8,128)}, f32[512,128]{1,0:T(8,128)S(1)}) custom-call(s32[9]{0:T(128)S(1)} %stack.55.flags, f32[128,2304]{1,0:T(8,128)S(1)} %copy-done, f32[128,2304]{1,0:T(8,128)S(1)} %collective-permute-done.got_ref), custom_call_target="tpu_custom_call" | custom-call | bytes 100000 | tf_op jit(solution)/shard_map/choose/pallas_call | solution.py:151
  9.7 0.0 collective-permute-done.1
  9.7 0.7 collective-permute-start.2
  10.4 1.7 %collective-permute-start.4 = (f32[128,128]{1,0:T(8,128)S(1)}, f32[128,128]{1,0:T(8,128)S(1)}, u32[]{:S(2)}, u32[]{:S(2)}) collective-permute-start(f32[128,128]{1,0:T(8,128)S(1)} %broadcast_select_fusion.7), channel_id=1, source_target_pairs={{0,2},{2,0},{4,6},{6,4},{1,3},{3,1},{5,7},{7,5},{8,10},{10,8},{12,... | collective-permute-start | bytes 196616 | tf_op jit(solution)/shard_map/ppermute | solution.py:350
  12.1 6.5 %all-to-all-start = ((f32[8,16,1792]{2,1,0:T(8,128)}), f32[8,16,1792]{2,1,0:T(8,128)S(1)}, u32[]{:S(2)}, u32[]{:S(2)}) async-start(f32[8,16,1792]{2,1,0:T(8,128)} %bitcast.11), calls=%async_computation | async-start | bytes 1835008 | tf_op jit(solution)/shard_map/all_to_all | solution.py:348
  18.6 1.4 %collective-permute-start.3 = (f32[128,896]{1,0:T(8,128)S(1)}, f32[128,896]{1,0:T(8,128)}, u32[]{:S(2)}, u32[]{:S(2)}) collective-permute-start(f32[128,896]{1,0:T(8,128)S(1)} %copy-done.4), channel_id=1, source_target_pairs={{123,127},{127,123}} | collective-permute-start | bytes 1376264 | tf_op jit(solution)/shard_map/ppermute | solution.py:359
  20.1 0.0 collective-permute-done.4
  20.1 5.3 %collective-permute-start.5 = (f32[128,128]{1,0:T(8,128)S(1)}, f32[128,128]{1,0:T(8,128)S(1)}, u32[]{:S(2)}, u32[]{:S(2)}) collective-permute-start(f32[128,128]{1,0:T(8,128)S(1)} %broadcast_select_fusion.8.diag_ref), channel_id=1, source_target_pairs={{0,4},{2,6},{4,0},{6,2},{1,5},{3,7},{5,1},{7,3},{8,12},{10,14},{12... | collective-permute-start | bytes 196616 | tf_op jit(solution)/shard_map/ppermute | solution.py:352
  25.4 2.1 %collective-permute-done.5.got_ref = f32[128,128]{1,0:T(8,128)S(1)} collective-permute-done((f32[128,128]{1,0:T(8,128)S(1)}, f32[128,128]{1,0:T(8,128)S(1)}, u32[]{:S(2)}, u32[]{:S(2)}) %collective-permute-start.5) | collective-permute-done | bytes 65568 | tf_op jit(solution)/shard_map/ppermute | solution.py:352
  27.5 0.6 join.1
  28.1 0.0 collective-permute-done.2
  28.1 0.1 broadcast_select_fusion.3
  28.2 0.0 collective-permute-done.3
  28.2 1.1 %broadcast_select_fusion.2 = f32[128,896]{1,0:T(8,128)S(1)} fusion(f32[128,896]{1,0:T(8,128)S(1)} %copy-done.4, f32[128,896]{1,0:T(8,128)} %collective-permute-done.3, pred[]{:T(512)S(6)} %ne.35), kind=kLoop, calls=%fused_computation.2 | loop fusion | flops 114688 | bytes 1376257 | tf_op jit(solution)/shard_map/jit(_where)/select_n | solution.py:362
  29.3 1.7 %all-to-all-done = f32[8,16,1792]{2,1,0:T(8,128)S(1)} async-done(((f32[8,16,1792]{2,1,0:T(8,128)}), f32[8,16,1792]{2,1,0:T(8,128)S(1)}, u32[]{:S(2)}, u32[]{:S(2)}) %all-to-all-start) | async-done | bytes 917536 | tf_op jit(solution)/shard_map/all_to_all | solution.py:348
  31.0 0.4 collective-permute-start.7
  31.4 0.7 collective-permute-start.8
  32.1 0.7 collective-permute-start.9
  32.9 8.1 %collective-permute-start.6 = (f32[16,1792]{1,0:T(8,128)S(1)}, f32[16,1792]{1,0:T(8,128)S(1)}, u32[]{:S(2)}, u32[]{:S(2)}) collective-permute-start(f32[16,1792]{1,0:T(8,128)S(1)} %constant_dynamic-slice_fusion), channel_id=1, source_target_pairs={{0,0},{1,16},{2,32},{3,48},{4,64},{5,80},{6,96},{7,112},{8,8},{9,2... | collective-permute-start | bytes 344072 | tf_op jit(solution)/shard_map/ppermute | solution.py:370
  41.0 10.4 %collective-permute-done.6.piece_ref = f32[16,1792]{1,0:T(8,128)S(1)} collective-permute-done((f32[16,1792]{1,0:T(8,128)S(1)}, f32[16,1792]{1,0:T(8,128)S(1)}, u32[]{:S(2)}, u32[]{:S(2)}) %collective-permute-start.6) | collective-permute-done | bytes 114720 | tf_op jit(solution)/shard_map/ppermute | solution.py:370
  51.4 1.5 %copies.1 = f32[8,16,1792]{2,1,0:T(8,128)} custom-call(s32[9]{0:T(128)S(1)} %stack.55.flags, f32[16,1792]{1,0:T(8,128)S(1)} %collective-permute-done.6.piece_ref), custom_call_target="tpu_custom_call" | custom-call | bytes 100000 | tf_op jit(solution)/shard_map/copies/pallas_call | solution.py:151
  53.0 1.0 %broadcast_select_fusion.6 = f32[640,128]{1,0:T(8,128)S(1)} fusion(f32[640,128]{1,0:T(8,128)S(1)} %join.1, f32[640,128]{1,0:T(8,128)} %collective-permute-done.7, pred[]{:T(512)S(6)} %eq.31), kind=kLoop, calls=%fused_computation.6 | loop fusion | flops 81920 | bytes 983041 | tf_op jit(solution)/shard_map/jit(_where)/select_n | solution.py:372
  54.0 0.0 collective-permute-done.8
  54.0 0.0 collective-permute-done.9
  54.0 0.1 collective-permute-start.10
  54.1 0.7 copy-done.6
  54.8 5.1 %all-to-all-start.1 = ((f32[8,16,1792]{2,1,0:T(8,128)}), f32[8,16,1792]{2,1,0:T(8,128)S(1)}, u32[]{:S(2)}, u32[]{:S(2)}) async-start(f32[8,16,1792]{2,1,0:T(8,128)} %copies.1), calls=%async_computation.1 | async-start | bytes 1835008 | tf_op jit(solution)/shard_map/all_to_all | solution.py:375
  59.8 0.0 copy-start.2
  59.8 1.2 %broadcast_select_fusion = (f32[128,896]{1,0:T(8,128)S(1)}, f32[128,896]{1,0:T(8,128)S(1)}) fusion(f32[128,896]{1,0:T(8,128)S(1)} %broadcast_select_fusion.2, f32[128,896]{1,0:T(8,128)} %copy-done.6, pred[]{:T(512)S(6)} %ne.36, f32[128,896]{1,0:T(8,128)S(1)} %broadcast_select_fusion.3, f32[128,896]{1,0:T(8,128)S(1)} %collective-permute-done.8), kind=kLoop, calls=%fused_computation | loop fusion | flops 229376 | bytes 2752513 | tf_op jit(solution)/shard_map/jit(_where)/select_n | solution.py:379
  61.0 2.0 %collective-permute-done.10 = f32[640,128]{1,0:T(8,128)} collective-permute-done((f32[640,128]{1,0:T(8,128)S(1)}, f32[640,128]{1,0:T(8,128)}, u32[]{:S(2)}, u32[]{:S(2)}) %collective-permute-start.10) | collective-permute-done | bytes 327712 | tf_op jit(solution)/shard_map/ppermute | solution.py:376
  63.0 1.0 %broadcast_select_fusion.4 = f32[640,128]{1,0:T(8,128)S(1)} fusion(f32[640,128]{1,0:T(8,128)S(1)} %broadcast_select_fusion.6, f32[640,128]{1,0:T(8,128)} %collective-permute-done.10, pred[]{:T(512)S(6)} %eq.33), kind=kLoop, calls=%fused_computation.4 | loop fusion | flops 81920 | bytes 983041 | tf_op jit(solution)/shard_map/jit(_where)/select_n | solution.py:377
  64.0 2.4 %collective-permute-start.11 = (f32[640,128]{1,0:T(8,128)S(1)}, f32[640,128]{1,0:T(8,128)}, u32[]{:S(2)}, u32[]{:S(2)}) collective-permute-start(f32[640,128]{1,0:T(8,128)S(1)} %broadcast_select_fusion.4), channel_id=1, source_target_pairs={{0,32},{16,48},{32,0},{48,16},{1,33},{17,49},{33,1},{49,17},{2,34}... | collective-permute-start | bytes 983048 | tf_op jit(solution)/shard_map/ppermute | solution.py:382
  66.3 1.9 %collective-permute-start.13 = (f32[128,896]{1,0:T(8,128)S(1)}, f32[128,896]{1,0:T(8,128)S(1)}, u32[]{:S(2)}, u32[]{:S(2)}) collective-permute-start(f32[128,896]{1,0:T(8,128)S(1)} %get-tuple-element.57.one_hbm), channel_id=1, source_target_pairs={{120,124},{121,125},{122,126},{123,127},{124,120},{125,121},{126,1... | collective-permute-start | bytes 1376264 | tf_op jit(solution)/shard_map/ppermute | solution.py:359
  68.3 2.6 %collective-permute-start.14 = (f32[128,896]{1,0:T(8,128)S(1)}, f32[128,896]{1,0:T(8,128)S(1)}, u32[]{:S(2)}, u32[]{:S(2)}) collective-permute-start(f32[128,896]{1,0:T(8,128)S(1)} %get-tuple-element.58.two_hbm), channel_id=1, source_target_pairs={{120,121},{121,120},{122,123},{123,122},{124,125},{125,124},{126,1... | collective-permute-start | bytes 1376264 | tf_op jit(solution)/shard_map/ppermute | solution.py:359
  70.8 2.7 %collective-permute-done.11 = f32[640,128]{1,0:T(8,128)} collective-permute-done((f32[640,128]{1,0:T(8,128)S(1)}, f32[640,128]{1,0:T(8,128)}, u32[]{:S(2)}, u32[]{:S(2)}) %collective-permute-start.11) | collective-permute-done | bytes 327712 | tf_op jit(solution)/shard_map/ppermute | solution.py:382
  73.5 1.0 %broadcast_select_fusion.5.small_ref = f32[640,128]{1,0:T(8,128)S(1)} fusion(f32[640,128]{1,0:T(8,128)S(1)} %broadcast_select_fusion.4, f32[640,128]{1,0:T(8,128)} %collective-permute-done.11, pred[]{:T(512)S(6)} %eq.32), kind=kLoop, calls=%fused_computation.5 | loop fusion | flops 81920 | bytes 983041 | tf_op jit(solution)/shard_map/jit(_where)/select_n | solution.py:383
  74.6 0.0 all-to-all-done.1
  74.6 2.3 %collective-permute-start.12 = (f32[640,128]{1,0:T(8,128)S(1)}, f32[640,128]{1,0:T(8,128)S(1)}, u32[]{:S(2)}, u32[]{:S(2)}) collective-permute-start(f32[640,128]{1,0:T(8,128)S(1)} %broadcast_select_fusion.5.small_ref), channel_id=1, source_target_pairs={{0,8},{8,0},{1,9},{9,1},{2,10},{10,2},{3,11},{11,3},{4,12},{12,4},... | collective-permute-start | bytes 983048 | tf_op jit(solution)/shard_map/ppermute | solution.py:385
  76.9 1.2 %collective-permute-done.12.other_ref = f32[640,128]{1,0:T(8,128)S(1)} collective-permute-done((f32[640,128]{1,0:T(8,128)S(1)}, f32[640,128]{1,0:T(8,128)S(1)}, u32[]{:S(2)}, u32[]{:S(2)}) %collective-permute-start.12) | collective-permute-done | bytes 327712 | tf_op jit(solution)/shard_map/ppermute | solution.py:385
  78.2 3.3 %round_first.1 = (bf16[1024,256]{1,0:T(8,128)(2,1)S(1)}, f32[1024,128]{1,0:T(8,128)S(1)}) custom-call(s32[9]{0:T(128)S(1)} %stack.55.flags, s32[16]{0:T(128)S(1)} %copy-done.2, f32[640,128]{1,0:T(8,128)S(1)} %broadcast_select_fusion.5.small_ref, f32[640,128]{1,0:T(8,128)S(1)} %collective-permute-done.12.other_ref, f32[1,1024]{1,0:T(1,128)S(1)} %bitcast.20, ...), custom_call_target="tpu_custom_call" | custom-call | bytes 100000 | tf_op jit(solution)/shard_map/round_first/pallas_call | solution.py:272
  81.4 0.0 collective-permute-done.13.got_one_hbm
  81.5 11.5 %update_all.1 = f32[1024,1792]{1,0:T(8,128)} custom-call(s32[9]{0:T(128)S(1)} %stack.55.flags, s32[16]{0:T(128)S(1)} %copy-done.2, f32[1024,1792]{1,0:T(8,128)} %weight_hbm.1, f32[1024,128]{1,0:T(8,128)S(1)} %get-tuple-element.54.rounded_ref, bf16[1024,256]{1,0:T(8,128)(2,1)S(1)} %get-tuple-element.55.error_ref, f32[128,1792]{1,0:T(8,128)} %bitcast.22, ...), custom_call_target="tpu_custom_call" | custom-call | flops 2000000000 | bytes 16000000 | tf_op jit(solution)/shard_map/update_all/pallas_call | solution.py:288
  (23 shorter events, 0.1 us)
Async XLA Ops:
  0.0 5.1 %copy-start.9 = (s32[2]{0:T(128)S(1)}, s32[2]{0:T(128)}, u32[]{:S(2)}) copy-start(s32[2]{0:T(128)} %param.11) | copy-start | bytes 28
  3.5 6.8 %copy-start.8 = (f32[128,128]{1,0:T(8,128)S(1)}, f32[128,128]{1,0:T(8,128)}, u32[]{:S(2)}) copy-start(f32[128,128]{1,0:T(8,128)} %get-tuple-element.42) | copy-start | bytes 196612
  3.5 3.3 %collective-permute-start = (f32[128,2304]{1,0:T(8,128)}, f32[128,2304]{1,0:T(8,128)S(1)}, u32[]{:S(2)}, u32[]{:S(2)}) collective-permute-start(f32[128,2304]{1,0:T(8,128)} %get-tuple-element.33), channel_id=1, source_target_pairs={{0,8},{8,0},{1,9},{9,1},{2,10},{10,2},{3,11},{11,3},{4,12},{12,4},... | collective-permute-start | bytes 3538952 | tf_op jit(solution)/shard_map/ppermute | solution.py:345
  4.2 5.5 %collective-permute-start.1 = (f32[128,128]{1,0:T(8,128)}, f32[128,128]{1,0:T(8,128)S(1)}, u32[]{:S(2)}, u32[]{:S(2)}) collective-permute-start(f32[128,128]{1,0:T(8,128)} %get-tuple-element.42), channel_id=1, source_target_pairs={{0,1},{1,0},{2,3},{3,2},{4,5},{5,4},{6,7},{7,6},{8,9},{9,8},{10,11... | collective-permute-start | bytes 196616 | tf_op jit(solution)/shard_map/ppermute | solution.py:343
  6.8 1.3 %copy-start = (f32[128,2304]{1,0:T(8,128)S(1)}, f32[128,2304]{1,0:T(8,128)}, u32[]{:S(2)}) copy-start(f32[128,2304]{1,0:T(8,128)} %get-tuple-element.32.own_ref) | copy-start | bytes 3538948
  8.1 1.6 %copy-start.5 = (f32[128,896]{1,0:T(8,128)S(1)}, f32[128,896]{1,0:T(8,128)}, u32[]{:S(2)}) copy-start(f32[128,896]{1,0:T(8,128)} %get-tuple-element.39) | copy-start | bytes 1376260
  8.1 10.5 %copy-start.4 = (f32[128,896]{1,0:T(8,128)S(1)}, f32[128,896]{1,0:T(8,128)}, u32[]{:S(2)}) copy-start(f32[128,896]{1,0:T(8,128)} %get-tuple-element.40) | copy-start | bytes 1376260
  9.7 18.4 %collective-permute-start.2 = (f32[128,896]{1,0:T(8,128)S(1)}, f32[128,896]{1,0:T(8,128)S(1)}, u32[]{:S(2)}, u32[]{:S(2)}) collective-permute-start(f32[128,896]{1,0:T(8,128)S(1)} %copy-done.5), channel_id=1, source_target_pairs={{126,127},{127,126}} | collective-permute-start | bytes 1376264 | tf_op jit(solution)/shard_map/ppermute | solution.py:359
  10.4 9.7 %collective-permute-start.4 = (f32[128,128]{1,0:T(8,128)S(1)}, f32[128,128]{1,0:T(8,128)S(1)}, u32[]{:S(2)}, u32[]{:S(2)}) collective-permute-start(f32[128,128]{1,0:T(8,128)S(1)} %broadcast_select_fusion.7), channel_id=1, source_target_pairs={{0,2},{2,0},{4,6},{6,4},{1,3},{3,1},{5,7},{7,5},{8,10},{10,8},{12,... | collective-permute-start | bytes 196616 | tf_op jit(solution)/shard_map/ppermute | solution.py:350
  12.1 18.9 %all-to-all-start = ((f32[8,16,1792]{2,1,0:T(8,128)}), f32[8,16,1792]{2,1,0:T(8,128)S(1)}, u32[]{:S(2)}, u32[]{:S(2)}) async-start(f32[8,16,1792]{2,1,0:T(8,128)} %bitcast.11), calls=%async_computation | async-start | bytes 1835008 | tf_op jit(solution)/shard_map/all_to_all | solution.py:348
  18.6 9.5 %collective-permute-start.3 = (f32[128,896]{1,0:T(8,128)S(1)}, f32[128,896]{1,0:T(8,128)}, u32[]{:S(2)}, u32[]{:S(2)}) collective-permute-start(f32[128,896]{1,0:T(8,128)S(1)} %copy-done.4), channel_id=1, source_target_pairs={{123,127},{127,123}} | collective-permute-start | bytes 1376264 | tf_op jit(solution)/shard_map/ppermute | solution.py:359
  20.1 7.4 %collective-permute-start.5 = (f32[128,128]{1,0:T(8,128)S(1)}, f32[128,128]{1,0:T(8,128)S(1)}, u32[]{:S(2)}, u32[]{:S(2)}) collective-permute-start(f32[128,128]{1,0:T(8,128)S(1)} %broadcast_select_fusion.8.diag_ref), channel_id=1, source_target_pairs={{0,4},{2,6},{4,0},{6,2},{1,5},{3,7},{5,1},{7,3},{8,12},{10,14},{12... | collective-permute-start | bytes 196616 | tf_op jit(solution)/shard_map/ppermute | solution.py:352
  31.0 21.9 %collective-permute-start.7 = (f32[640,128]{1,0:T(8,128)S(1)}, f32[640,128]{1,0:T(8,128)}, u32[]{:S(2)}, u32[]{:S(2)}) collective-permute-start(f32[640,128]{1,0:T(8,128)S(1)} %join.1), channel_id=1, source_target_pairs={{0,64},{64,0},{1,65},{65,1},{2,66},{66,2},{3,67},{67,3},{4,68},{68... | collective-permute-start | bytes 983048 | tf_op jit(solution)/shard_map/ppermute | solution.py:371
  31.4 22.5 %collective-permute-start.8 = (f32[128,896]{1,0:T(8,128)S(1)}, f32[128,896]{1,0:T(8,128)S(1)}, u32[]{:S(2)}, u32[]{:S(2)}) collective-permute-start(f32[128,896]{1,0:T(8,128)S(1)} %broadcast_select_fusion.3), channel_id=1, source_target_pairs={{124,126},{125,127},{126,124},{127,125}} | collective-permute-start | bytes 1376264 | tf_op jit(solution)/shard_map/ppermute | solution.py:359
  32.1 21.9 %collective-permute-start.9 = (f32[128,896]{1,0:T(8,128)S(1)}, f32[128,896]{1,0:T(8,128)S(1)}, u32[]{:S(2)}, u32[]{:S(2)}) collective-permute-start(f32[128,896]{1,0:T(8,128)S(1)} %broadcast_select_fusion.2), channel_id=1, source_target_pairs={{121,123},{123,121},{125,127},{127,125}} | collective-permute-start | bytes 1376264 | tf_op jit(solution)/shard_map/ppermute | solution.py:359
  32.9 18.6 %collective-permute-start.6 = (f32[16,1792]{1,0:T(8,128)S(1)}, f32[16,1792]{1,0:T(8,128)S(1)}, u32[]{:S(2)}, u32[]{:S(2)}) collective-permute-start(f32[16,1792]{1,0:T(8,128)S(1)} %constant_dynamic-slice_fusion), channel_id=1, source_target_pairs={{0,0},{1,16},{2,32},{3,48},{4,64},{5,80},{6,96},{7,112},{8,8},{9,2... | collective-permute-start | bytes 344072 | tf_op jit(solution)/shard_map/ppermute | solution.py:370
  54.0 0.8 copy-start.6
  54.0 9.0 %collective-permute-start.10 = (f32[640,128]{1,0:T(8,128)S(1)}, f32[640,128]{1,0:T(8,128)}, u32[]{:S(2)}, u32[]{:S(2)}) collective-permute-start(f32[640,128]{1,0:T(8,128)S(1)} %broadcast_select_fusion.6), channel_id=1, source_target_pairs={{0,16},{16,0},{32,48},{48,32},{1,17},{17,1},{33,49},{49,33},{2,18}... | collective-permute-start | bytes 983048 | tf_op jit(solution)/shard_map/ppermute | solution.py:376
  54.8 19.8 %all-to-all-start.1 = ((f32[8,16,1792]{2,1,0:T(8,128)}), f32[8,16,1792]{2,1,0:T(8,128)S(1)}, u32[]{:S(2)}, u32[]{:S(2)}) async-start(f32[8,16,1792]{2,1,0:T(8,128)} %copies.1), calls=%async_computation.1 | async-start | bytes 1835008 | tf_op jit(solution)/shard_map/all_to_all | solution.py:375
  59.8 18.4 %copy-start.1 = (f32[1024]{0:T(1024)S(1)}, f32[1024]{0:T(1024)}, u32[]{:S(2)}) copy-start(f32[1024]{0:T(1024)} %param.7) | copy-start | bytes 12292
  59.8 18.4 %copy-start.2 = (s32[16]{0:T(128)S(1)}, s32[16]{0:T(128)}, u32[]{:S(2)}) copy-start(s32[16]{0:T(128)} %codes.3) | copy-start | bytes 196
  61.0 15.9 %copy-start.7 = (f32[2,128,128]{2,1,0:T(8,128)S(1)}, f32[2,128,128]{2,1,0:T(8,128)}, u32[]{:S(2)}) copy-start(f32[2,128,128]{2,1,0:T(8,128)} %param.9) | copy-start | bytes 393220
  64.0 9.6 %collective-permute-start.11 = (f32[640,128]{1,0:T(8,128)S(1)}, f32[640,128]{1,0:T(8,128)}, u32[]{:S(2)}, u32[]{:S(2)}) collective-permute-start(f32[640,128]{1,0:T(8,128)S(1)} %broadcast_select_fusion.4), channel_id=1, source_target_pairs={{0,32},{16,48},{32,0},{48,16},{1,33},{17,49},{33,1},{49,17},{2,34}... | collective-permute-start | bytes 983048 | tf_op jit(solution)/shard_map/ppermute | solution.py:382
  66.3 15.1 %collective-permute-start.13 = (f32[128,896]{1,0:T(8,128)S(1)}, f32[128,896]{1,0:T(8,128)S(1)}, u32[]{:S(2)}, u32[]{:S(2)}) collective-permute-start(f32[128,896]{1,0:T(8,128)S(1)} %get-tuple-element.57.one_hbm), channel_id=1, source_target_pairs={{120,124},{121,125},{122,126},{123,127},{124,120},{125,121},{126,1... | collective-permute-start | bytes 1376264 | tf_op jit(solution)/shard_map/ppermute | solution.py:359
  68.3 13.2 %collective-permute-start.14 = (f32[128,896]{1,0:T(8,128)S(1)}, f32[128,896]{1,0:T(8,128)S(1)}, u32[]{:S(2)}, u32[]{:S(2)}) collective-permute-start(f32[128,896]{1,0:T(8,128)S(1)} %get-tuple-element.58.two_hbm), channel_id=1, source_target_pairs={{120,121},{121,120},{122,123},{123,122},{124,125},{125,124},{126,1... | collective-permute-start | bytes 1376264 | tf_op jit(solution)/shard_map/ppermute | solution.py:359
  74.6 6.9 %copy-start.3 = (f32[8,16,1792]{2,1,0:T(8,128)}, f32[8,16,1792]{2,1,0:T(8,128)S(1)}, u32[]{:S(2)}) copy-start(f32[8,16,1792]{2,1,0:T(8,128)S(1)} %all-to-all-done.1) | copy-start | bytes 2752516
  74.6 3.6 %collective-permute-start.12 = (f32[640,128]{1,0:T(8,128)S(1)}, f32[640,128]{1,0:T(8,128)S(1)}, u32[]{:S(2)}, u32[]{:S(2)}) collective-permute-start(f32[640,128]{1,0:T(8,128)S(1)} %broadcast_select_fusion.5.small_ref), channel_id=1, source_target_pairs={{0,8},{8,0},{1,9},{9,1},{2,10},{10,2},{3,11},{11,3},{4,12},{12,4},... | collective-permute-start | bytes 983048 | tf_op jit(solution)/shard_map/ppermute | solution.py:385

commit v3 on v2

--- a/solution.py
+++ b/solution.py
@@ -177,7 +177,7 @@
 
 def last_kernel(
     flags, codes, weight_hbm, rounded_ref, error_ref, panel_ref, one_hbm, got_one_hbm, two_hbm, got_two_hbm, scales_ref, inverse_ref,
-    out_ref, m0_ref, m0_low_ref, m1_ref, m1_low_ref, error1_ref, rounded1_ref, weight_ref, arrived, panel1_ref, block_ref, down_done,
+    out_ref, m_ref, error1_ref, rounded1_ref, weight_ref, arrived, panel1_ref, block_ref, down_done,
 ):
     step = pl.program_id(0)
     after, owner, last = flags[1], flags[2], flags[3]
@@ -207,28 +207,29 @@
         for i in range(weight_hbm.shape[0] // rows):
             read(i).start()
 
-    def stage(source, masked, pair_ref, low_ref):
+    span0 = slice(0, 3 * BLK)
+
+    def stage(source, masked, base):
         value = source[...]
         ids = lax.broadcasted_iota(jnp.int32, value.shape, 1)
         value = jnp.where(jnp.logical_and(masked == 1, ids < BLK), 0.0, value)
         high, low = split(value)
-        pair_ref[:BLK, :] = high
-        pair_ref[BLK:, :] = high
-        low_ref[...] = low
-
-    def product(error, pair, low):
-        return fast_dot(error, pair) + fast_dot(error[:, :BLK], low)
+        for i, part in enumerate((high, high, low)):
+            m_ref[base + i * BLK : base + (i + 1) * BLK, :] = part
+
+    def three(error):
+        return [error, error[:, :BLK]]
 
     @pl.when(jnp.logical_and(step == 0, after == 1))
     def _():
-        stage(panel_ref, owner, m0_ref, m0_low_ref)
+        stage(panel_ref, owner, 0)
 
     @pl.when(jnp.logical_and(step == 0, last == 1))
     def _():
         pltpu.make_async_copy(one_hbm, left, down_done.at[0]).wait()
         pltpu.make_async_copy(two_hbm, right, down_done.at[2]).wait()
         block_read.wait()
-        block = block_ref[...] - product(error_ref[...], m0_ref[:, :BLK], m0_low_ref[:, :BLK])
+        block = block_ref[...] - fast_dot(jnp.concatenate(three(error_ref[...]), 1), m_ref[span0, :BLK])
         tiles = [block[i * BLK : (i + 1) * BLK] for i in range(block.shape[0] // BLK)]
         parts = transposed_parts(tiles)
         steps = [scales_ref[:, i * LANES : (i + 1) * LANES] for i in range(len(parts))]
@@ -239,7 +240,7 @@
             high, low = split(errors[i].T)
             error1_ref[span, :BLK] = high
             error1_ref[span, BLK:] = low
-        stage(panel1_ref, last, m1_ref, m1_low_ref)
+        stage(panel1_ref, last, 3 * BLK)
 
     here = pl.ds(pl.multiple_of(step * rows, rows), rows)
     read(step).wait()
@@ -250,15 +251,13 @@
 
     @pl.when(jnp.logical_and(after == 1, last == 0))
     def _():
-        out_ref[...] = weight_ref[here, :] - product(error_ref[here, :], m0_ref[...], m0_low_ref[...])
+        error = jnp.concatenate(three(error_ref[here, :]), 1)
+        out_ref[...] = weight_ref[here, :] - fast_dot(error, m_ref[span0, :])
 
     @pl.when(last == 1)
     def _():
-        out_ref[...] = (
-            weight_ref[here, :]
-            - product(error_ref[here, :], m0_ref[...], m0_low_ref[...])
-            - product(error1_ref[here, :], m1_ref[...], m1_low_ref[...])
-        )
+        error = jnp.concatenate(three(error_ref[here, :]) + three(error1_ref[here, :]), 1)
+        out_ref[...] = weight_ref[here, :] - fast_dot(error, m_ref[...])
         out_ref[:, :BLK] = rounded1_ref[here, :]
 
     @pl.when(owner == 1)
@@ -292,10 +291,7 @@
         in_specs=[smem, smem, hbm] + [vmem] * 3 + [hbm] * 4 + [vmem] * 2,
         out_specs=tall,
         scratch_shapes=[
-            pltpu.VMEM((2 * BLK, width), jnp.bfloat16),
-            pltpu.VMEM((BLK, width), jnp.bfloat16),
-            pltpu.VMEM((2 * BLK, width), jnp.bfloat16),
-            pltpu.VMEM((BLK, width), jnp.bfloat16),
+            pltpu.VMEM((6 * BLK, width), jnp.bfloat16),
             pltpu.VMEM((n, 2 * BLK), jnp.bfloat16),
             pltpu.VMEM((n, BLK), jnp.float32),
             pltpu.VMEM((n, width), jnp.float32),

time: 92.6 us -> 91.4 us (0.987); the launches traced: 93 us -> 90.4 us
  other arithmetic: 5.38 us -> 3.44 us
    select_n x1, other arithmetic: 1.01 us -> 0.04 us  [local(): small = jnp.where(chip & 4 == owner_chip & 4, small, got)]
    select_n x1, other arithmetic: 1.02 us -> 0.05 us  [local(): small = jnp.where(chip & 2 == owner_chip & 2, small, got)]
    all_to_all x1, starting transfers between devices: 5.06 us -> 6.03 us  [local(): panel0 = lax.all_to_all(copies, ROWS, 0, 0, tiled=True).reshape(BLK, width)]
    ppermute x1, waiting for transfers between devices: 1.95 us -> 0.98 us  [local(): got = lax.ppermute(small, 'y', [(i, i ^ 1) for i in range(4)])]
  transfers between devices with their start and end apart: 17 -> 17, of which waited for: 7 -> 8; matrix products, arithmetic and copies ran while one was open for 6% -> 4% of each run, Pallas kernels for 7% -> 8%
where the time goes in v3:
time: 91.4 us; the launch traced here: 90.4 us
  starting transfers between devices  42 us (46%)
  Pallas kernels  21.3 us (23%)
  waiting for transfers between devices  21.2 us (23%)
  other arithmetic  3.44 us (4%)
  local copies, waits for them, and re-layouts  2.07 us (2%)
    pallas_call x1, Pallas kernels, last_call(): pl.pallas_call(last_kernel, grid=(n // rows,), out_shape=jax.ShapeDtypeSt...  10.8 us
    ppermute x1, waiting for transfers between devices, local(): lax.ppermute(lax.dynamic_slice_in_dim(came, owner_chip * piece, piece, 0)...  10.4 us
    ppermute x6, starting transfers between devices, down(): return lax.ppermute(value, AXES, [(at(r), at(r ^ bit)) for r in rows])  8.27 us
    ppermute x1, starting transfers between devices, local(): lax.ppermute(lax.dynamic_slice_in_dim(came, owner_chip * piece, piece, 0)...  8.14 us
    all_to_all x1, starting transfers between devices, local(): came = lax.all_to_all(sent, CHIPS, 0, 0, tiled=True)  6.53 us
    all_to_all x1, starting transfers between devices, local(): panel0 = lax.all_to_all(copies, ROWS, 0, 0, tiled=True).reshape(BLK, width)  6.03 us
    ppermute x1, starting transfers between devices, local(): got = lax.ppermute(diag, 'z', [(i, i ^ 2) for i in range(4)])  5.34 us
    pallas_call x3, Pallas kernels, small_call(): pl.pallas_call(kernel, out_shape=tuple((jax.ShapeDtypeStruct(shape, jnp.f...  3.63 us
  transfers between devices with their start and end apart: 17, of which 8 were waited for; matrix products, arithmetic and copies ran while one was open for 4% of the time, Pallas kernels for 8%

profile of v3, /device:TPU:29, one launch (start us, length us, event | category | flops | bytes accessed | tf_op | source)
XLA Modules:
  0.0 90.4 jit_solution(11618986649595216723)
XLA Ops:
  0.0 3.5 %halves.1 = (f32[128,2304]{1,0:T(8,128)}, f32[128,2304]{1,0:T(8,128)}, f32[128,128]{1,0:T(8,128)}, f32[128,896]{1,0:T(8,128)}, f32[128,896]{1,0:T(8,128)}) custom-call(f32[128,3584]{1,0:T(8,128)} %panel_ref.1, f32[1024,1792]{1,0:T(8,128)} %weight_hbm.1), custom_call_target="tpu_custom_call" | custom-call | tf_op jit(solution)/shard_map/halves/pallas_call | solution.py:167
  3.5 0.6 collective-permute-start
  4.2 0.9 %collective-permute-start.1 = (f32[128,128]{1,0:T(8,128)}, f32[128,128]{1,0:T(8,128)S(1)}, u32[]{:S(2)}, u32[]{:S(2)}) collective-permute-start(f32[128,128]{1,0:T(8,128)} %get-tuple-element.42), channel_id=1, source_target_pairs={{0,1},{1,0},{2,3},{3,2},{4,5},{5,4},{6,7},{7,6},{8,9},{9,8},{10,11... | collective-permute-start | bytes 196616 | tf_op jit(solution)/shard_map/ppermute | solution.py:339
  5.3 0.1 stack.55.flags
  5.3 1.5 %collective-permute-done.got_ref = f32[128,2304]{1,0:T(8,128)S(1)} collective-permute-done((f32[128,2304]{1,0:T(8,128)}, f32[128,2304]{1,0:T(8,128)S(1)}, u32[]{:S(2)}, u32[]{:S(2)}) %collective-permute-start) | collective-permute-done | bytes 1179680 | tf_op jit(solution)/shard_map/ppermute | solution.py:341
  6.8 1.3 %copy-done = f32[128,2304]{1,0:T(8,128)S(1)} copy-done((f32[128,2304]{1,0:T(8,128)S(1)}, f32[128,2304]{1,0:T(8,128)}, u32[]{:S(2)}) %copy-start) | copy-done | bytes 1179672
  8.1 1.5 %choose.1 = (f32[128,1792]{1,0:T(8,128)}, f32[512,128]{1,0:T(8,128)S(1)}) custom-call(s32[9]{0:T(128)S(1)} %stack.55.flags, f32[128,2304]{1,0:T(8,128)S(1)} %copy-done, f32[128,2304]{1,0:T(8,128)S(1)} %collective-permute-done.got_ref), custom_call_target="tpu_custom_call" | custom-call | bytes 100000 | tf_op jit(solution)/shard_map/choose/pallas_call | solution.py:151
  9.7 0.0 collective-permute-done.1
  9.7 0.7 collective-permute-start.2
  10.4 1.7 %collective-permute-start.4 = (f32[128,128]{1,0:T(8,128)S(1)}, f32[128,128]{1,0:T(8,128)S(1)}, u32[]{:S(2)}, u32[]{:S(2)}) collective-permute-start(f32[128,128]{1,0:T(8,128)S(1)} %broadcast_select_fusion.7), channel_id=1, source_target_pairs={{0,2},{2,0},{4,6},{6,4},{1,3},{3,1},{5,7},{7,5},{8,10},{10,8},{12,... | collective-permute-start | bytes 196616 | tf_op jit(solution)/shard_map/ppermute | solution.py:346
  12.1 6.5 %all-to-all-start = ((f32[8,16,1792]{2,1,0:T(8,128)}), f32[8,16,1792]{2,1,0:T(8,128)S(1)}, u32[]{:S(2)}, u32[]{:S(2)}) async-start(f32[8,16,1792]{2,1,0:T(8,128)} %bitcast.11), calls=%async_computation | async-start | bytes 1835008 | tf_op jit(solution)/shard_map/all_to_all | solution.py:344
  18.6 1.4 %collective-permute-start.3 = (f32[128,896]{1,0:T(8,128)S(1)}, f32[128,896]{1,0:T(8,128)}, u32[]{:S(2)}, u32[]{:S(2)}) collective-permute-start(f32[128,896]{1,0:T(8,128)S(1)} %copy-done.4), channel_id=1, source_target_pairs={{123,127},{127,123}} | collective-permute-start | bytes 1376264 | tf_op jit(solution)/shard_map/ppermute | solution.py:355
  20.1 0.0 collective-permute-done.4
  20.1 5.3 %collective-permute-start.5 = (f32[128,128]{1,0:T(8,128)S(1)}, f32[128,128]{1,0:T(8,128)S(1)}, u32[]{:S(2)}, u32[]{:S(2)}) collective-permute-start(f32[128,128]{1,0:T(8,128)S(1)} %broadcast_select_fusion.8.diag_ref), channel_id=1, source_target_pairs={{0,4},{2,6},{4,0},{6,2},{1,5},{3,7},{5,1},{7,3},{8,12},{10,14},{12... | collective-permute-start | bytes 196616 | tf_op jit(solution)/shard_map/ppermute | solution.py:348
  25.4 2.1 %collective-permute-done.5.got_ref = f32[128,128]{1,0:T(8,128)S(1)} collective-permute-done((f32[128,128]{1,0:T(8,128)S(1)}, f32[128,128]{1,0:T(8,128)S(1)}, u32[]{:S(2)}, u32[]{:S(2)}) %collective-permute-start.5) | collective-permute-done | bytes 65568 | tf_op jit(solution)/shard_map/ppermute | solution.py:348
  27.5 0.6 join.1
  28.1 0.0 collective-permute-done.2
  28.1 0.1 broadcast_select_fusion.3
  28.2 0.0 collective-permute-done.3
  28.2 1.1 %broadcast_select_fusion.2 = f32[128,896]{1,0:T(8,128)S(1)} fusion(f32[128,896]{1,0:T(8,128)S(1)} %copy-done.4, f32[128,896]{1,0:T(8,128)} %collective-permute-done.3, pred[]{:T(512)S(6)} %ne.35), kind=kLoop, calls=%fused_computation.2 | loop fusion | flops 114688 | bytes 1376257 | tf_op jit(solution)/shard_map/jit(_where)/select_n | solution.py:358
  29.3 1.7 %all-to-all-done = f32[8,16,1792]{2,1,0:T(8,128)S(1)} async-done(((f32[8,16,1792]{2,1,0:T(8,128)}), f32[8,16,1792]{2,1,0:T(8,128)S(1)}, u32[]{:S(2)}, u32[]{:S(2)}) %all-to-all-start) | async-done | bytes 917536 | tf_op jit(solution)/shard_map/all_to_all | solution.py:344
  31.0 0.4 collective-permute-start.7
  31.4 0.7 collective-permute-start.8
  32.1 0.7 collective-permute-start.9
  32.9 8.1 %collective-permute-start.6 = (f32[16,1792]{1,0:T(8,128)S(1)}, f32[16,1792]{1,0:T(8,128)S(1)}, u32[]{:S(2)}, u32[]{:S(2)}) collective-permute-start(f32[16,1792]{1,0:T(8,128)S(1)} %constant_dynamic-slice_fusion), channel_id=1, source_target_pairs={{0,0},{1,16},{2,32},{3,48},{4,64},{5,80},{6,96},{7,112},{8,8},{9,2... | collective-permute-start | bytes 344072 | tf_op jit(solution)/shard_map/ppermute | solution.py:366
  41.0 10.4 %collective-permute-done.6.piece_ref = f32[16,1792]{1,0:T(8,128)S(1)} collective-permute-done((f32[16,1792]{1,0:T(8,128)S(1)}, f32[16,1792]{1,0:T(8,128)S(1)}, u32[]{:S(2)}, u32[]{:S(2)}) %collective-permute-start.6) | collective-permute-done | bytes 114720 | tf_op jit(solution)/shard_map/ppermute | solution.py:366
  51.4 1.5 %copies.1 = f32[8,16,1792]{2,1,0:T(8,128)} custom-call(s32[9]{0:T(128)S(1)} %stack.55.flags, f32[16,1792]{1,0:T(8,128)S(1)} %collective-permute-done.6.piece_ref), custom_call_target="tpu_custom_call" | custom-call | bytes 100000 | tf_op jit(solution)/shard_map/copies/pallas_call | solution.py:151
  53.0 0.0 collective-permute-done.7
  53.0 0.0 collective-permute-done.8
  53.0 0.0 collective-permute-done.9
  53.0 0.1 collective-permute-start.10
  53.1 0.7 copy-done.6
  53.8 6.0 %all-to-all-start.1 = ((f32[8,16,1792]{2,1,0:T(8,128)}), f32[8,16,1792]{2,1,0:T(8,128)S(1)}, u32[]{:S(2)}, u32[]{:S(2)}) async-start(f32[8,16,1792]{2,1,0:T(8,128)} %copies.1), calls=%async_computation.1 | async-start | bytes 1835008 | tf_op jit(solution)/shard_map/all_to_all | solution.py:371
  59.8 0.0 copy-start.2
  59.8 1.2 %broadcast_select_fusion = (f32[128,896]{1,0:T(8,128)S(1)}, f32[128,896]{1,0:T(8,128)S(1)}) fusion(f32[128,896]{1,0:T(8,128)S(1)} %broadcast_select_fusion.2, f32[128,896]{1,0:T(8,128)} %copy-done.6, pred[]{:T(512)S(6)} %ne.36, f32[128,896]{1,0:T(8,128)S(1)} %broadcast_select_fusion.3, f32[128,896]{1,0:T(8,128)S(1)} %collective-permute-done.8), kind=kLoop, calls=%fused_computation | loop fusion | flops 229376 | bytes 2752513 | tf_op jit(solution)/shard_map/jit(_where)/select_n | solution.py:375
  61.0 1.0 %collective-permute-done.10 = f32[640,128]{1,0:T(8,128)} collective-permute-done((f32[640,128]{1,0:T(8,128)S(1)}, f32[640,128]{1,0:T(8,128)}, u32[]{:S(2)}, u32[]{:S(2)}) %collective-permute-start.10) | collective-permute-done | bytes 327712 | tf_op jit(solution)/shard_map/ppermute | solution.py:372
  62.0 1.0 %broadcast_select_fusion.4 = f32[640,128]{1,0:T(8,128)S(1)} fusion(f32[640,128]{1,0:T(8,128)S(1)} %broadcast_select_fusion.6, f32[640,128]{1,0:T(8,128)} %collective-permute-done.10, pred[]{:T(512)S(6)} %eq.33), kind=kLoop, calls=%fused_computation.4 | loop fusion | flops 81920 | bytes 983041 | tf_op jit(solution)/shard_map/jit(_where)/select_n | solution.py:373
  63.0 2.3 %collective-permute-start.11 = (f32[640,128]{1,0:T(8,128)S(1)}, f32[640,128]{1,0:T(8,128)}, u32[]{:S(2)}, u32[]{:S(2)}) collective-permute-start(f32[640,128]{1,0:T(8,128)S(1)} %broadcast_select_fusion.4), channel_id=1, source_target_pairs={{0,32},{16,48},{32,0},{48,16},{1,33},{17,49},{33,1},{49,17},{2,34}... | collective-permute-start | bytes 983048 | tf_op jit(solution)/shard_map/ppermute | solution.py:378
  65.4 1.9 %collective-permute-start.13 = (f32[128,896]{1,0:T(8,128)S(1)}, f32[128,896]{1,0:T(8,128)S(1)}, u32[]{:S(2)}, u32[]{:S(2)}) collective-permute-start(f32[128,896]{1,0:T(8,128)S(1)} %get-tuple-element.57.one_hbm), channel_id=1, source_target_pairs={{120,124},{121,125},{122,126},{123,127},{124,120},{125,121},{126,1... | collective-permute-start | bytes 1376264 | tf_op jit(solution)/shard_map/ppermute | solution.py:355
  67.3 2.9 %collective-permute-start.14 = (f32[128,896]{1,0:T(8,128)S(1)}, f32[128,896]{1,0:T(8,128)S(1)}, u32[]{:S(2)}, u32[]{:S(2)}) collective-permute-start(f32[128,896]{1,0:T(8,128)S(1)} %get-tuple-element.58.two_hbm), channel_id=1, source_target_pairs={{120,121},{121,120},{122,123},{123,122},{124,125},{125,124},{126,1... | collective-permute-start | bytes 1376264 | tf_op jit(solution)/shard_map/ppermute | solution.py:355
  70.2 2.4 %collective-permute-done.11 = f32[640,128]{1,0:T(8,128)} collective-permute-done((f32[640,128]{1,0:T(8,128)S(1)}, f32[640,128]{1,0:T(8,128)}, u32[]{:S(2)}, u32[]{:S(2)}) %collective-permute-start.11) | collective-permute-done | bytes 327712 | tf_op jit(solution)/shard_map/ppermute | solution.py:378
  72.6 0.8 all-to-all-done.1
  73.4 1.6 %collective-permute-start.12 = (f32[640,128]{1,0:T(8,128)S(1)}, f32[640,128]{1,0:T(8,128)S(1)}, u32[]{:S(2)}, u32[]{:S(2)}) collective-permute-start(f32[640,128]{1,0:T(8,128)S(1)} %broadcast_select_fusion.5.small_ref), channel_id=1, source_target_pairs={{0,8},{8,0},{1,9},{9,1},{2,10},{10,2},{3,11},{11,3},{4,12},{12,4},... | collective-permute-start | bytes 983048 | tf_op jit(solution)/shard_map/ppermute | solution.py:381
  75.0 1.2 %collective-permute-done.12.other_ref = f32[640,128]{1,0:T(8,128)S(1)} collective-permute-done((f32[640,128]{1,0:T(8,128)S(1)}, f32[640,128]{1,0:T(8,128)S(1)}, u32[]{:S(2)}, u32[]{:S(2)}) %collective-permute-start.12) | collective-permute-done | bytes 327712 | tf_op jit(solution)/shard_map/ppermute | solution.py:381
  76.2 3.3 %round_first.1 = (bf16[1024,256]{1,0:T(8,128)(2,1)S(1)}, f32[1024,128]{1,0:T(8,128)S(1)}) custom-call(s32[9]{0:T(128)S(1)} %stack.55.flags, s32[16]{0:T(128)S(1)} %copy-done.2, f32[640,128]{1,0:T(8,128)S(1)} %broadcast_select_fusion.5.small_ref, f32[640,128]{1,0:T(8,128)S(1)} %collective-permute-done.12.other_ref, f32[1,1024]{1,0:T(1,128)S(1)} %bitcast.20, ...), custom_call_target="tpu_custom_call" | custom-call | bytes 100000 | tf_op jit(solution)/shard_map/round_first/pallas_call | solution.py:271
  79.5 0.0 collective-permute-done.13.got_one_hbm
  79.5 0.0 collective-permute-done.14.got_two_hbm
  79.5 10.8 %update_all.1 = f32[1024,1792]{1,0:T(8,128)} custom-call(s32[9]{0:T(128)S(1)} %stack.55.flags, s32[16]{0:T(128)S(1)} %copy-done.2, f32[1024,1792]{1,0:T(8,128)} %weight_hbm.1, f32[1024,128]{1,0:T(8,128)S(1)} %get-tuple-element.54.rounded_ref, bf16[1024,256]{1,0:T(8,128)(2,1)S(1)} %get-tuple-element.55.error_ref, f32[128,1792]{1,0:T(8,128)} %bitcast.22, ...), custom_call_target="tpu_custom_call" | custom-call | flops 2000000000 | bytes 16000000 | tf_op jit(solution)/shard_map/update_all/pallas_call | solution.py:287
  (23 shorter events, 0.2 us)
Async XLA Ops:
  0.0 5.1 %copy-start.9 = (s32[2]{0:T(128)S(1)}, s32[2]{0:T(128)}, u32[]{:S(2)}) copy-start(s32[2]{0:T(128)} %param.11) | copy-start | bytes 28
  3.5 6.8 %copy-start.8 = (f32[128,128]{1,0:T(8,128)S(1)}, f32[128,128]{1,0:T(8,128)}, u32[]{:S(2)}) copy-start(f32[128,128]{1,0:T(8,128)} %get-tuple-element.42) | copy-start | bytes 196612
  3.5 3.3 %collective-permute-start = (f32[128,2304]{1,0:T(8,128)}, f32[128,2304]{1,0:T(8,128)S(1)}, u32[]{:S(2)}, u32[]{:S(2)}) collective-permute-start(f32[128,2304]{1,0:T(8,128)} %get-tuple-element.33), channel_id=1, source_target_pairs={{0,8},{8,0},{1,9},{9,1},{2,10},{10,2},{3,11},{11,3},{4,12},{12,4},... | collective-permute-start | bytes 3538952 | tf_op jit(solution)/shard_map/ppermute | solution.py:341
  4.2 5.5 %collective-permute-start.1 = (f32[128,128]{1,0:T(8,128)}, f32[128,128]{1,0:T(8,128)S(1)}, u32[]{:S(2)}, u32[]{:S(2)}) collective-permute-start(f32[128,128]{1,0:T(8,128)} %get-tuple-element.42), channel_id=1, source_target_pairs={{0,1},{1,0},{2,3},{3,2},{4,5},{5,4},{6,7},{7,6},{8,9},{9,8},{10,11... | collective-permute-start | bytes 196616 | tf_op jit(solution)/shard_map/ppermute | solution.py:339
  6.8 1.3 %copy-start = (f32[128,2304]{1,0:T(8,128)S(1)}, f32[128,2304]{1,0:T(8,128)}, u32[]{:S(2)}) copy-start(f32[128,2304]{1,0:T(8,128)} %get-tuple-element.32.own_ref) | copy-start | bytes 3538948
  8.1 1.6 %copy-start.5 = (f32[128,896]{1,0:T(8,128)S(1)}, f32[128,896]{1,0:T(8,128)}, u32[]{:S(2)}) copy-start(f32[128,896]{1,0:T(8,128)} %get-tuple-element.39) | copy-start | bytes 1376260
  8.1 10.5 %copy-start.4 = (f32[128,896]{1,0:T(8,128)S(1)}, f32[128,896]{1,0:T(8,128)}, u32[]{:S(2)}) copy-start(f32[128,896]{1,0:T(8,128)} %get-tuple-element.40) | copy-start | bytes 1376260
  9.7 18.4 %collective-permute-start.2 = (f32[128,896]{1,0:T(8,128)S(1)}, f32[128,896]{1,0:T(8,128)S(1)}, u32[]{:S(2)}, u32[]{:S(2)}) collective-permute-start(f32[128,896]{1,0:T(8,128)S(1)} %copy-done.5), channel_id=1, source_target_pairs={{126,127},{127,126}} | collective-permute-start | bytes 1376264 | tf_op jit(solution)/shard_map/ppermute | solution.py:355
  10.4 9.7 %collective-permute-start.4 = (f32[128,128]{1,0:T(8,128)S(1)}, f32[128,128]{1,0:T(8,128)S(1)}, u32[]{:S(2)}, u32[]{:S(2)}) collective-permute-start(f32[128,128]{1,0:T(8,128)S(1)} %broadcast_select_fusion.7), channel_id=1, source_target_pairs={{0,2},{2,0},{4,6},{6,4},{1,3},{3,1},{5,7},{7,5},{8,10},{10,8},{12,... | collective-permute-start | bytes 196616 | tf_op jit(solution)/shard_map/ppermute | solution.py:346
  12.1 18.9 %all-to-all-start = ((f32[8,16,1792]{2,1,0:T(8,128)}), f32[8,16,1792]{2,1,0:T(8,128)S(1)}, u32[]{:S(2)}, u32[]{:S(2)}) async-start(f32[8,16,1792]{2,1,0:T(8,128)} %bitcast.11), calls=%async_computation | async-start | bytes 1835008 | tf_op jit(solution)/shard_map/all_to_all | solution.py:344
  18.6 9.5 %collective-permute-start.3 = (f32[128,896]{1,0:T(8,128)S(1)}, f32[128,896]{1,0:T(8,128)}, u32[]{:S(2)}, u32[]{:S(2)}) collective-permute-start(f32[128,896]{1,0:T(8,128)S(1)} %copy-done.4), channel_id=1, source_target_pairs={{123,127},{127,123}} | collective-permute-start | bytes 1376264 | tf_op jit(solution)/shard_map/ppermute | solution.py:355
  20.1 7.4 %collective-permute-start.5 = (f32[128,128]{1,0:T(8,128)S(1)}, f32[128,128]{1,0:T(8,128)S(1)}, u32[]{:S(2)}, u32[]{:S(2)}) collective-permute-start(f32[128,128]{1,0:T(8,128)S(1)} %broadcast_select_fusion.8.diag_ref), channel_id=1, source_target_pairs={{0,4},{2,6},{4,0},{6,2},{1,5},{3,7},{5,1},{7,3},{8,12},{10,14},{12... | collective-permute-start | bytes 196616 | tf_op jit(solution)/shard_map/ppermute | solution.py:348
  31.0 21.9 %collective-permute-start.7 = (f32[640,128]{1,0:T(8,128)S(1)}, f32[640,128]{1,0:T(8,128)}, u32[]{:S(2)}, u32[]{:S(2)}) collective-permute-start(f32[640,128]{1,0:T(8,128)S(1)} %join.1), channel_id=1, source_target_pairs={{0,64},{64,0},{1,65},{65,1},{2,66},{66,2},{3,67},{67,3},{4,68},{68... | collective-permute-start | bytes 983048 | tf_op jit(solution)/shard_map/ppermute | solution.py:367
  31.4 21.6 %collective-permute-start.8 = (f32[128,896]{1,0:T(8,128)S(1)}, f32[128,896]{1,0:T(8,128)S(1)}, u32[]{:S(2)}, u32[]{:S(2)}) collective-permute-start(f32[128,896]{1,0:T(8,128)S(1)} %broadcast_select_fusion.3), channel_id=1, source_target_pairs={{124,126},{125,127},{126,124},{127,125}} | collective-permute-start | bytes 1376264 | tf_op jit(solution)/shard_map/ppermute | solution.py:355
  32.1 20.9 %collective-permute-start.9 = (f32[128,896]{1,0:T(8,128)S(1)}, f32[128,896]{1,0:T(8,128)S(1)}, u32[]{:S(2)}, u32[]{:S(2)}) collective-permute-start(f32[128,896]{1,0:T(8,128)S(1)} %broadcast_select_fusion.2), channel_id=1, source_target_pairs={{121,123},{123,121},{125,127},{127,125}} | collective-permute-start | bytes 1376264 | tf_op jit(solution)/shard_map/ppermute | solution.py:355
  32.9 18.6 %collective-permute-start.6 = (f32[16,1792]{1,0:T(8,128)S(1)}, f32[16,1792]{1,0:T(8,128)S(1)}, u32[]{:S(2)}, u32[]{:S(2)}) collective-permute-start(f32[16,1792]{1,0:T(8,128)S(1)} %constant_dynamic-slice_fusion), channel_id=1, source_target_pairs={{0,0},{1,16},{2,32},{3,48},{4,64},{5,80},{6,96},{7,112},{8,8},{9,2... | collective-permute-start | bytes 344072 | tf_op jit(solution)/shard_map/ppermute | solution.py:366
  53.0 0.8 copy-start.6
  53.0 9.0 %collective-permute-start.10 = (f32[640,128]{1,0:T(8,128)S(1)}, f32[640,128]{1,0:T(8,128)}, u32[]{:S(2)}, u32[]{:S(2)}) collective-permute-start(f32[640,128]{1,0:T(8,128)S(1)} %broadcast_select_fusion.6), channel_id=1, source_target_pairs={{0,16},{16,0},{32,48},{48,32},{1,17},{17,1},{33,49},{49,33},{2,18}... | collective-permute-start | bytes 983048 | tf_op jit(solution)/shard_map/ppermute | solution.py:372
  53.8 19.6 %all-to-all-start.1 = ((f32[8,16,1792]{2,1,0:T(8,128)}), f32[8,16,1792]{2,1,0:T(8,128)S(1)}, u32[]{:S(2)}, u32[]{:S(2)}) async-start(f32[8,16,1792]{2,1,0:T(8,128)} %copies.1), calls=%async_computation.1 | async-start | bytes 1835008 | tf_op jit(solution)/shard_map/all_to_all | solution.py:371
  59.8 16.4 %copy-start.1 = (f32[1024]{0:T(1024)S(1)}, f32[1024]{0:T(1024)}, u32[]{:S(2)}) copy-start(f32[1024]{0:T(1024)} %param.7) | copy-start | bytes 12292
  59.8 16.4 %copy-start.2 = (s32[16]{0:T(128)S(1)}, s32[16]{0:T(128)}, u32[]{:S(2)}) copy-start(s32[16]{0:T(128)} %codes.3) | copy-start | bytes 196
  61.0 14.0 %copy-start.7 = (f32[2,128,128]{2,1,0:T(8,128)S(1)}, f32[2,128,128]{2,1,0:T(8,128)}, u32[]{:S(2)}) copy-start(f32[2,128,128]{2,1,0:T(8,128)} %param.9) | copy-start | bytes 393220
  63.0 9.6 %collective-permute-start.11 = (f32[640,128]{1,0:T(8,128)S(1)}, f32[640,128]{1,0:T(8,128)}, u32[]{:S(2)}, u32[]{:S(2)}) collective-permute-start(f32[640,128]{1,0:T(8,128)S(1)} %broadcast_select_fusion.4), channel_id=1, source_target_pairs={{0,32},{16,48},{32,0},{48,16},{1,33},{17,49},{33,1},{49,17},{2,34}... | collective-permute-start | bytes 983048 | tf_op jit(solution)/shard_map/ppermute | solution.py:378
  65.4 14.1 %collective-permute-start.13 = (f32[128,896]{1,0:T(8,128)S(1)}, f32[128,896]{1,0:T(8,128)S(1)}, u32[]{:S(2)}, u32[]{:S(2)}) collective-permute-start(f32[128,896]{1,0:T(8,128)S(1)} %get-tuple-element.57.one_hbm), channel_id=1, source_target_pairs={{120,124},{121,125},{122,126},{123,127},{124,120},{125,121},{126,1... | collective-permute-start | bytes 1376264 | tf_op jit(solution)/shard_map/ppermute | solution.py:355
  67.3 12.2 %collective-permute-start.14 = (f32[128,896]{1,0:T(8,128)S(1)}, f32[128,896]{1,0:T(8,128)S(1)}, u32[]{:S(2)}, u32[]{:S(2)}) collective-permute-start(f32[128,896]{1,0:T(8,128)S(1)} %get-tuple-element.58.two_hbm), channel_id=1, source_target_pairs={{120,121},{121,120},{122,123},{123,122},{124,125},{125,124},{126,1... | collective-permute-start | bytes 1376264 | tf_op jit(solution)/shard_map/ppermute | solution.py:355
  73.4 6.1 %copy-start.3 = (f32[8,16,1792]{2,1,0:T(8,128)}, f32[8,16,1792]{2,1,0:T(8,128)S(1)}, u32[]{:S(2)}) copy-start(f32[8,16,1792]{2,1,0:T(8,128)S(1)} %all-to-all-done.1) | copy-start | bytes 2752516
  73.4 2.8 %collective-permute-start.12 = (f32[640,128]{1,0:T(8,128)S(1)}, f32[640,128]{1,0:T(8,128)S(1)}, u32[]{:S(2)}, u32[]{:S(2)}) collective-permute-start(f32[640,128]{1,0:T(8,128)S(1)} %broadcast_select_fusion.5.small_ref), channel_id=1, source_target_pairs={{0,8},{8,0},{1,9},{9,1},{2,10},{10,2},{3,11},{11,3},{4,12},{12,4},... | collective-permute-start | bytes 983048 | tf_op jit(solution)/shard_map/ppermute | solution.py:381

commit v4 on v3

--- a/solution.py
+++ b/solution.py
@@ -26,8 +26,21 @@
 BIG_VMEM = 54 * 1024 * 1024
 
 
-def dot(a, b):
-    return jnp.dot(a, b, precision=lax.Precision.HIGHEST, preferred_element_type=jnp.float32)
+def split3(value):
+    high = value.astype(jnp.bfloat16)
+    rest = value - high.astype(jnp.float32)
+    middle = rest.astype(jnp.bfloat16)
+    return high, middle, (rest - middle.astype(jnp.float32)).astype(jnp.bfloat16)
+
+
+def left_side(value):
+    h, m, l = split3(value)
+    return jnp.concatenate([h, h, m, h, l, m], 1)
+
+
+def right_side(value):
+    h, m, l = split3(value)
+    return jnp.concatenate([h, m, h, l, h, m], 0)
 
 
 def fast_dot(a, b):
@@ -59,16 +72,17 @@
     recip = [1.0 / s for s in steps]
     for g in range(BLK // SUB):
         low = g * SUB
-        inv_g = inverse_t[low : low + SUB, low : low + SUB]
-        later = diag_t[low + SUB :, low : low + SUB]
+        inv_g = left_side(inverse_t[low : low + SUB, low : low + SUB])
+        if low + SUB < BLK:
+            later = left_side(diag_t[low + SUB :, low : low + SUB])
         for i, part in enumerate(parts):
             current = part[:SUB]
             quantized = quantize(current, steps[i], recip[i], codes)
-            error = dot(inv_g, current - quantized)
+            error = fast_dot(inv_g, right_side(current - quantized))
             rounded[i].append(quantized)
             errors[i].append(error)
             if low + SUB < BLK:
-                parts[i] = part[SUB:] - dot(later, error)
+                parts[i] = part[SUB:] - fast_dot(later, right_side(error))
     return [jnp.concatenate(r, 0) for r in rounded], [jnp.concatenate(e, 0) for e in errors]
 
 

time: 91.4 us -> 90.3 us (0.988)
  waiting for transfers between devices: 21.2 us -> 23.6 us
  starting transfers between devices: 42 us -> 39.6 us
  Pallas kernels: 21.3 us -> 20.1 us
    all_to_all x1, waiting for transfers between devices: 0.8 us -> 1.89 us  [local(): panel0 = lax.all_to_all(copies, ROWS, 0, 0, tiled=True).reshape(BLK, width)]
    ppermute x1, starting transfers between devices: 1.56 us -> 0.47 us  [local(): other = lax.ppermute(small, 'k', swap)]
    select_n x1, other arithmetic: 0.04 us -> 1.01 us  [local(): small = jnp.where(chip & 4 == owner_chip & 4, small, got)]
    select_n x1, other arithmetic: 1.01 us -> 0.04 us  [local(): small = jnp.where(chip & 1 == owner_chip & 1, small, got)]
    all_to_all x1, starting transfers between devices: 6.03 us -> 5.06 us  [local(): panel0 = lax.all_to_all(copies, ROWS, 0, 0, tiled=True).reshape(BLK, width)]
    ppermute x1, waiting for transfers between devices: 0.98 us -> 1.95 us  [local(): got = lax.ppermute(small, 'y', [(i, i ^ 1) for i in range(4)])]
  transfers between devices with their start and end apart: 17 -> 17, of which waited for: 8 -> 8; matrix products, arithmetic and copies ran while one was open for 4% -> 4% of each run, Pallas kernels for 8% -> 7%
where the time goes in v4:
time: 90.3 us; the launch traced here: 89.2 us
  starting transfers between devices  39.6 us (44%)
  waiting for transfers between devices  23.6 us (26%)
  Pallas kernels  20.1 us (22%)
  other arithmetic  3.44 us (4%)
  local copies, waits for them, and re-layouts  2.07 us (2%)
    ppermute x1, waiting for transfers between devices, local(): lax.ppermute(lax.dynamic_slice_in_dim(came, owner_chip * piece, piece, 0)...  10.4 us
    pallas_call x1, Pallas kernels, last_call(): pl.pallas_call(last_kernel, grid=(n // rows,), out_shape=jax.ShapeDtypeSt...  10.4 us
    ppermute x1, starting transfers between devices, local(): lax.ppermute(lax.dynamic_slice_in_dim(came, owner_chip * piece, piece, 0)...  8.14 us
    ppermute x6, starting transfers between devices, down(): return lax.ppermute(value, AXES, [(at(r), at(r ^ bit)) for r in rows])  7.92 us
    all_to_all x1, starting transfers between devices, local(): came = lax.all_to_all(sent, CHIPS, 0, 0, tiled=True)  6.53 us
    ppermute x1, starting transfers between devices, local(): got = lax.ppermute(diag, 'z', [(i, i ^ 2) for i in range(4)])  5.34 us
    all_to_all x1, starting transfers between devices, local(): panel0 = lax.all_to_all(copies, ROWS, 0, 0, tiled=True).reshape(BLK, width)  5.06 us
    pallas_call x3, Pallas kernels, small_call(): pl.pallas_call(kernel, out_shape=tuple((jax.ShapeDtypeStruct(shape, jnp.f...  3.63 us
  transfers between devices with their start and end apart: 17, of which 8 were waited for; matrix products, arithmetic and copies ran while one was open for 4% of the time, Pallas kernels for 7%

profile of v4, /device:TPU:29, one launch (start us, length us, event | category | flops | bytes accessed | tf_op | source)
XLA Modules:
  0.0 89.2 jit_solution(12430184705157794927)
XLA Ops:
  0.0 3.5 %halves.1 = (f32[128,2304]{1,0:T(8,128)}, f32[128,2304]{1,0:T(8,128)}, f32[128,128]{1,0:T(8,128)}, f32[128,896]{1,0:T(8,128)}, f32[128,896]{1,0:T(8,128)}) custom-call(f32[128,3584]{1,0:T(8,128)} %panel_ref.1, f32[1024,1792]{1,0:T(8,128)} %weight_hbm.1), custom_call_target="tpu_custom_call" | custom-call | tf_op jit(solution)/shard_map/halves/pallas_call | solution.py:181
  3.5 0.6 collective-permute-start
  4.2 0.9 %collective-permute-start.1 = (f32[128,128]{1,0:T(8,128)}, f32[128,128]{1,0:T(8,128)S(1)}, u32[]{:S(2)}, u32[]{:S(2)}) collective-permute-start(f32[128,128]{1,0:T(8,128)} %get-tuple-element.42), channel_id=1, source_target_pairs={{0,1},{1,0},{2,3},{3,2},{4,5},{5,4},{6,7},{7,6},{8,9},{9,8},{10,11... | collective-permute-start | bytes 196616 | tf_op jit(solution)/shard_map/ppermute | solution.py:353
  5.3 0.1 stack.55.flags
  5.3 1.5 %collective-permute-done.got_ref = f32[128,2304]{1,0:T(8,128)S(1)} collective-permute-done((f32[128,2304]{1,0:T(8,128)}, f32[128,2304]{1,0:T(8,128)S(1)}, u32[]{:S(2)}, u32[]{:S(2)}) %collective-permute-start) | collective-permute-done | bytes 1179680 | tf_op jit(solution)/shard_map/ppermute | solution.py:355
  6.8 1.3 %copy-done = f32[128,2304]{1,0:T(8,128)S(1)} copy-done((f32[128,2304]{1,0:T(8,128)S(1)}, f32[128,2304]{1,0:T(8,128)}, u32[]{:S(2)}) %copy-start) | copy-done | bytes 1179672
  8.1 1.5 %choose.1 = (f32[128,1792]{1,0:T(8,128)}, f32[512,128]{1,0:T(8,128)S(1)}) custom-call(s32[9]{0:T(128)S(1)} %stack.55.flags, f32[128,2304]{1,0:T(8,128)S(1)} %copy-done, f32[128,2304]{1,0:T(8,128)S(1)} %collective-permute-done.got_ref), custom_call_target="tpu_custom_call" | custom-call | bytes 100000 | tf_op jit(solution)/shard_map/choose/pallas_call | solution.py:165
  9.7 0.0 collective-permute-done.1
  9.7 0.7 collective-permute-start.2
  10.4 1.7 %collective-permute-start.4 = (f32[128,128]{1,0:T(8,128)S(1)}, f32[128,128]{1,0:T(8,128)S(1)}, u32[]{:S(2)}, u32[]{:S(2)}) collective-permute-start(f32[128,128]{1,0:T(8,128)S(1)} %broadcast_select_fusion.7), channel_id=1, source_target_pairs={{0,2},{2,0},{4,6},{6,4},{1,3},{3,1},{5,7},{7,5},{8,10},{10,8},{12,... | collective-permute-start | bytes 196616 | tf_op jit(solution)/shard_map/ppermute | solution.py:360
  12.1 6.5 %all-to-all-start = ((f32[8,16,1792]{2,1,0:T(8,128)}), f32[8,16,1792]{2,1,0:T(8,128)S(1)}, u32[]{:S(2)}, u32[]{:S(2)}) async-start(f32[8,16,1792]{2,1,0:T(8,128)} %bitcast.11), calls=%async_computation | async-start | bytes 1835008 | tf_op jit(solution)/shard_map/all_to_all | solution.py:358
  18.6 1.4 %collective-permute-start.3 = (f32[128,896]{1,0:T(8,128)S(1)}, f32[128,896]{1,0:T(8,128)}, u32[]{:S(2)}, u32[]{:S(2)}) collective-permute-start(f32[128,896]{1,0:T(8,128)S(1)} %copy-done.4), channel_id=1, source_target_pairs={{123,127},{127,123}} | collective-permute-start | bytes 1376264 | tf_op jit(solution)/shard_map/ppermute | solution.py:369
  20.1 0.0 collective-permute-done.4
  20.1 5.3 %collective-permute-start.5 = (f32[128,128]{1,0:T(8,128)S(1)}, f32[128,128]{1,0:T(8,128)S(1)}, u32[]{:S(2)}, u32[]{:S(2)}) collective-permute-start(f32[128,128]{1,0:T(8,128)S(1)} %broadcast_select_fusion.8.diag_ref), channel_id=1, source_target_pairs={{0,4},{2,6},{4,0},{6,2},{1,5},{3,7},{5,1},{7,3},{8,12},{10,14},{12... | collective-permute-start | bytes 196616 | tf_op jit(solution)/shard_map/ppermute | solution.py:362
  25.4 2.1 %collective-permute-done.5.got_ref = f32[128,128]{1,0:T(8,128)S(1)} collective-permute-done((f32[128,128]{1,0:T(8,128)S(1)}, f32[128,128]{1,0:T(8,128)S(1)}, u32[]{:S(2)}, u32[]{:S(2)}) %collective-permute-start.5) | collective-permute-done | bytes 65568 | tf_op jit(solution)/shard_map/ppermute | solution.py:362
  27.5 0.6 join.1
  28.1 0.0 collective-permute-done.2
  28.1 0.1 broadcast_select_fusion.3
  28.2 0.0 collective-permute-done.3
  28.2 1.1 %broadcast_select_fusion.2 = f32[128,896]{1,0:T(8,128)S(1)} fusion(f32[128,896]{1,0:T(8,128)S(1)} %copy-done.4, f32[128,896]{1,0:T(8,128)} %collective-permute-done.3, pred[]{:T(512)S(6)} %ne.35), kind=kLoop, calls=%fused_computation.2 | loop fusion | flops 114688 | bytes 1376257 | tf_op jit(solution)/shard_map/jit(_where)/select_n | solution.py:372
  29.3 1.7 %all-to-all-done = f32[8,16,1792]{2,1,0:T(8,128)S(1)} async-done(((f32[8,16,1792]{2,1,0:T(8,128)}), f32[8,16,1792]{2,1,0:T(8,128)S(1)}, u32[]{:S(2)}, u32[]{:S(2)}) %all-to-all-start) | async-done | bytes 917536 | tf_op jit(solution)/shard_map/all_to_all | solution.py:358
  31.0 0.4 collective-permute-start.7
  31.4 0.7 collective-permute-start.8
  32.1 0.7 collective-permute-start.9
  32.9 8.1 %collective-permute-start.6 = (f32[16,1792]{1,0:T(8,128)S(1)}, f32[16,1792]{1,0:T(8,128)S(1)}, u32[]{:S(2)}, u32[]{:S(2)}) collective-permute-start(f32[16,1792]{1,0:T(8,128)S(1)} %constant_dynamic-slice_fusion), channel_id=1, source_target_pairs={{0,0},{1,16},{2,32},{3,48},{4,64},{5,80},{6,96},{7,112},{8,8},{9,2... | collective-permute-start | bytes 344072 | tf_op jit(solution)/shard_map/ppermute | solution.py:380
  41.0 10.4 %collective-permute-done.6.piece_ref = f32[16,1792]{1,0:T(8,128)S(1)} collective-permute-done((f32[16,1792]{1,0:T(8,128)S(1)}, f32[16,1792]{1,0:T(8,128)S(1)}, u32[]{:S(2)}, u32[]{:S(2)}) %collective-permute-start.6) | collective-permute-done | bytes 114720 | tf_op jit(solution)/shard_map/ppermute | solution.py:380
  51.4 1.5 %copies.1 = f32[8,16,1792]{2,1,0:T(8,128)} custom-call(s32[9]{0:T(128)S(1)} %stack.55.flags, f32[16,1792]{1,0:T(8,128)S(1)} %collective-permute-done.6.piece_ref), custom_call_target="tpu_custom_call" | custom-call | bytes 100000 | tf_op jit(solution)/shard_map/copies/pallas_call | solution.py:165
  53.0 0.0 collective-permute-done.7
  53.0 1.0 %broadcast_select_fusion.6 = f32[640,128]{1,0:T(8,128)S(1)} fusion(f32[640,128]{1,0:T(8,128)S(1)} %join.1, f32[640,128]{1,0:T(8,128)} %collective-permute-done.7, pred[]{:T(512)S(6)} %eq.31), kind=kLoop, calls=%fused_computation.6 | loop fusion | flops 81920 | bytes 983041 | tf_op jit(solution)/shard_map/jit(_where)/select_n | solution.py:382
  54.0 0.0 collective-permute-done.8
  54.0 0.0 collective-permute-done.9
  54.0 0.1 collective-permute-start.10
  54.1 0.7 copy-done.6
  54.8 5.1 %all-to-all-start.1 = ((f32[8,16,1792]{2,1,0:T(8,128)}), f32[8,16,1792]{2,1,0:T(8,128)S(1)}, u32[]{:S(2)}, u32[]{:S(2)}) async-start(f32[8,16,1792]{2,1,0:T(8,128)} %copies.1), calls=%async_computation.1 | async-start | bytes 1835008 | tf_op jit(solution)/shard_map/all_to_all | solution.py:385
  59.8 0.0 copy-start.2
  59.8 1.2 %broadcast_select_fusion = (f32[128,896]{1,0:T(8,128)S(1)}, f32[128,896]{1,0:T(8,128)S(1)}) fusion(f32[128,896]{1,0:T(8,128)S(1)} %broadcast_select_fusion.2, f32[128,896]{1,0:T(8,128)} %copy-done.6, pred[]{:T(512)S(6)} %ne.36, f32[128,896]{1,0:T(8,128)S(1)} %broadcast_select_fusion.3, f32[128,896]{1,0:T(8,128)S(1)} %collective-permute-done.8), kind=kLoop, calls=%fused_computation | loop fusion | flops 229376 | bytes 2752513 | tf_op jit(solution)/shard_map/jit(_where)/select_n | solution.py:389
  61.0 2.0 %collective-permute-done.10 = f32[640,128]{1,0:T(8,128)} collective-permute-done((f32[640,128]{1,0:T(8,128)S(1)}, f32[640,128]{1,0:T(8,128)}, u32[]{:S(2)}, u32[]{:S(2)}) %collective-permute-start.10) | collective-permute-done | bytes 327712 | tf_op jit(solution)/shard_map/ppermute | solution.py:386
  63.0 2.4 %collective-permute-start.11 = (f32[640,128]{1,0:T(8,128)S(1)}, f32[640,128]{1,0:T(8,128)}, u32[]{:S(2)}, u32[]{:S(2)}) collective-permute-start(f32[640,128]{1,0:T(8,128)S(1)} %broadcast_select_fusion.4), channel_id=1, source_target_pairs={{0,32},{16,48},{32,0},{48,16},{1,33},{17,49},{33,1},{49,17},{2,34}... | collective-permute-start | bytes 983048 | tf_op jit(solution)/shard_map/ppermute | solution.py:392
  65.4 1.9 %collective-permute-start.13 = (f32[128,896]{1,0:T(8,128)S(1)}, f32[128,896]{1,0:T(8,128)S(1)}, u32[]{:S(2)}, u32[]{:S(2)}) collective-permute-start(f32[128,896]{1,0:T(8,128)S(1)} %get-tuple-element.57.one_hbm), channel_id=1, source_target_pairs={{120,124},{121,125},{122,126},{123,127},{124,120},{125,121},{126,1... | collective-permute-start | bytes 1376264 | tf_op jit(solution)/shard_map/ppermute | solution.py:369
  67.3 2.5 %collective-permute-start.14 = (f32[128,896]{1,0:T(8,128)S(1)}, f32[128,896]{1,0:T(8,128)S(1)}, u32[]{:S(2)}, u32[]{:S(2)}) collective-permute-start(f32[128,896]{1,0:T(8,128)S(1)} %get-tuple-element.58.two_hbm), channel_id=1, source_target_pairs={{120,121},{121,120},{122,123},{123,122},{124,125},{125,124},{126,1... | collective-permute-start | bytes 1376264 | tf_op jit(solution)/shard_map/ppermute | solution.py:369
  69.8 2.7 %collective-permute-done.11 = f32[640,128]{1,0:T(8,128)} collective-permute-done((f32[640,128]{1,0:T(8,128)S(1)}, f32[640,128]{1,0:T(8,128)}, u32[]{:S(2)}, u32[]{:S(2)}) %collective-permute-start.11) | collective-permute-done | bytes 327712 | tf_op jit(solution)/shard_map/ppermute | solution.py:392
  72.6 1.9 %all-to-all-done.1 = f32[8,16,1792]{2,1,0:T(8,128)S(1)} async-done(((f32[8,16,1792]{2,1,0:T(8,128)}), f32[8,16,1792]{2,1,0:T(8,128)S(1)}, u32[]{:S(2)}, u32[]{:S(2)}) %all-to-all-start.1) | async-done | bytes 917536 | tf_op jit(solution)/shard_map/all_to_all | solution.py:385
  74.5 0.5 collective-permute-start.12
  75.0 1.2 %collective-permute-done.12.other_ref = f32[640,128]{1,0:T(8,128)S(1)} collective-permute-done((f32[640,128]{1,0:T(8,128)S(1)}, f32[640,128]{1,0:T(8,128)S(1)}, u32[]{:S(2)}, u32[]{:S(2)}) %collective-permute-start.12) | collective-permute-done | bytes 327712 | tf_op jit(solution)/shard_map/ppermute | solution.py:395
  76.2 2.6 %round_first.1 = (bf16[1024,256]{1,0:T(8,128)(2,1)S(1)}, f32[1024,128]{1,0:T(8,128)S(1)}) custom-call(s32[9]{0:T(128)S(1)} %stack.55.flags, s32[16]{0:T(128)S(1)} %copy-done.2, f32[640,128]{1,0:T(8,128)S(1)} %broadcast_select_fusion.5.small_ref, f32[640,128]{1,0:T(8,128)S(1)} %collective-permute-done.12.other_ref, f32[1,1024]{1,0:T(1,128)S(1)} %bitcast.20, ...), custom_call_target="tpu_custom_call" | custom-call | bytes 100000 | tf_op jit(solution)/shard_map/round_first/pallas_call | solution.py:285
  78.8 0.0 collective-permute-done.13.got_one_hbm
  78.8 0.0 collective-permute-done.14.got_two_hbm
  78.8 10.4 %update_all.1 = f32[1024,1792]{1,0:T(8,128)} custom-call(s32[9]{0:T(128)S(1)} %stack.55.flags, s32[16]{0:T(128)S(1)} %copy-done.2, f32[1024,1792]{1,0:T(8,128)} %weight_hbm.1, f32[1024,128]{1,0:T(8,128)S(1)} %get-tuple-element.54.rounded_ref, bf16[1024,256]{1,0:T(8,128)(2,1)S(1)} %get-tuple-element.55.error_ref, f32[128,1792]{1,0:T(8,128)} %bitcast.22, ...), custom_call_target="tpu_custom_call" | custom-call | flops 2000000000 | bytes 16000000 | tf_op jit(solution)/shard_map/update_all/pallas_call | solution.py:301
  (23 shorter events, 0.2 us)
Async XLA Ops:
  0.0 5.1 %copy-start.9 = (s32[2]{0:T(128)S(1)}, s32[2]{0:T(128)}, u32[]{:S(2)}) copy-start(s32[2]{0:T(128)} %param.11) | copy-start | bytes 28
  3.5 6.8 %copy-start.8 = (f32[128,128]{1,0:T(8,128)S(1)}, f32[128,128]{1,0:T(8,128)}, u32[]{:S(2)}) copy-start(f32[128,128]{1,0:T(8,128)} %get-tuple-element.42) | copy-start | bytes 196612
  3.5 3.3 %collective-permute-start = (f32[128,2304]{1,0:T(8,128)}, f32[128,2304]{1,0:T(8,128)S(1)}, u32[]{:S(2)}, u32[]{:S(2)}) collective-permute-start(f32[128,2304]{1,0:T(8,128)} %get-tuple-element.33), channel_id=1, source_target_pairs={{0,8},{8,0},{1,9},{9,1},{2,10},{10,2},{3,11},{11,3},{4,12},{12,4},... | collective-permute-start | bytes 3538952 | tf_op jit(solution)/shard_map/ppermute | solution.py:355
  4.2 5.5 %collective-permute-start.1 = (f32[128,128]{1,0:T(8,128)}, f32[128,128]{1,0:T(8,128)S(1)}, u32[]{:S(2)}, u32[]{:S(2)}) collective-permute-start(f32[128,128]{1,0:T(8,128)} %get-tuple-element.42), channel_id=1, source_target_pairs={{0,1},{1,0},{2,3},{3,2},{4,5},{5,4},{6,7},{7,6},{8,9},{9,8},{10,11... | collective-permute-start | bytes 196616 | tf_op jit(solution)/shard_map/ppermute | solution.py:353
  6.8 1.3 %copy-start = (f32[128,2304]{1,0:T(8,128)S(1)}, f32[128,2304]{1,0:T(8,128)}, u32[]{:S(2)}) copy-start(f32[128,2304]{1,0:T(8,128)} %get-tuple-element.32.own_ref) | copy-start | bytes 3538948
  8.1 1.6 %copy-start.5 = (f32[128,896]{1,0:T(8,128)S(1)}, f32[128,896]{1,0:T(8,128)}, u32[]{:S(2)}) copy-start(f32[128,896]{1,0:T(8,128)} %get-tuple-element.39) | copy-start | bytes 1376260
  8.1 10.5 %copy-start.4 = (f32[128,896]{1,0:T(8,128)S(1)}, f32[128,896]{1,0:T(8,128)}, u32[]{:S(2)}) copy-start(f32[128,896]{1,0:T(8,128)} %get-tuple-element.40) | copy-start | bytes 1376260
  9.7 18.4 %collective-permute-start.2 = (f32[128,896]{1,0:T(8,128)S(1)}, f32[128,896]{1,0:T(8,128)S(1)}, u32[]{:S(2)}, u32[]{:S(2)}) collective-permute-start(f32[128,896]{1,0:T(8,128)S(1)} %copy-done.5), channel_id=1, source_target_pairs={{126,127},{127,126}} | collective-permute-start | bytes 1376264 | tf_op jit(solution)/shard_map/ppermute | solution.py:369
  10.4 9.7 %collective-permute-start.4 = (f32[128,128]{1,0:T(8,128)S(1)}, f32[128,128]{1,0:T(8,128)S(1)}, u32[]{:S(2)}, u32[]{:S(2)}) collective-permute-start(f32[128,128]{1,0:T(8,128)S(1)} %broadcast_select_fusion.7), channel_id=1, source_target_pairs={{0,2},{2,0},{4,6},{6,4},{1,3},{3,1},{5,7},{7,5},{8,10},{10,8},{12,... | collective-permute-start | bytes 196616 | tf_op jit(solution)/shard_map/ppermute | solution.py:360
  12.1 18.9 %all-to-all-start = ((f32[8,16,1792]{2,1,0:T(8,128)}), f32[8,16,1792]{2,1,0:T(8,128)S(1)}, u32[]{:S(2)}, u32[]{:S(2)}) async-start(f32[8,16,1792]{2,1,0:T(8,128)} %bitcast.11), calls=%async_computation | async-start | bytes 1835008 | tf_op jit(solution)/shard_map/all_to_all | solution.py:358
  18.6 9.5 %collective-permute-start.3 = (f32[128,896]{1,0:T(8,128)S(1)}, f32[128,896]{1,0:T(8,128)}, u32[]{:S(2)}, u32[]{:S(2)}) collective-permute-start(f32[128,896]{1,0:T(8,128)S(1)} %copy-done.4), channel_id=1, source_target_pairs={{123,127},{127,123}} | collective-permute-start | bytes 1376264 | tf_op jit(solution)/shard_map/ppermute | solution.py:369
  20.1 7.4 %collective-permute-start.5 = (f32[128,128]{1,0:T(8,128)S(1)}, f32[128,128]{1,0:T(8,128)S(1)}, u32[]{:S(2)}, u32[]{:S(2)}) collective-permute-start(f32[128,128]{1,0:T(8,128)S(1)} %broadcast_select_fusion.8.diag_ref), channel_id=1, source_target_pairs={{0,4},{2,6},{4,0},{6,2},{1,5},{3,7},{5,1},{7,3},{8,12},{10,14},{12... | collective-permute-start | bytes 196616 | tf_op jit(solution)/shard_map/ppermute | solution.py:362
  31.0 21.9 %collective-permute-start.7 = (f32[640,128]{1,0:T(8,128)S(1)}, f32[640,128]{1,0:T(8,128)}, u32[]{:S(2)}, u32[]{:S(2)}) collective-permute-start(f32[640,128]{1,0:T(8,128)S(1)} %join.1), channel_id=1, source_target_pairs={{0,64},{64,0},{1,65},{65,1},{2,66},{66,2},{3,67},{67,3},{4,68},{68... | collective-permute-start | bytes 983048 | tf_op jit(solution)/shard_map/ppermute | solution.py:381
  31.4 22.5 %collective-permute-start.8 = (f32[128,896]{1,0:T(8,128)S(1)}, f32[128,896]{1,0:T(8,128)S(1)}, u32[]{:S(2)}, u32[]{:S(2)}) collective-permute-start(f32[128,896]{1,0:T(8,128)S(1)} %broadcast_select_fusion.3), channel_id=1, source_target_pairs={{124,126},{125,127},{126,124},{127,125}} | collective-permute-start | bytes 1376264 | tf_op jit(solution)/shard_map/ppermute | solution.py:369
  32.1 21.9 %collective-permute-start.9 = (f32[128,896]{1,0:T(8,128)S(1)}, f32[128,896]{1,0:T(8,128)S(1)}, u32[]{:S(2)}, u32[]{:S(2)}) collective-permute-start(f32[128,896]{1,0:T(8,128)S(1)} %broadcast_select_fusion.2), channel_id=1, source_target_pairs={{121,123},{123,121},{125,127},{127,125}} | collective-permute-start | bytes 1376264 | tf_op jit(solution)/shard_map/ppermute | solution.py:369
  32.9 18.6 %collective-permute-start.6 = (f32[16,1792]{1,0:T(8,128)S(1)}, f32[16,1792]{1,0:T(8,128)S(1)}, u32[]{:S(2)}, u32[]{:S(2)}) collective-permute-start(f32[16,1792]{1,0:T(8,128)S(1)} %constant_dynamic-slice_fusion), channel_id=1, source_target_pairs={{0,0},{1,16},{2,32},{3,48},{4,64},{5,80},{6,96},{7,112},{8,8},{9,2... | collective-permute-start | bytes 344072 | tf_op jit(solution)/shard_map/ppermute | solution.py:380
  54.0 0.8 copy-start.6
  54.0 9.0 %collective-permute-start.10 = (f32[640,128]{1,0:T(8,128)S(1)}, f32[640,128]{1,0:T(8,128)}, u32[]{:S(2)}, u32[]{:S(2)}) collective-permute-start(f32[640,128]{1,0:T(8,128)S(1)} %broadcast_select_fusion.6), channel_id=1, source_target_pairs={{0,16},{16,0},{32,48},{48,32},{1,17},{17,1},{33,49},{49,33},{2,18}... | collective-permute-start | bytes 983048 | tf_op jit(solution)/shard_map/ppermute | solution.py:386
  54.8 19.7 %all-to-all-start.1 = ((f32[8,16,1792]{2,1,0:T(8,128)}), f32[8,16,1792]{2,1,0:T(8,128)S(1)}, u32[]{:S(2)}, u32[]{:S(2)}) async-start(f32[8,16,1792]{2,1,0:T(8,128)} %copies.1), calls=%async_computation.1 | async-start | bytes 1835008 | tf_op jit(solution)/shard_map/all_to_all | solution.py:385
  59.8 16.4 %copy-start.1 = (f32[1024]{0:T(1024)S(1)}, f32[1024]{0:T(1024)}, u32[]{:S(2)}) copy-start(f32[1024]{0:T(1024)} %param.7) | copy-start | bytes 12292
  59.8 16.4 %copy-start.2 = (s32[16]{0:T(128)S(1)}, s32[16]{0:T(128)}, u32[]{:S(2)}) copy-start(s32[16]{0:T(128)} %codes.3) | copy-start | bytes 196
  61.0 14.0 %copy-start.7 = (f32[2,128,128]{2,1,0:T(8,128)S(1)}, f32[2,128,128]{2,1,0:T(8,128)}, u32[]{:S(2)}) copy-start(f32[2,128,128]{2,1,0:T(8,128)} %param.9) | copy-start | bytes 393220
  63.0 9.6 %collective-permute-start.11 = (f32[640,128]{1,0:T(8,128)S(1)}, f32[640,128]{1,0:T(8,128)}, u32[]{:S(2)}, u32[]{:S(2)}) collective-permute-start(f32[640,128]{1,0:T(8,128)S(1)} %broadcast_select_fusion.4), channel_id=1, source_target_pairs={{0,32},{16,48},{32,0},{48,16},{1,33},{17,49},{33,1},{49,17},{2,34}... | collective-permute-start | bytes 983048 | tf_op jit(solution)/shard_map/ppermute | solution.py:392
  65.4 13.4 %collective-permute-start.13 = (f32[128,896]{1,0:T(8,128)S(1)}, f32[128,896]{1,0:T(8,128)S(1)}, u32[]{:S(2)}, u32[]{:S(2)}) collective-permute-start(f32[128,896]{1,0:T(8,128)S(1)} %get-tuple-element.57.one_hbm), channel_id=1, source_target_pairs={{120,124},{121,125},{122,126},{123,127},{124,120},{125,121},{126,1... | collective-permute-start | bytes 1376264 | tf_op jit(solution)/shard_map/ppermute | solution.py:369
  67.3 11.5 %collective-permute-start.14 = (f32[128,896]{1,0:T(8,128)S(1)}, f32[128,896]{1,0:T(8,128)S(1)}, u32[]{:S(2)}, u32[]{:S(2)}) collective-permute-start(f32[128,896]{1,0:T(8,128)S(1)} %get-tuple-element.58.two_hbm), channel_id=1, source_target_pairs={{120,121},{121,120},{122,123},{123,122},{124,125},{125,124},{126,1... | collective-permute-start | bytes 1376264 | tf_op jit(solution)/shard_map/ppermute | solution.py:369
  74.5 4.3 %copy-start.3 = (f32[8,16,1792]{2,1,0:T(8,128)}, f32[8,16,1792]{2,1,0:T(8,128)S(1)}, u32[]{:S(2)}) copy-start(f32[8,16,1792]{2,1,0:T(8,128)S(1)} %all-to-all-done.1) | copy-start | bytes 2752516
  74.5 1.7 %collective-permute-start.12 = (f32[640,128]{1,0:T(8,128)S(1)}, f32[640,128]{1,0:T(8,128)S(1)}, u32[]{:S(2)}, u32[]{:S(2)}) collective-permute-start(f32[640,128]{1,0:T(8,128)S(1)} %broadcast_select_fusion.5.small_ref), channel_id=1, source_target_pairs={{0,8},{8,0},{1,9},{9,1},{2,10},{10,2},{3,11},{11,3},{4,12},{12,4},... | collective-permute-start | bytes 983048 | tf_op jit(solution)/shard_map/ppermute | solution.py:395

commit v5 on v4

--- a/solution.py
+++ b/solution.py
@@ -20,7 +20,7 @@
 CHIPS = ("xh", "y")
 N_CHIPS = 8
 N_ROWS = 8
-LANES = 256
+LANES = 512
 VMEM = 16 * 1024 * 1024
 WIDE_VMEM = 51 * 1024 * 1024
 BIG_VMEM = 54 * 1024 * 1024
@@ -142,11 +142,6 @@
     n = rows_ref.shape[0]
     small_ref[:n, :] = rows_ref[...]
     small_ref[n:, :] = jnp.where(near, diag_ref[...], got_ref[...])
-
-
-def copies_kernel(flags, piece_ref, spread_ref):
-    for e in range(N_ROWS):
-        spread_ref[e] = piece_ref[...]
 
 
 def choose_kernel(flags, own_ref, got_ref, panel_ref, rows_ref):
@@ -380,7 +375,7 @@
     turned = lax.ppermute(lax.dynamic_slice_in_dim(came, owner_chip * piece, piece, 0), AXES, pairs)
     got = lax.ppermute(small, "xh", swap)
     small = jnp.where((chip & 4) == (owner_chip & 4), small, got)
-    (copies,) = small_call(copies_kernel, "copies", ((N_ROWS, piece, width),), flags, turned)
+    copies = jnp.broadcast_to(turned, (N_ROWS, piece, width))
     copies, small, got_one, got_two = lax.optimization_barrier((copies, small, got_one, got_two))
     panel0 = lax.all_to_all(copies, ROWS, 0, 0, tiled=True).reshape(BLK, width)
     got = lax.ppermute(small, "y", [(i, i ^ 1) for i in range(4)])

time: 90.3 us -> 89.4 us (0.990)
  waiting for transfers between devices: 23.6 us -> 19.3 us
  starting transfers between devices: 39.6 us -> 43.5 us
  Pallas kernels: 20.1 us -> 19.1 us
    all_to_all x1, starting transfers between devices: 5.06 us -> 7.61 us  [local(): panel0 = lax.all_to_all(copies, ROWS, 0, 0, tiled=True).reshape(BLK, width)]
    ppermute x1, waiting for transfers between devices: 1.95 us -> 0.07 us  [local(): got = lax.ppermute(small, 'y', [(i, i ^ 1) for i in range(4)])]
    pallas_call x3 -> x2, Pallas kernels: 3.63 us -> 2.11 us  [small_call(): pl.pallas_call(kernel, out_shape=tuple((jax.ShapeDtypeStruct(shape, jnp.f...]
    ppermute x1, waiting for transfers between devices: 10.4 us -> 9.01 us  [local(): lax.ppermute(lax.dynamic_slice_in_dim(came, owner_chip * piece, piece, 0)...]
    ppermute x6, starting transfers between devices: 7.92 us -> 9.24 us  [down(): return lax.ppermute(value, AXES, [(at(r), at(r ^ bit)) for r in rows])]
    ppermute x1, waiting for transfers between devices: 2.74 us -> 1.51 us  [local(): got = lax.ppermute(small, 'y', [(i, i ^ 2) for i in range(4)])]
    broadcast_in_dim x0 -> x1, local copies, waits for them, and re-layouts: none -> 1.05 us  [local(): copies = jnp.broadcast_to(turned, (N_ROWS, piece, width))]
  transfers between devices with their start and end apart: 17 -> 17, of which waited for: 8 -> 9; matrix products, arithmetic and copies ran while one was open for 4% -> 4% of each run, Pallas kernels for 7% -> 6%
where the time goes in v5:
time: 89.4 us; the launch traced here: 88.1 us
  starting transfers between devices  43.5 us (49%)
  waiting for transfers between devices  19.3 us (22%)
  Pallas kernels  19.1 us (21%)
  other arithmetic  3.43 us (4%)
  local copies, waits for them, and re-layouts  2.48 us (3%)
    pallas_call x1, Pallas kernels, last_call(): pl.pallas_call(last_kernel, grid=(n // rows,), out_shape=jax.ShapeDtypeSt...  10.5 us
    ppermute x6, starting transfers between devices, down(): return lax.ppermute(value, AXES, [(at(r), at(r ^ bit)) for r in rows])  9.24 us
    ppermute x1, waiting for transfers between devices, local(): lax.ppermute(lax.dynamic_slice_in_dim(came, owner_chip * piece, piece, 0)...  9.01 us
    ppermute x1, starting transfers between devices, local(): lax.ppermute(lax.dynamic_slice_in_dim(came, owner_chip * piece, piece, 0)...  8.14 us
    all_to_all x1, starting transfers between devices, local(): panel0 = lax.all_to_all(copies, ROWS, 0, 0, tiled=True).reshape(BLK, width)  7.61 us
    all_to_all x1, starting transfers between devices, local(): came = lax.all_to_all(sent, CHIPS, 0, 0, tiled=True)  6.53 us
    ppermute x1, starting transfers between devices, local(): got = lax.ppermute(diag, 'z', [(i, i ^ 2) for i in range(4)])  5.34 us
    pallas_call x1, Pallas kernels, prepare_call(): pl.pallas_call(prepare_kernel, grid=(1,), out_shape=tuple((jax.ShapeDtype...  3.54 us
  transfers between devices with their start and end apart: 17, of which 9 were waited for; matrix products, arithmetic and copies ran while one was open for 4% of the time, Pallas kernels for 6%

profile of v5, /device:TPU:29, one launch (start us, length us, event | category | flops | bytes accessed | tf_op | source)
XLA Modules:
  0.0 88.1 jit_solution(13025846700737775762)
XLA Ops:
  0.0 3.5 %halves.1 = (f32[128,2304]{1,0:T(8,128)}, f32[128,2304]{1,0:T(8,128)}, f32[128,128]{1,0:T(8,128)}, f32[128,896]{1,0:T(8,128)}, f32[128,896]{1,0:T(8,128)}) custom-call(f32[128,3584]{1,0:T(8,128)} %panel_ref.1, f32[1024,1792]{1,0:T(8,128)} %weight_hbm.1), custom_call_target="tpu_custom_call" | custom-call | tf_op jit(solution)/shard_map/halves/pallas_call | solution.py:176
  3.5 0.6 collective-permute-start
  4.2 0.9 %collective-permute-start.1 = (f32[128,128]{1,0:T(8,128)}, f32[128,128]{1,0:T(8,128)S(1)}, u32[]{:S(2)}, u32[]{:S(2)}) collective-permute-start(f32[128,128]{1,0:T(8,128)} %get-tuple-element.42), channel_id=1, source_target_pairs={{0,1},{1,0},{2,3},{3,2},{4,5},{5,4},{6,7},{7,6},{8,9},{9,8},{10,11... | collective-permute-start | bytes 196616 | tf_op jit(solution)/shard_map/ppermute | solution.py:348
  5.3 0.1 stack.55.flags
  5.3 1.5 %collective-permute-done.got_ref = f32[128,2304]{1,0:T(8,128)S(1)} collective-permute-done((f32[128,2304]{1,0:T(8,128)}, f32[128,2304]{1,0:T(8,128)S(1)}, u32[]{:S(2)}, u32[]{:S(2)}) %collective-permute-start) | collective-permute-done | bytes 1179680 | tf_op jit(solution)/shard_map/ppermute | solution.py:350
  6.8 1.3 %copy-done = f32[128,2304]{1,0:T(8,128)S(1)} copy-done((f32[128,2304]{1,0:T(8,128)S(1)}, f32[128,2304]{1,0:T(8,128)}, u32[]{:S(2)}) %copy-start) | copy-done | bytes 1179672
  8.1 1.5 %choose.1 = (f32[128,1792]{1,0:T(8,128)}, f32[512,128]{1,0:T(8,128)S(1)}) custom-call(s32[9]{0:T(128)S(1)} %stack.55.flags, f32[128,2304]{1,0:T(8,128)S(1)} %copy-done, f32[128,2304]{1,0:T(8,128)S(1)} %collective-permute-done.got_ref), custom_call_target="tpu_custom_call" | custom-call | bytes 100000 | tf_op jit(solution)/shard_map/choose/pallas_call | solution.py:160
  9.7 0.0 collective-permute-done.1
  9.7 0.7 collective-permute-start.2
  10.4 1.7 %collective-permute-start.4 = (f32[128,128]{1,0:T(8,128)S(1)}, f32[128,128]{1,0:T(8,128)S(1)}, u32[]{:S(2)}, u32[]{:S(2)}) collective-permute-start(f32[128,128]{1,0:T(8,128)S(1)} %broadcast_select_fusion.7), channel_id=1, source_target_pairs={{0,2},{2,0},{4,6},{6,4},{1,3},{3,1},{5,7},{7,5},{8,10},{10,8},{12,... | collective-permute-start | bytes 196616 | tf_op jit(solution)/shard_map/ppermute | solution.py:355
  12.1 6.5 %all-to-all-start = ((f32[8,16,1792]{2,1,0:T(8,128)}), f32[8,16,1792]{2,1,0:T(8,128)S(1)}, u32[]{:S(2)}, u32[]{:S(2)}) async-start(f32[8,16,1792]{2,1,0:T(8,128)} %bitcast.11), calls=%async_computation | async-start | bytes 1835008 | tf_op jit(solution)/shard_map/all_to_all | solution.py:353
  18.6 1.4 %collective-permute-start.3 = (f32[128,896]{1,0:T(8,128)S(1)}, f32[128,896]{1,0:T(8,128)}, u32[]{:S(2)}, u32[]{:S(2)}) collective-permute-start(f32[128,896]{1,0:T(8,128)S(1)} %copy-done.4), channel_id=1, source_target_pairs={{123,127},{127,123}} | collective-permute-start | bytes 1376264 | tf_op jit(solution)/shard_map/ppermute | solution.py:364
  20.1 0.0 collective-permute-done.4
  20.1 5.3 %collective-permute-start.5 = (f32[128,128]{1,0:T(8,128)S(1)}, f32[128,128]{1,0:T(8,128)S(1)}, u32[]{:S(2)}, u32[]{:S(2)}) collective-permute-start(f32[128,128]{1,0:T(8,128)S(1)} %broadcast_select_fusion.8.diag_ref), channel_id=1, source_target_pairs={{0,4},{2,6},{4,0},{6,2},{1,5},{3,7},{5,1},{7,3},{8,12},{10,14},{12... | collective-permute-start | bytes 196616 | tf_op jit(solution)/shard_map/ppermute | solution.py:357
  25.4 2.1 %collective-permute-done.5.got_ref = f32[128,128]{1,0:T(8,128)S(1)} collective-permute-done((f32[128,128]{1,0:T(8,128)S(1)}, f32[128,128]{1,0:T(8,128)S(1)}, u32[]{:S(2)}, u32[]{:S(2)}) %collective-permute-start.5) | collective-permute-done | bytes 65568 | tf_op jit(solution)/shard_map/ppermute | solution.py:357
  27.5 0.6 join.1
  28.1 0.0 collective-permute-done.2
  28.1 0.1 broadcast_select_fusion.3
  28.2 0.0 collective-permute-done.3
  28.2 1.1 %broadcast_select_fusion.2 = f32[128,896]{1,0:T(8,128)S(1)} fusion(f32[128,896]{1,0:T(8,128)S(1)} %copy-done.4, f32[128,896]{1,0:T(8,128)} %collective-permute-done.3, pred[]{:T(512)S(6)} %ne.35), kind=kLoop, calls=%fused_computation.2 | loop fusion | flops 114688 | bytes 1376257 | tf_op jit(solution)/shard_map/jit(_where)/select_n | solution.py:367
  29.3 1.7 %all-to-all-done = f32[8,16,1792]{2,1,0:T(8,128)S(1)} async-done(((f32[8,16,1792]{2,1,0:T(8,128)}), f32[8,16,1792]{2,1,0:T(8,128)S(1)}, u32[]{:S(2)}, u32[]{:S(2)}) %all-to-all-start) | async-done | bytes 917536 | tf_op jit(solution)/shard_map/all_to_all | solution.py:353
  31.0 0.4 collective-permute-start.7
  31.4 0.7 collective-permute-start.8
  32.1 0.7 collective-permute-start.9
  32.9 8.1 %collective-permute-start.6 = (f32[16,1792]{1,0:T(8,128)S(1)}, f32[16,1792]{1,0:T(8,128)S(1)}, u32[]{:S(2)}, u32[]{:S(2)}) collective-permute-start(f32[16,1792]{1,0:T(8,128)S(1)} %constant_dynamic-slice_fusion), channel_id=1, source_target_pairs={{0,0},{1,16},{2,32},{3,48},{4,64},{5,80},{6,96},{7,112},{8,8},{9,2... | collective-permute-start | bytes 344072 | tf_op jit(solution)/shard_map/ppermute | solution.py:375
  41.0 0.4 collective-permute-done.7
  41.4 1.0 %broadcast_select_fusion.6 = f32[640,128]{1,0:T(8,128)S(1)} fusion(f32[640,128]{1,0:T(8,128)S(1)} %join.1, f32[640,128]{1,0:T(8,128)} %collective-permute-done.7, pred[]{:T(512)S(6)} %eq.31), kind=kLoop, calls=%fused_computation.6 | loop fusion | flops 81920 | bytes 983041 | tf_op jit(solution)/shard_map/jit(_where)/select_n | solution.py:377
  42.4 9.0 %collective-permute-done.6 = f32[16,1792]{1,0:T(8,128)S(1)} collective-permute-done((f32[16,1792]{1,0:T(8,128)S(1)}, f32[16,1792]{1,0:T(8,128)S(1)}, u32[]{:S(2)}, u32[]{:S(2)}) %collective-permute-start.6) | collective-permute-done | bytes 114720 | tf_op jit(solution)/shard_map/ppermute | solution.py:375
  51.4 0.0 collective-permute-done.8
  51.4 0.0 collective-permute-done.9
  51.4 1.0 %broadcast_in_dim.6 = f32[8,16,1792]{2,1,0:T(8,128)} broadcast(f32[16,1792]{1,0:T(8,128)S(1)} %collective-permute-done.6), dimensions={1,2} | broadcast | bytes 1032192 | tf_op jit(solution)/shard_map/broadcast_in_dim | solution.py:378
  52.5 0.0 collective-permute-start.10
  52.5 0.0 copy-done.6
  52.5 7.6 %all-to-all-start.1 = ((f32[8,16,1792]{2,1,0:T(8,128)}), f32[8,16,1792]{2,1,0:T(8,128)S(1)}, u32[]{:S(2)}, u32[]{:S(2)}) async-start(f32[8,16,1792]{2,1,0:T(8,128)} %broadcast_in_dim.6), calls=%async_computation.1 | async-start | bytes 1835008 | tf_op jit(solution)/shard_map/all_to_all | solution.py:380
  60.1 0.0 copy-start.2
  60.1 1.2 %broadcast_select_fusion = (f32[128,896]{1,0:T(8,128)S(1)}, f32[128,896]{1,0:T(8,128)S(1)}) fusion(f32[128,896]{1,0:T(8,128)S(1)} %broadcast_select_fusion.2, f32[128,896]{1,0:T(8,128)} %copy-done.6, pred[]{:T(512)S(6)} %ne.36, f32[128,896]{1,0:T(8,128)S(1)} %broadcast_select_fusion.3, f32[128,896]{1,0:T(8,128)S(1)} %collective-permute-done.8), kind=kLoop, calls=%fused_computation | loop fusion | flops 229376 | bytes 2752513 | tf_op jit(solution)/shard_map/jit(_where)/select_n | solution.py:384
  61.3 0.1 collective-permute-done.10
  61.4 2.3 %collective-permute-start.11 = (f32[640,128]{1,0:T(8,128)S(1)}, f32[640,128]{1,0:T(8,128)}, u32[]{:S(2)}, u32[]{:S(2)}) collective-permute-start(f32[640,128]{1,0:T(8,128)S(1)} %broadcast_select_fusion.4), channel_id=1, source_target_pairs={{0,32},{16,48},{32,0},{48,16},{1,33},{17,49},{33,1},{49,17},{2,34}... | collective-permute-start | bytes 983048 | tf_op jit(solution)/shard_map/ppermute | solution.py:387
  63.7 2.7 %collective-permute-start.13 = (f32[128,896]{1,0:T(8,128)S(1)}, f32[128,896]{1,0:T(8,128)S(1)}, u32[]{:S(2)}, u32[]{:S(2)}) collective-permute-start(f32[128,896]{1,0:T(8,128)S(1)} %get-tuple-element.57.one_hbm), channel_id=1, source_target_pairs={{120,124},{121,125},{122,126},{123,127},{124,120},{125,121},{126,1... | collective-permute-start | bytes 1376264 | tf_op jit(solution)/shard_map/ppermute | solution.py:364
  66.4 3.1 %collective-permute-start.14 = (f32[128,896]{1,0:T(8,128)S(1)}, f32[128,896]{1,0:T(8,128)S(1)}, u32[]{:S(2)}, u32[]{:S(2)}) collective-permute-start(f32[128,896]{1,0:T(8,128)S(1)} %get-tuple-element.58.two_hbm), channel_id=1, source_target_pairs={{120,121},{121,120},{122,123},{123,122},{124,125},{125,124},{126,1... | collective-permute-start | bytes 1376264 | tf_op jit(solution)/shard_map/ppermute | solution.py:364
  69.5 1.5 %collective-permute-done.11 = f32[640,128]{1,0:T(8,128)} collective-permute-done((f32[640,128]{1,0:T(8,128)S(1)}, f32[640,128]{1,0:T(8,128)}, u32[]{:S(2)}, u32[]{:S(2)}) %collective-permute-start.11) | collective-permute-done | bytes 327712 | tf_op jit(solution)/shard_map/ppermute | solution.py:387
  71.0 1.7 %all-to-all-done.1 = f32[8,16,1792]{2,1,0:T(8,128)S(1)} async-done(((f32[8,16,1792]{2,1,0:T(8,128)}), f32[8,16,1792]{2,1,0:T(8,128)S(1)}, u32[]{:S(2)}, u32[]{:S(2)}) %all-to-all-start.1) | async-done | bytes 917536 | tf_op jit(solution)/shard_map/all_to_all | solution.py:380
  72.7 0.7 collective-permute-start.12
  73.4 1.2 %collective-permute-done.12.other_ref = f32[640,128]{1,0:T(8,128)S(1)} collective-permute-done((f32[640,128]{1,0:T(8,128)S(1)}, f32[640,128]{1,0:T(8,128)S(1)}, u32[]{:S(2)}, u32[]{:S(2)}) %collective-permute-start.12) | collective-permute-done | bytes 327712 | tf_op jit(solution)/shard_map/ppermute | solution.py:390
  74.7 3.0 %round_first.1 = (bf16[1024,256]{1,0:T(8,128)(2,1)S(1)}, f32[1024,128]{1,0:T(8,128)S(1)}) custom-call(s32[9]{0:T(128)S(1)} %stack.55.flags, s32[16]{0:T(128)S(1)} %copy-done.2, f32[640,128]{1,0:T(8,128)S(1)} %broadcast_select_fusion.5.small_ref, f32[640,128]{1,0:T(8,128)S(1)} %collective-permute-done.12.other_ref, f32[1,1024]{1,0:T(1,128)S(1)} %bitcast.20, ...), custom_call_target="tpu_custom_call" | custom-call | bytes 100000 | tf_op jit(solution)/shard_map/round_first/pallas_call | solution.py:280
  77.6 0.0 collective-permute-done.13.got_one_hbm
  77.7 0.0 collective-permute-done.14.got_two_hbm
  77.7 10.5 %update_all.1 = f32[1024,1792]{1,0:T(8,128)} custom-call(s32[9]{0:T(128)S(1)} %stack.55.flags, s32[16]{0:T(128)S(1)} %copy-done.2, f32[1024,1792]{1,0:T(8,128)} %weight_hbm.1, f32[1024,128]{1,0:T(8,128)S(1)} %get-tuple-element.54.rounded_ref, bf16[1024,256]{1,0:T(8,128)(2,1)S(1)} %get-tuple-element.55.error_ref, f32[128,1792]{1,0:T(8,128)} %bitcast.22, ...), custom_call_target="tpu_custom_call" | custom-call | flops 2000000000 | bytes 16000000 | tf_op jit(solution)/shard_map/update_all/pallas_call | solution.py:296
  (23 shorter events, 0.2 us)
Async XLA Ops:
  0.0 5.1 %copy-start.9 = (s32[2]{0:T(128)S(1)}, s32[2]{0:T(128)}, u32[]{:S(2)}) copy-start(s32[2]{0:T(128)} %param.11) | copy-start | bytes 28
  3.5 6.8 %copy-start.8 = (f32[128,128]{1,0:T(8,128)S(1)}, f32[128,128]{1,0:T(8,128)}, u32[]{:S(2)}) copy-start(f32[128,128]{1,0:T(8,128)} %get-tuple-element.42) | copy-start | bytes 196612
  3.5 3.3 %collective-permute-start = (f32[128,2304]{1,0:T(8,128)}, f32[128,2304]{1,0:T(8,128)S(1)}, u32[]{:S(2)}, u32[]{:S(2)}) collective-permute-start(f32[128,2304]{1,0:T(8,128)} %get-tuple-element.33), channel_id=1, source_target_pairs={{0,8},{8,0},{1,9},{9,1},{2,10},{10,2},{3,11},{11,3},{4,12},{12,4},... | collective-permute-start | bytes 3538952 | tf_op jit(solution)/shard_map/ppermute | solution.py:350
  4.2 5.5 %collective-permute-start.1 = (f32[128,128]{1,0:T(8,128)}, f32[128,128]{1,0:T(8,128)S(1)}, u32[]{:S(2)}, u32[]{:S(2)}) collective-permute-start(f32[128,128]{1,0:T(8,128)} %get-tuple-element.42), channel_id=1, source_target_pairs={{0,1},{1,0},{2,3},{3,2},{4,5},{5,4},{6,7},{7,6},{8,9},{9,8},{10,11... | collective-permute-start | bytes 196616 | tf_op jit(solution)/shard_map/ppermute | solution.py:348
  6.8 1.3 %copy-start = (f32[128,2304]{1,0:T(8,128)S(1)}, f32[128,2304]{1,0:T(8,128)}, u32[]{:S(2)}) copy-start(f32[128,2304]{1,0:T(8,128)} %get-tuple-element.32.own_ref) | copy-start | bytes 3538948
  8.1 1.6 %copy-start.5 = (f32[128,896]{1,0:T(8,128)S(1)}, f32[128,896]{1,0:T(8,128)}, u32[]{:S(2)}) copy-start(f32[128,896]{1,0:T(8,128)} %get-tuple-element.39) | copy-start | bytes 1376260
  8.1 10.5 %copy-start.4 = (f32[128,896]{1,0:T(8,128)S(1)}, f32[128,896]{1,0:T(8,128)}, u32[]{:S(2)}) copy-start(f32[128,896]{1,0:T(8,128)} %get-tuple-element.40) | copy-start | bytes 1376260
  9.7 18.4 %collective-permute-start.2 = (f32[128,896]{1,0:T(8,128)S(1)}, f32[128,896]{1,0:T(8,128)S(1)}, u32[]{:S(2)}, u32[]{:S(2)}) collective-permute-start(f32[128,896]{1,0:T(8,128)S(1)} %copy-done.5), channel_id=1, source_target_pairs={{126,127},{127,126}} | collective-permute-start | bytes 1376264 | tf_op jit(solution)/shard_map/ppermute | solution.py:364
  10.4 9.7 %collective-permute-start.4 = (f32[128,128]{1,0:T(8,128)S(1)}, f32[128,128]{1,0:T(8,128)S(1)}, u32[]{:S(2)}, u32[]{:S(2)}) collective-permute-start(f32[128,128]{1,0:T(8,128)S(1)} %broadcast_select_fusion.7), channel_id=1, source_target_pairs={{0,2},{2,0},{4,6},{6,4},{1,3},{3,1},{5,7},{7,5},{8,10},{10,8},{12,... | collective-permute-start | bytes 196616 | tf_op jit(solution)/shard_map/ppermute | solution.py:355
  12.1 18.9 %all-to-all-start = ((f32[8,16,1792]{2,1,0:T(8,128)}), f32[8,16,1792]{2,1,0:T(8,128)S(1)}, u32[]{:S(2)}, u32[]{:S(2)}) async-start(f32[8,16,1792]{2,1,0:T(8,128)} %bitcast.11), calls=%async_computation | async-start | bytes 1835008 | tf_op jit(solution)/shard_map/all_to_all | solution.py:353
  18.6 9.5 %collective-permute-start.3 = (f32[128,896]{1,0:T(8,128)S(1)}, f32[128,896]{1,0:T(8,128)}, u32[]{:S(2)}, u32[]{:S(2)}) collective-permute-start(f32[128,896]{1,0:T(8,128)S(1)} %copy-done.4), channel_id=1, source_target_pairs={{123,127},{127,123}} | collective-permute-start | bytes 1376264 | tf_op jit(solution)/shard_map/ppermute | solution.py:364
  20.1 7.4 %collective-permute-start.5 = (f32[128,128]{1,0:T(8,128)S(1)}, f32[128,128]{1,0:T(8,128)S(1)}, u32[]{:S(2)}, u32[]{:S(2)}) collective-permute-start(f32[128,128]{1,0:T(8,128)S(1)} %broadcast_select_fusion.8.diag_ref), channel_id=1, source_target_pairs={{0,4},{2,6},{4,0},{6,2},{1,5},{3,7},{5,1},{7,3},{8,12},{10,14},{12... | collective-permute-start | bytes 196616 | tf_op jit(solution)/shard_map/ppermute | solution.py:357
  31.0 10.4 %collective-permute-start.7 = (f32[640,128]{1,0:T(8,128)S(1)}, f32[640,128]{1,0:T(8,128)}, u32[]{:S(2)}, u32[]{:S(2)}) collective-permute-start(f32[640,128]{1,0:T(8,128)S(1)} %join.1), channel_id=1, source_target_pairs={{0,64},{64,0},{1,65},{65,1},{2,66},{66,2},{3,67},{67,3},{4,68},{68... | collective-permute-start | bytes 983048 | tf_op jit(solution)/shard_map/ppermute | solution.py:376
  31.4 20.0 %collective-permute-start.8 = (f32[128,896]{1,0:T(8,128)S(1)}, f32[128,896]{1,0:T(8,128)S(1)}, u32[]{:S(2)}, u32[]{:S(2)}) collective-permute-start(f32[128,896]{1,0:T(8,128)S(1)} %broadcast_select_fusion.3), channel_id=1, source_target_pairs={{124,126},{125,127},{126,124},{127,125}} | collective-permute-start | bytes 1376264 | tf_op jit(solution)/shard_map/ppermute | solution.py:364
  32.1 19.3 %collective-permute-start.9 = (f32[128,896]{1,0:T(8,128)S(1)}, f32[128,896]{1,0:T(8,128)S(1)}, u32[]{:S(2)}, u32[]{:S(2)}) collective-permute-start(f32[128,896]{1,0:T(8,128)S(1)} %broadcast_select_fusion.2), channel_id=1, source_target_pairs={{121,123},{123,121},{125,127},{127,125}} | collective-permute-start | bytes 1376264 | tf_op jit(solution)/shard_map/ppermute | solution.py:364
  32.9 18.6 %collective-permute-start.6 = (f32[16,1792]{1,0:T(8,128)S(1)}, f32[16,1792]{1,0:T(8,128)S(1)}, u32[]{:S(2)}, u32[]{:S(2)}) collective-permute-start(f32[16,1792]{1,0:T(8,128)S(1)} %constant_dynamic-slice_fusion), channel_id=1, source_target_pairs={{0,0},{1,16},{2,32},{3,48},{4,64},{5,80},{6,96},{7,112},{8,8},{9,2... | collective-permute-start | bytes 344072 | tf_op jit(solution)/shard_map/ppermute | solution.py:375
  51.4 1.1 %copy-start.6 = (f32[128,896]{1,0:T(8,128)}, f32[128,896]{1,0:T(8,128)S(1)}, u32[]{:S(2)}) copy-start(f32[128,896]{1,0:T(8,128)S(1)} %collective-permute-done.9) | copy-start | bytes 1376260
  52.5 8.9 %collective-permute-start.10 = (f32[640,128]{1,0:T(8,128)S(1)}, f32[640,128]{1,0:T(8,128)}, u32[]{:S(2)}, u32[]{:S(2)}) collective-permute-start(f32[640,128]{1,0:T(8,128)S(1)} %broadcast_select_fusion.6), channel_id=1, source_target_pairs={{0,16},{16,0},{32,48},{48,32},{1,17},{17,1},{33,49},{49,33},{2,18}... | collective-permute-start | bytes 983048 | tf_op jit(solution)/shard_map/ppermute | solution.py:381
  52.5 20.2 %all-to-all-start.1 = ((f32[8,16,1792]{2,1,0:T(8,128)}), f32[8,16,1792]{2,1,0:T(8,128)S(1)}, u32[]{:S(2)}, u32[]{:S(2)}) async-start(f32[8,16,1792]{2,1,0:T(8,128)} %broadcast_in_dim.6), calls=%async_computation.1 | async-start | bytes 1835008 | tf_op jit(solution)/shard_map/all_to_all | solution.py:380
  60.1 14.5 %copy-start.1 = (f32[1024]{0:T(1024)S(1)}, f32[1024]{0:T(1024)}, u32[]{:S(2)}) copy-start(f32[1024]{0:T(1024)} %param.7) | copy-start | bytes 12292
  60.1 14.5 %copy-start.2 = (s32[16]{0:T(128)S(1)}, s32[16]{0:T(128)}, u32[]{:S(2)}) copy-start(s32[16]{0:T(128)} %codes.3) | copy-start | bytes 196
  61.3 12.1 %copy-start.7 = (f32[2,128,128]{2,1,0:T(8,128)S(1)}, f32[2,128,128]{2,1,0:T(8,128)}, u32[]{:S(2)}) copy-start(f32[2,128,128]{2,1,0:T(8,128)} %param.9) | copy-start | bytes 393220
  61.4 9.6 %collective-permute-start.11 = (f32[640,128]{1,0:T(8,128)S(1)}, f32[640,128]{1,0:T(8,128)}, u32[]{:S(2)}, u32[]{:S(2)}) collective-permute-start(f32[640,128]{1,0:T(8,128)S(1)} %broadcast_select_fusion.4), channel_id=1, source_target_pairs={{0,32},{16,48},{32,0},{48,16},{1,33},{17,49},{33,1},{49,17},{2,34}... | collective-permute-start | bytes 983048 | tf_op jit(solution)/shard_map/ppermute | solution.py:387
  63.7 14.0 %collective-permute-start.13 = (f32[128,896]{1,0:T(8,128)S(1)}, f32[128,896]{1,0:T(8,128)S(1)}, u32[]{:S(2)}, u32[]{:S(2)}) collective-permute-start(f32[128,896]{1,0:T(8,128)S(1)} %get-tuple-element.57.one_hbm), channel_id=1, source_target_pairs={{120,124},{121,125},{122,126},{123,127},{124,120},{125,121},{126,1... | collective-permute-start | bytes 1376264 | tf_op jit(solution)/shard_map/ppermute | solution.py:364
  66.4 11.3 %collective-permute-start.14 = (f32[128,896]{1,0:T(8,128)S(1)}, f32[128,896]{1,0:T(8,128)S(1)}, u32[]{:S(2)}, u32[]{:S(2)}) collective-permute-start(f32[128,896]{1,0:T(8,128)S(1)} %get-tuple-element.58.two_hbm), channel_id=1, source_target_pairs={{120,121},{121,120},{122,123},{123,122},{124,125},{125,124},{126,1... | collective-permute-start | bytes 1376264 | tf_op jit(solution)/shard_map/ppermute | solution.py:364
  72.7 4.9 %copy-start.3 = (f32[8,16,1792]{2,1,0:T(8,128)}, f32[8,16,1792]{2,1,0:T(8,128)S(1)}, u32[]{:S(2)}) copy-start(f32[8,16,1792]{2,1,0:T(8,128)S(1)} %all-to-all-done.1) | copy-start | bytes 2752516
  72.7 1.9 %collective-permute-start.12 = (f32[640,128]{1,0:T(8,128)S(1)}, f32[640,128]{1,0:T(8,128)S(1)}, u32[]{:S(2)}, u32[]{:S(2)}) collective-permute-start(f32[640,128]{1,0:T(8,128)S(1)} %broadcast_select_fusion.5.small_ref), channel_id=1, source_target_pairs={{0,8},{8,0},{1,9},{9,1},{2,10},{10,2},{3,11},{11,3},{4,12},{12,4},... | collective-permute-start | bytes 983048 | tf_op jit(solution)/shard_map/ppermute | solution.py:390
